TPU v7x, 128 devices: a whole 4x4x4 slice. The times are simulated.
128 devices in a mesh: lat: 4 (over z), lon: 32 (over x, y, core).
Axes of the slice: x: 4, y: 4, z: 4, core: 2. Of those that a mesh axis runs over, the one named last changes fastest.
Arguments:
- obs_tiles: bfloat16 [128, 128, 4, 8, 256], P(('lat', 'lon'))
- tile_block: int32 [128, 128, 4], P(('lat', 'lon')), may hold values from 0 to 11
- tile_rows: int32 [128, 128, 4], P(('lat', 'lon')), may hold values from 0 to 256, as said below
- embed_weight: bfloat16 [6, 23], replicated, may hold values from -2.5 to 2.5
- conv1_weight: bfloat16 [9, 24, 256], replicated, may hold values from -0.4375 to 0.4375
- conv1_bias: float32 [256], replicated, may hold values from -3 to 3
- conv2_weight: bfloat16 [9, 256, 512], replicated, may hold values from -0.125 to 0.125
- conv2_bias: float32 [512], replicated, may hold values from -3 to 3
Outputs:
- coarse: bfloat16 [64, 384, 512], P('lat')
Inputs may be any that keep to these rules, and one draw needn't show every extreme that they name: `tile_rows`: for each source and destination the live slots come first: all hold 256 rows but the last live one, which holds 1 to 256; later slots hold 0. In every draw one destination block receives 4 live tiles from every source.
All inputs are finite; a program needn't handle non-finite values.
Results may differ from a plain program's by a relative error of at most 0.0052.
Values may be sent and summed in bfloat16 or wider, within the bound.
No kernel may reach another device: no remote copies, remote signals or barrier semaphores. Data moves between devices by JAX's collectives and lax.ppermute only.
A program may use at most 64 MiB of HBM per device.

v0:
```python
import jax
import jax.numpy as jnp
from jax import lax
from jax.sharding import PartitionSpec as P

BX = 64
BY = 48
SB = 16


kernel_scale = 0.5


def shifted(value, axis, by):
    length = lax.axis_size(axis)
    return lax.ppermute(value, axis, [(i, (i + by) % length) for i in range(length)])


def from_behind(block, axis, distance):
    devices = range(lax.axis_size(axis))
    route = [(i - distance, i) for i in devices if i - distance in devices]
    return lax.ppermute(block, axis, route)


def tile_terms(tiles, row_count, embed_weight):
    cell_ids = jnp.arange(SB * SB, dtype=jnp.int32)
    center_row = (cell_ids // SB).astype(jnp.float32) + 0.5
    center_col = (cell_ids % SB).astype(jnp.float32) + 0.5
    place_row = tiles[:, 0, :].astype(jnp.float32)
    place_col = tiles[:, 1, :].astype(jnp.float32)
    distance = (center_row[None, :, None] - place_row[:, None, :]) ** 2 + (
        center_col[None, :, None] - place_col[:, None, :]
    ) ** 2
    is_live = jnp.arange(tiles.shape[2], dtype=jnp.int32)[None, None, :] < row_count[:, None, None]
    kernel = jnp.where(is_live, jnp.exp(-distance * kernel_scale), jnp.float32(0.0)).astype(
        jnp.bfloat16
    )
    embedded = jnp.einsum(
        "tvo,vc->tco", tiles[:, 2:, :], embed_weight, preferred_element_type=jnp.float32
    ).astype(jnp.bfloat16)
    features = jnp.concatenate(
        [jnp.ones((tiles.shape[0], 1, tiles.shape[2]), jnp.bfloat16), embedded], axis=1
    )
    return jnp.einsum("tco,tko->tck", features, kernel, preferred_element_type=jnp.float32)


def stride_conv(padded, weight, out_rows, out_cols):
    running = jnp.zeros((out_rows * out_cols, weight.shape[2]), jnp.float32)
    for row_tap in range(3):
        for col_tap in range(3):
            tap_rows = lax.slice(
                padded,
                (row_tap, col_tap, 0),
                (row_tap + 2 * out_rows - 1, col_tap + 2 * out_cols - 1, padded.shape[2]),
                (2, 2, 1),
            )
            running = running + jnp.dot(
                tap_rows.reshape(-1, padded.shape[2]),
                weight[3 * row_tap + col_tap],
                preferred_element_type=jnp.float32,
            )
    return running.reshape(out_rows, out_cols, weight.shape[2])


def shards(
    obs_tiles,
    tile_block,
    tile_rows,
    embed_weight,
    conv1_weight,
    conv1_bias,
    conv2_weight,
    conv2_bias,
):
    block_count = obs_tiles.shape[1]
    slot_count = obs_tiles.shape[2]
    feat_rows = obs_tiles.shape[3]
    tile_len = obs_tiles.shape[4]
    arrived_all = (
        lax.all_to_all(obs_tiles, ("lat", "lon"), split_axis=1, concat_axis=0, tiled=True),
        lax.all_to_all(tile_block, ("lat", "lon"), split_axis=1, concat_axis=0, tiled=True),
        lax.all_to_all(tile_rows, ("lat", "lon"), split_axis=1, concat_axis=0, tiled=True),
    )
    group_count = block_count // 8
    group_size = 8 * slot_count
    arrived = arrived_all[0].reshape(group_count, group_size, feat_rows, tile_len)
    block_ids = arrived_all[1].reshape(group_count, group_size)
    row_count = arrived_all[2].reshape(group_count, group_size)
    sub_count = BX // SB * (BY // SB)
    channel_count = conv1_weight.shape[1]

    def add_group(running, inputs):
        tiles, group_ids, group_rows = inputs
        tile_sums = tile_terms(tiles, group_rows, embed_weight)
        onehot = (group_ids[:, None] == jnp.arange(sub_count, dtype=jnp.int32)[None, :]).astype(
            jnp.float32
        )
        return (
            running + jnp.einsum("ts,tck->sck", onehot, tile_sums, precision=lax.Precision.HIGHEST),
            None,
        )

    start = jnp.zeros((sub_count, channel_count, tile_len), jnp.float32)
    block_sums, _ = lax.scan(add_group, start, (arrived, block_ids, row_count))
    density = block_sums[:, 0, :]
    data_part = block_sums[:, 1:, :] / (1.0 + density[:, None, :])
    channels = jnp.concatenate([jnp.log1p(density)[:, None, :], data_part], axis=1).astype(
        jnp.bfloat16
    )
    grid_field = (
        channels.reshape(BX // SB, BY // SB, channel_count, SB, SB)
        .transpose(0, 3, 1, 4, 2)
        .reshape(BX, BY, channel_count)
    )
    rim_width = 1
    side_rim = shifted(grid_field[:, BY - rim_width :, :], "lon", 1)
    padded = jnp.concatenate([side_rim, grid_field], axis=1)
    top_rim = from_behind(padded[BX - rim_width :, :, :], "lat", 1)
    padded = jnp.concatenate([top_rim, padded], axis=0)
    first_layer = jax.nn.silu(
        stride_conv(padded, conv1_weight, BX // 2, BY // 2) + conv1_bias
    ).astype(jnp.bfloat16)
    first_side = shifted(first_layer[:, BY // 2 - 1 :, :], "lon", 1)
    first_padded = jnp.concatenate([first_side, first_layer], axis=1)
    first_top = from_behind(first_padded[BX // 2 - 1 :, :, :], "lat", 1)
    first_padded = jnp.concatenate([first_top, first_padded], axis=0)
    coarse = (stride_conv(first_padded, conv2_weight, BX // 4, BY // 4) + conv2_bias).astype(
        jnp.bfloat16
    )
    return lax.all_gather(coarse, "lon", axis=1, tiled=True)


def solution(mesh):
    placed = (
        P(("lat", "lon"), None, None, None, None),
        P(("lat", "lon"), None, None),
        P(("lat", "lon"), None, None),
        P(),
        P(),
        P(),
        P(),
        P(),
    )
    return jax.shard_map(
        shards, mesh=mesh, in_specs=placed, out_specs=P("lat", None, None), check_vma=False
    )
```

profile of v0, /device:TPU:1, one launch (start us, length us, event | category | flops | bytes accessed | tf_op | source)
XLA Modules:
  0.0 268.7 jit_solution(6266015869091623327)
XLA Ops:
  8.0 11.5 %all-to-all-start = ((s32[1,128,4]{2,0,1:T(1,128)}), s32[1,128,4]{2,0,1:T(1,128)S(1)}, u32[]{:S(2)}, u32[]{:S(2)}) async-start(s32[1,128,4]{2,0,1:T(1,128)} %copy.26), calls=%async_computation | async-start | bytes 131072 | tf_op jit(solution)/shard_map/all_to_all | solution.py:81
  20.3 8.7 %all-to-all-done = s32[1,128,4]{2,0,1:T(1,128)S(1)} async-done(((s32[1,128,4]{2,0,1:T(1,128)}), s32[1,128,4]{2,0,1:T(1,128)S(1)}, u32[]{:S(2)}, u32[]{:S(2)}) %all-to-all-start) | async-done | bytes 2080 | tf_op jit(solution)/shard_map/all_to_all | solution.py:81
  29.0 13.8 %all_to_all.12 = s32[1,128,4]{2,0,1:T(1,128)S(1)} all-to-all(s32[1,128,4]{2,0,1:T(1,128)S(1)} %copy.28), channel_id=1, replica_groups=mesh['lat'=4,'lon'=32] {'lat','lon'}, dimensions={1} | all-to-all | bytes 4096 | tf_op jit(solution)/shard_map/all_to_all | solution.py:82
  42.8 4.4 %all-to-all-start.1 = ((bf16[1,128,4,8,256]{4,3,2,0,1:T(8,128)(2,1)}), bf16[1,128,4,8,256]{4,3,2,0,1:T(8,128)(2,1)S(1)}, u32[]{:S(2)}, u32[]{:S(2)}) async-start(bf16[1,128,4,8,256]{4,3,2,0,1:T(8,128)(2,1)} %bitcast.136), calls=%async_computation.1 | async-start | bytes 4194304 | tf_op jit(solution)/shard_map/all_to_all | solution.py:80
  49.5 28.2 %all-to-all-done.1 = bf16[1,128,4,8,256]{4,3,2,0,1:T(8,128)(2,1)S(1)} async-done(((bf16[1,128,4,8,256]{4,3,2,0,1:T(8,128)(2,1)}), bf16[1,128,4,8,256]{4,3,2,0,1:T(8,128)(2,1)S(1)}, u32[]{:S(2)}, u32[]{:S(2)}) %all-to-all-start.1) | async-done | bytes 2097184 | tf_op jit(solution)/shard_map/all_to_all | solution.py:80
  77.7 61.0 %while.13 = (s32[]{:T(128)}, f32[12,24,256]{2,0,1:T(8,128)S(1)}, s32[16,32]{1,0:T(8,128)S(1)}, bf16[16,32,8,256]{3,2,1,0:T(8,128)(2,1)S(1)}, bf16[6,23]{1,0:T(8,...) while((s32[]{:T(128)}, f32[12,24,256]{2,0,1:T(8,128)S(1)}, ...), condition=%wide.region_1.2_spmd.clone, body=%wide.region_0.1_spmd.clone.sunk | while | flops 150475136 | bytes 3626115 | solution.py:104
  78.2 2.7 fusion.104
  82.0 2.7 fusion.104
  89.6 2.7 fusion.104
  93.5 2.7 fusion.104
  97.3 2.7 fusion.104
  101.1 2.7 fusion.104
  104.9 2.7 fusion.104
  108.7 2.7 fusion.104
  112.5 2.7 fusion.104
  116.3 2.7 fusion.104
  120.2 2.7 fusion.104
  156.7 3.7 %slice.160 = bf16[32,24,24]{0,2,1:T(8,128)(2,1)S(1)} slice(bf16[64,49,24]{0,2,1:T(8,128)(2,1)S(1)} %pad_maximum_fusion.1), slice={[1:64:2], [0:47:2], [0:24:1]} | slice | bytes 73728 | tf_op jit(solution)/shard_map/slice | solution.py:51
  160.4 3.7 %slice.154 = bf16[32,24,24]{0,2,1:T(8,128)(2,1)S(1)} slice(bf16[64,49,24]{0,2,1:T(8,128)(2,1)S(1)} %pad_maximum_fusion.1), slice={[0:63:2], [0:47:2], [0:24:1]} | slice | bytes 73728 | tf_op jit(solution)/shard_map/slice | solution.py:51
  167.3 4.2 %slice.152 = bf16[32,24,24]{0,2,1:T(8,128)(2,1)S(1)} slice(bf16[65,49,24]{0,2,1:T(8,128)(2,1)S(1)} %maximum_maximum_fusion.1), slice={[0:63:2], [2:49:2], [0:24:1]} | slice | bytes 73728 | tf_op jit(solution)/shard_map/slice | solution.py:51
  171.5 3.7 %slice.150 = bf16[32,24,24]{0,2,1:T(8,128)(2,1)S(1)} slice(bf16[65,49,24]{0,2,1:T(8,128)(2,1)S(1)} %maximum_maximum_fusion.1), slice={[0:63:2], [1:48:2], [0:24:1]} | slice | bytes 73728 | tf_op jit(solution)/shard_map/slice | solution.py:51
  175.2 3.7 %slice.148 = bf16[32,24,24]{0,2,1:T(8,128)(2,1)S(1)} slice(bf16[65,49,24]{0,2,1:T(8,128)(2,1)S(1)} %maximum_maximum_fusion.1), slice={[0:63:2], [0:47:2], [0:24:1]} | slice | bytes 73728 | tf_op jit(solution)/shard_map/slice | solution.py:51
  201.4 51.4 %all-gather.2.cloned.1.call-done = bf16[16,384,512]{2,0,1:T(8,128)(2,1)} async-done(((bf16[16,12,512]{2,0,1:T(8,128)(2,1)}), bf16[16,384,512]{2,0,1:T(8,128)(2,1)}) %all-gather.2.cloned.1.call-update) | async-done | bytes 6291472 | tf_op jit(solution)/shard_map/all_gather | solution.py:130
  252.8 9.0 %copy.39 = bf16[16,384,512]{2,1,0:T(8,128)(2,1)} copy(bf16[16,384,512]{2,0,1:T(8,128)(2,1)} %all-gather.2.cloned.1.call-done) | data formatting | bytes 12582912 | tf_op jit(solution)/shard_map/all_gather | solution.py:130
  (248 shorter events, 78.4 us)
Async XLA Ops:
  8.0 21.0 %all-to-all-start = ((s32[1,128,4]{2,0,1:T(1,128)}), s32[1,128,4]{2,0,1:T(1,128)S(1)}, u32[]{:S(2)}, u32[]{:S(2)}) async-start(s32[1,128,4]{2,0,1:T(1,128)} %copy.26), calls=%async_computation | async-start | bytes 131072 | tf_op jit(solution)/shard_map/all_to_all | solution.py:81
  20.2 57.5 %copy-start.10 = (bf16[6,23]{1,0:T(8,128)(2,1)S(1)}, bf16[6,23]{1,0:T(8,128)(2,1)}, u32[]{:S(2)}) copy-start(bf16[6,23]{1,0:T(8,128)(2,1)} %param.13) | copy-start | bytes 832
  42.8 34.9 %all-to-all-start.1 = ((bf16[1,128,4,8,256]{4,3,2,0,1:T(8,128)(2,1)}), bf16[1,128,4,8,256]{4,3,2,0,1:T(8,128)(2,1)S(1)}, u32[]{:S(2)}, u32[]{:S(2)}) async-start(bf16[1,128,4,8,256]{4,3,2,0,1:T(8,128)(2,1)} %bitcast.136), calls=%async_computation.1 | async-start | bytes 4194304 | tf_op jit(solution)/shard_map/all_to_all | solution.py:80
  47.2 205.6 %all-gather.2.cloned.1.call-start = ((), (), s32[]{:S(2)}) async-start(), calls=%async_computation.3 | async-start | bytes 6488064 | tf_op jit(solution)/shard_map/all_gather | solution.py:130
  146.8 6.2 %collective-permute-start = (bf16[64,1,24]{2,1,0:T(2,128)(2,1)}, bf16[64,1,24]{2,1,0:T(2,128)(2,1)}, u32[]{:S(2)}, u32[]{:S(2)}) collective-permute-start(bf16[64,1,24]{2,1,0:T(2,128)(2,1)} %slice.192), channel_id=1, source_target_pairs={{0,1},{1,2},{2,3},{3,4},{4,5},{5,6},{6,7},{7,8},{8,9},{9,10},{10,1... | collective-permute-start | bytes 9224 | tf_op jit(solution)/shard_map/ppermute | solution.py:16
  154.7 11.5 %collective-permute-start.1 = (bf16[1,49,24]{0,2,1:T(8,128)(2,1)}, bf16[1,49,24]{0,2,1:T(8,128)(2,1)}, u32[]{:S(2)}, u32[]{:S(2)}) collective-permute-start(bf16[1,49,24]{0,2,1:T(8,128)(2,1)} %fusion.25), channel_id=1, source_target_pairs={{0,32},{32,64},{64,96},{1,33},{33,65},{65,97},{2,34},{34,66},{66,9... | collective-permute-start | bytes 7064 | tf_op jit(solution)/shard_map/ppermute | solution.py:22
  180.3 3.5 %copy-start = (f32[768,256]{1,0:T(8,128)S(1)}, f32[768,256]{1,0:T(8,128)}, u32[]{:S(2)}) copy-start(f32[768,256]{1,0:T(8,128)} %fusion.51) | copy-start | bytes 2359300
  180.5 3.4 %copy-start.9 = (bf16[768,24]{0,1:T(8,128)(2,1)S(1)}, bf16[768,24]{0,1:T(8,128)(2,1)}, u32[]{:S(2)}) copy-start(bf16[768,24]{0,1:T(8,128)(2,1)} %reshape.154) | copy-start | bytes 110596
  182.8 2.1 copy-start.8
  184.9 1.0 copy-start.12
  186.2 5.1 %collective-permute-start.2 = (bf16[32,1,256]{2,1,0:T(2,128)(2,1)S(1)}, bf16[32,1,256]{2,1,0:T(2,128)(2,1)S(1)}, u32[]{:S(2)}, u32[]{:S(2)}) collective-permute-start(bf16[32,1,256]{2,1,0:T(2,128)(2,1)S(1)} %slice.195), channel_id=1, source_target_pairs={{0,1},{1,2},{2,3},{3,4},{4,5},{5,6},{6,7},{7,8},{8,9},{9,10},{10,1... | collective-permute-start | bytes 49160 | tf_op jit(solution)/shard_map/ppermute | solution.py:16
  191.3 7.1 %copy-start.1 = (bf16[9,256,512]{2,1,0:T(8,128)(2,1)S(1)}, bf16[9,256,512]{2,1,0:T(8,128)(2,1)}, u32[]{:S(2)}) copy-start(bf16[9,256,512]{2,1,0:T(8,128)(2,1)} %param.16) | copy-start | bytes 7077892
  191.3 2.7 copy-start.7
  191.9 4.1 %collective-permute-start.3 = (bf16[1,25,256]{2,1,0:T(8,128)(2,1)}, bf16[1,25,256]{2,1,0:T(8,128)(2,1)S(1)}, u32[]{:S(2)}, u32[]{:S(2)}) collective-permute-start(bf16[1,25,256]{2,1,0:T(8,128)(2,1)} %fusion.45), channel_id=1, source_target_pairs={{0,32},{32,64},{64,96},{1,33},{33,65},{65,97},{2,34},{34,66},{66,9... | collective-permute-start | bytes 38408 | tf_op jit(solution)/shard_map/ppermute | solution.py:22
  197.0 2.0 copy-start.6
  198.3 1.0 copy-start.5
  198.6 0.9 copy-start.4
  199.1 0.9 copy-start.3
  199.3 0.9 copy-start.2
  199.7 0.7 copy-start.11
Sparse Core Ops, SparseCore 0:
  201.5 51.2 all-gather.1
where the time goes:
time: 270 us; the launch traced here: 269 us
  waiting for transfers between devices  88.4 us (33%)
  matrix products  69.2 us (26%)
  local copies, waits for them, and re-layouts  53.3 us (20%)
  starting transfers between devices  20.9 us (8%)
  between operations  14 us (5%)
  blocking collectives  13.8 us (5%)
  other arithmetic  7.95 us (3%)
    all_gather x1, waiting for transfers between devices, shards(): return lax.all_gather(coarse, 'lon', axis=1, tiled=True)  51.4 us
    dot_general x16, matrix products, tile_terms(): jnp.einsum('tco,tko->tck', features, kernel, preferred_element_type=jnp.f...  42.6 us
    slice x23, local copies, waits for them, and re-layouts, stride_conv(): lax.slice(padded, (row_tap, col_tap, 0), (row_tap + 2 * out_rows - 1, col...  29.3 us
    all_to_all x1, waiting for transfers between devices, shards(): lax.all_to_all(obs_tiles, ('lat', 'lon'), split_axis=1, concat_axis=0, ti...  28.2 us
    all_to_all x1, blocking collectives, shards(): lax.all_to_all(tile_rows, ('lat', 'lon'), split_axis=1, concat_axis=0, ti...  13.8 us
    dot_general x18, matrix products, stride_conv(): jnp.dot(tap_rows.reshape(-1, padded.shape[2]), weight[3 * row_tap + col_t...  11.6 us
    all_to_all x1, starting transfers between devices, shards(): lax.all_to_all(tile_block, ('lat', 'lon'), split_axis=1, concat_axis=0, t...  11.5 us
    dot_general x16, matrix products, add_group(): jnp.einsum('ts,tck->sck', onehot, tile_sums, precision=lax.Precision.HIGH...  10.1 us
  transfers between devices with their start and end apart: 7, of which 3 were waited for; matrix products, arithmetic and copies ran while one was open for 9% of the time, Pallas kernels for 0%

commit v1 on v0

v1 whole, which is shorter than its diff:
```python
import jax
import jax.numpy as jnp
from jax import lax
from jax.experimental import pallas as pl
from jax.experimental.pallas import tpu as pltpu
from jax.sharding import PartitionSpec as P

BX = 64
BY = 48
SB = 16
TILE = 256
CAP = 4
FEAT = 8
C1 = 256
C2 = 512
SUBS = 12
PHASES = 4
QUADS = BY // PHASES
ROW_LANES = PHASES * FEAT
HALF_LANES = (BX // 2 + 4) * ROW_LANES
FAR = 8192.0
ROOT_HALF_LOG2E = (0.5 * 1.4426950408889634) ** 0.5
SOURCES = 16


def iota(shape, axis):
    return lax.broadcasted_iota(jnp.int32, shape, axis)


def setconv_kernel(sub_ref, core_ref, tiles_ref, mine_ref, send_ref, tail_ref, *sums):
    step = pl.program_id(0)

    @pl.when(step == 0)
    def _():
        for total in sums:
            total[...] = jnp.zeros_like(total)

    row = iota((SB, 1), 0)
    center_row = (row.astype(jnp.float32) + 0.5) * ROOT_HALF_LOG2E
    center_col = ((row % 4 * 4 + row // 4).astype(jnp.float32) + 0.5) * ROOT_HALF_LOG2E

    def add_tile(source, slot, total):
        tile = jnp.concatenate([tiles_ref[source, slot], tiles_ref[source, slot + CAP]], axis=1)
        place = tile.astype(jnp.float32)
        off_row = center_row - place[0:1] * ROOT_HALF_LOG2E
        off_col = center_col - place[1:2] * ROOT_HALF_LOG2E
        along_row = jnp.exp2(-(off_row * off_row)).astype(jnp.bfloat16)
        along_col = jnp.exp2(-(off_col * off_col)).astype(jnp.bfloat16)
        weighted = [along_row, jnp.zeros_like(along_row)]
        weighted += [tile[k : k + 1] * along_row for k in range(2, FEAT)]
        part = lax.dot_general(
            along_col,
            jnp.concatenate(weighted, axis=0),
            (((1,), (1,)), ((), ())),
            preferred_element_type=jnp.float32,
        )
        sub = sub_ref[step * SOURCES + source, slot]
        total[sub] = total[sub] + part

    def add_sources(m, carry):
        for k in range(4):
            for slot in range(CAP):
                add_tile(4 * m + k, slot, sums[slot])
        return carry

    lax.fori_loop(0, SOURCES // 4, add_sources, 0)

    @pl.when(step == pl.num_programs(0) - 1)
    def _():
        total = sums[0][...]
        for more in sums[1:]:
            total = total + more[...]
        total = total.reshape(SUBS * SB, FEAT * SB)
        pick = (iota((128, 128), 0) == iota((128, 128), 1) % SB).astype(jnp.float32)
        density = jnp.dot(
            total, pick, precision=lax.Precision.HIGHEST, preferred_element_type=jnp.float32
        )
        lane = iota((SUBS * SB, 128), 1)
        grid = jnp.where(lane < SB, jnp.log1p(density), total / (1.0 + density))
        grid = grid.astype(jnp.bfloat16)
        core = core_ref[0]
        target = iota((4 * 32, SUBS * SB), 0)
        source = iota((4 * 32, SUBS * SB), 1)
        quad = target % 32 - QUADS * core
        wanted = (target // 32) * BY + (quad // 4) * SB + quad % 4
        inside = (quad >= 0) & (quad < QUADS)
        parts = []
        for phase in range(PHASES):
            take = (inside & (source == wanted + 4 * phase)).astype(jnp.bfloat16)
            parts.append(
                jnp.dot(take, grid, preferred_element_type=jnp.float32).astype(jnp.bfloat16)
            )
        spread = jnp.concatenate(parts, axis=1)
        lane_in = iota((512, 512), 0)
        lane_out = iota((512, 512), 1)
        moved = (
            lane_in % SB * ROW_LANES + lane_in // 128 * FEAT + lane_in % 128 // SB == lane_out
        ).astype(jnp.bfloat16)
        ordered = jnp.dot(spread, moved, preferred_element_type=jnp.float32).astype(jnp.bfloat16)
        whole = jnp.concatenate(
            [ordered[32 * k : 32 * k + 2 * QUADS] for k in range(4)], axis=1
        )
        upper = jnp.concatenate([jnp.zeros((2 * QUADS, 128), jnp.bfloat16), whole[:, :1024]], axis=1)
        lower = whole[:, 896:]
        tail_ref[...] = whole[:, 1920:]

        @pl.when(core == 0)
        def _():
            mine_ref[...] = upper
            send_ref[...] = lower

        @pl.when(core != 0)
        def _():
            mine_ref[...] = lower
            send_ref[...] = upper


def set_convolution(subs, core, arrived):
    half = jax.ShapeDtypeStruct((2 * QUADS, HALF_LANES), jnp.bfloat16)
    tail = jax.ShapeDtypeStruct((2 * QUADS, 128), jnp.bfloat16)
    same = lambda i, *_: (0, 0)
    return pl.pallas_call(
        setconv_kernel,
        grid_spec=pltpu.PrefetchScalarGridSpec(
            num_scalar_prefetch=2,
            grid=(arrived.shape[0] // SOURCES,),
            in_specs=[pl.BlockSpec((SOURCES,) + arrived.shape[1:], lambda i, *_: (i, 0, 0, 0))],
            out_specs=[
                pl.BlockSpec(half.shape, same),
                pl.BlockSpec(half.shape, same),
                pl.BlockSpec(tail.shape, same),
            ],
            scratch_shapes=[pltpu.VMEM((SUBS, SB, FEAT * SB), jnp.float32)] * CAP,
        ),
        out_shape=[half, half, tail],
        compiler_params=pltpu.CompilerParams(
            dimension_semantics=("arbitrary",), vmem_limit_bytes=48 << 20
        ),
    )(subs, core, arrived)


def conv_kernel(
    top_ref, grid_ref, odd1_ref, odd2_ref, even1_ref, even2_ref, bias1_ref, weight2_ref,
    bias2_ref, out_ref, moved_ref, even_rows, odd_rows,
):
    step = pl.program_id(0)
    columns = grid_ref.shape[0]

    def first_row(t, step_rows):
        block = t // 2
        if t % 2 == 0:
            here = grid_ref[:, 128 * block : 128 * block + 128]
            left = moved_ref[:, 128 * block : 128 * block + 128]
            odd = jnp.dot(here, odd1_ref[...], preferred_element_type=jnp.float32)
            weights = even1_ref
        else:
            here = grid_ref[:, 128 * block : 128 * block + 256]
            left = moved_ref[:, 128 * block : 128 * block + 256]
            odd = jnp.dot(here, odd2_ref[...], preferred_element_type=jnp.float32)
            weights = even2_ref
        even = jnp.dot(
            jnp.concatenate([here, left], axis=1), weights[...], preferred_element_type=jnp.float32
        )

        def activate(half):
            half = half + bias1_ref[...]
            return half * jnp.tanh(half) + half

        odd = activate(odd)
        even = activate(even)
        if t == 0:
            live = top_ref[0].astype(jnp.float32)
            odd = odd * live
            even = even * live
        before = pltpu.roll(odd, 1, axis=0)
        store = even_rows if t % 2 == 0 else odd_rows
        at = pl.ds(block * columns, columns)
        store[at, 0:C1] = before.astype(jnp.bfloat16)
        store[at, C1 : 2 * C1] = even.astype(jnp.bfloat16)
        store[at, 2 * C1 :] = odd.astype(jnp.bfloat16)

    def second_rows(pair):
        total = None
        for tap, (store, at) in enumerate(
            [(even_rows, 2 * pair), (odd_rows, 2 * pair), (even_rows, 2 * pair + 1)]
        ):
            part = jnp.dot(
                store[at * columns : (at + 2) * columns, :],
                weight2_ref[tap],
                preferred_element_type=jnp.float32,
            )
            total = part if total is None else total + part
        total = (total + bias2_ref[...]).astype(jnp.bfloat16)
        out_ref[...] = total.reshape(out_ref.shape)

    @pl.when(step == 0)
    def _():
        moved_ref[...] = pltpu.roll(grid_ref[...].astype(jnp.float32), 1, axis=0).astype(
            jnp.bfloat16
        )
        first_row(0, 0)

    for pair in range(4):

        @pl.when(step == pair)
        def _(pair=pair):
            for t in range(4 * pair + 1, 4 * pair + 5):
                first_row(t, 0)
            second_rows(pair)


def convolutions(top, gathered, weights1, bias1, weights2, bias2):
    columns = gathered.shape[0]
    full = lambda a: pl.BlockSpec(a.shape, lambda i, *_: (0,) * a.ndim)
    operands = [gathered, *weights1, bias1, weights2, bias2]
    return pl.pallas_call(
        conv_kernel,
        grid_spec=pltpu.PrefetchScalarGridSpec(
            num_scalar_prefetch=1,
            grid=(4,),
            in_specs=[full(a) for a in operands],
            out_specs=pl.BlockSpec((2, columns, C2), lambda i, *_: (i, 0, 0)),
            scratch_shapes=[
                pltpu.VMEM(gathered.shape, jnp.bfloat16),
                pltpu.VMEM((9 * columns, 3 * C1), jnp.bfloat16),
                pltpu.VMEM((8 * columns, 3 * C1), jnp.bfloat16),
            ],
        ),
        out_shape=jax.ShapeDtypeStruct((8, columns, C2), jnp.bfloat16),
        compiler_params=pltpu.CompilerParams(
            dimension_semantics=("arbitrary",), vmem_limit_bytes=56 << 20
        ),
    )(top, *operands)


def first_weights(embed_weight, conv1_weight):
    channels = conv1_weight.astype(jnp.float32)
    values = jnp.einsum(
        "vc,tco->tvo",
        embed_weight.astype(jnp.float32),
        channels[:, 1:],
        precision=lax.Precision.HIGHEST,
    )
    taps = jnp.concatenate([channels[:, :1], jnp.zeros_like(channels[:, :1]), values], axis=1)
    taps = (0.5 * taps).astype(jnp.bfloat16).reshape(3, 3, FEAT, C1)

    def placed(part, above, below, phase):
        pads = ((above, below), (phase, PHASES - phase - part.shape[1]), (0, 0), (0, 0))
        return jnp.pad(part, pads).reshape(-1, C1)

    odd = [placed(taps, above, below, 1) for above, below in ((1, 0), (3, 2))]
    even = [
        jnp.concatenate(
            [placed(taps[:, 1:], above, below, 0), placed(taps[:, :1], above, below, 3)], axis=0
        )
        for above, below in ((1, 0), (3, 2))
    ]
    return odd + even


def shards(
    obs_tiles,
    tile_block,
    tile_rows,
    embed_weight,
    conv1_weight,
    conv1_bias,
    conv2_weight,
    conv2_bias,
):
    blocks = obs_tiles.shape[1]
    n_lon = lax.axis_size("lon")
    n_lat = lax.axis_size("lat")
    core = lax.axis_index("lon") % 2

    tiles = obs_tiles[0]
    dead = iota(tiles.shape, 3) >= tile_rows[0][:, :, None, None]
    tiles = jnp.where(dead & (iota(tiles.shape, 2) == 0), jnp.bfloat16(FAR), tiles)
    notes = jnp.pad(
        tile_block[0].astype(jnp.bfloat16)[:, None, None, :], ((0, 0), (0, 0), (0, 7), (0, 124))
    )
    leaving = jnp.concatenate([tiles[..., :128], tiles[..., 128:], notes], axis=1)
    arrived = lax.all_to_all(leaving, ("lat", "lon"), 0, 0, tiled=True)
    subs = arrived[:, 2 * CAP, 0, :CAP].astype(jnp.int32)
    mine, send, tail = set_convolution(subs, core.reshape(1), arrived)

    pairs = [(i, i ^ 1) for i in range(n_lon)]
    other = lax.ppermute(send, "lon", pairs)
    from_same = [
        (z * n_lon + i, (z + 1) * n_lon + i) for z in range(n_lat - 1) for i in range(0, n_lon, 2)
    ]
    from_other = [(a + 1, b) for a, b in from_same]
    halo = lax.ppermute(tail, ("lat", "lon"), from_same) + lax.ppermute(
        tail, ("lat", "lon"), from_other
    )
    joined = mine + other + jnp.pad(halo, ((0, 0), (0, HALF_LANES - 128)))
    groups = [[2 * k + c for k in range(n_lon // 2)] for c in range(2)]
    gathered = lax.all_gather(joined, "lon", axis=0, tiled=True, axis_index_groups=groups)

    weights1 = first_weights(embed_weight, conv1_weight)
    top = jnp.where((lax.axis_index("lat") == 0) & (core == 0), 0, 1).reshape(1)
    half = convolutions(
        top,
        gathered,
        weights1,
        0.5 * conv1_bias[None],
        conv2_weight.reshape(3, 3 * C1, C2),
        conv2_bias[None],
    )
    swapped = lax.ppermute(half, "lon", pairs)
    first = core == 0
    return jnp.concatenate(
        [jnp.where(first, half, swapped), jnp.where(first, swapped, half)], axis=0
    )


def solution(mesh):
    placed = (
        P(("lat", "lon"), None, None, None, None),
        P(("lat", "lon"), None, None),
        P(("lat", "lon"), None, None),
        P(),
        P(),
        P(),
        P(),
        P(),
    )
    return jax.shard_map(
        shards, mesh=mesh, in_specs=placed, out_specs=P("lat", None, None), check_vma=False
    )
```

time: 270 us -> 124 us (0.46)
  matrix products: 69.2 us -> 0.14 us
  waiting for transfers between devices: 88.4 us -> 37 us
  local copies, waits for them, and re-layouts: 53.3 us -> 2.71 us
  Pallas kernels: 0 us -> 29.3 us
  between operations: 14 us -> 0.18 us
  blocking collectives: 13.8 us -> 19.6 us
  other arithmetic: 7.95 us -> 13.1 us
    dot_general x66 -> x1, matrix products: 69.2 us -> 0.14 us  [first_weights(): jnp.einsum('vc,tco->tvo', embed_weight.astype(jnp.float32), channels[:, 1...]
    all_gather x1 -> x0, waiting for transfers between devices: 51.4 us -> none  [shards(): return lax.all_gather(coarse, 'lon', axis=1, tiled=True)]
    slice x25 -> x4, local copies, waits for them, and re-layouts: 30 us -> 0.38 us  [the longest x1 0.37 us: shards(): tiles[..., :128]]
    pallas_call x0 -> x2, Pallas kernels: none -> 29.3 us  [the longest x1 15.4 us: set_convolution(): pl.pallas_call(setconv_kernel, grid_spec=pltpu.PrefetchScalarGridSpec(num...]
    all_gather x0 -> x1, blocking collectives: none -> 19.6 us  [shards(): lax.all_gather(joined, 'lon', axis=0, tiled=True, axis_index_groups=groups)]
    all_to_all x1 -> x0, blocking collectives: 13.8 us -> none  [shards(): lax.all_to_all(tile_rows, ('lat', 'lon'), split_axis=1, concat_axis=0, ti...]
    all_gather x1 -> x0, local copies, waits for them, and re-layouts: 9.02 us -> none  [shards(): return lax.all_gather(coarse, 'lon', axis=1, tiled=True)]
    reshape x18 -> x0, local copies, waits for them, and re-layouts: 7.41 us -> none  [the longest x14 6.54 us: stride_conv(): tap_rows.reshape(-1, padded.shape[2])]
  transfers between devices with their start and end apart: 7 -> 5, of which waited for: 3 -> 2; matrix products, arithmetic and copies ran while one was open for 9% -> 3% of each run, Pallas kernels for 0% -> 0%
where the time goes in v1:
time: 124 us
  waiting for transfers between devices  37 us (30%)
  Pallas kernels  29.3 us (24%)
  starting transfers between devices  21.4 us (17%)
  blocking collectives  19.6 us (16%)
  other arithmetic  13.1 us (11%)
  local copies, waits for them, and re-layouts  2.71 us (2%)
    all_to_all x1, waiting for transfers between devices, shards(): arrived = lax.all_to_all(leaving, ('lat', 'lon'), 0, 0, tiled=True)  31.5 us
    all_gather x1, blocking collectives, shards(): lax.all_gather(joined, 'lon', axis=0, tiled=True, axis_index_groups=groups)  19.6 us
    pallas_call x1, Pallas kernels, set_convolution(): pl.pallas_call(setconv_kernel, grid_spec=pltpu.PrefetchScalarGridSpec(num...  15.4 us
    pallas_call x1, Pallas kernels, convolutions(): pl.pallas_call(conv_kernel, grid_spec=pltpu.PrefetchScalarGridSpec(num_sc...  13.9 us
    all_to_all x1, starting transfers between devices, shards(): arrived = lax.all_to_all(leaving, ('lat', 'lon'), 0, 0, tiled=True)  11.5 us
    ppermute x1, waiting for transfers between devices, shards(): swapped = lax.ppermute(half, 'lon', pairs)  5.5 us
    ppermute x1, starting transfers between devices, shards(): swapped = lax.ppermute(half, 'lon', pairs)  4.97 us
    concatenate x1, other arithmetic, shards(): jnp.concatenate([jnp.where(first, half, swapped), jnp.where(first, swappe...  3.24 us
  transfers between devices with their start and end apart: 5, of which 2 were waited for; matrix products, arithmetic and copies ran while one was open for 3% of the time, Pallas kernels for 0%

profile of v1, /device:TPU:1, one launch (start us, length us, event | category | flops | bytes accessed | tf_op | source)
XLA Modules:
  0.0 123.6 jit_solution(13261015578719349739)
XLA Ops:
  0.0 0.7 convert_bitcast_fusion
  0.7 0.1 copy.12
  0.8 0.8 copy.11
  1.6 3.0 %fusion.2 = bf16[128,4,8,256]{3,2,1,0:T(8,128)(2,1)S(1)} fusion(bf16[1,128,4,8,256]{4,3,2,1,0:T(8,128)(2,1)} %param.8, s32[128,4]{1,0:T(8,128)S(1)} %copy.11, pred[8]{0:T(512)(128)(4,1)S(1)} %iota_compare_fusion.2), kind=kLoop, calls=%fused_computation.5 | loop fusion | flops 3145728 | bytes 4196360 | tf_op jit(solution)/shard_map/jit(_where)/select_n | solution.py:278
  4.7 0.4 fusion.8
  5.1 1.7 %fusion.3 = bf16[128,9,8,128]{3,2,1,0:T(8,128)(2,1)} fusion(bf16[128,1,1,4]{3,2,1,0:T(2,128)(2,1)S(1)} %copy.12, bf16[128,4,8,128]{3,2,1,0:T(8,128)(2,1)S(1)} %get-tuple-element.14, bf16[128,4,8,128]{3,2,1,0:T(8,128)(2,1)S(1)} %get-tuple-element.13), kind=kLoop, calls=%fused_computation.8 | loop fusion | flops 9437184 | bytes 4457472 | tf_op jit(solution)/shard_map/concatenate | solution.py:282
  6.7 11.5 %all-to-all-start = ((bf16[128,9,8,128]{3,2,1,0:T(8,128)(2,1)}), bf16[128,9,8,128]{3,2,1,0:T(8,128)(2,1)S(1)}, u32[]{:S(2)}, u32[]{:S(2)}) async-start(bf16[128,9,8,128]{3,2,1,0:T(8,128)(2,1)} %fusion.3), calls=%async_computation | async-start | bytes 4718592 | tf_op jit(solution)/shard_map/all_to_all | solution.py:283
  18.4 0.1 fusion.4
  18.7 0.7 pad_maximum_fusion.1.even2_ref
  19.5 0.6 broadcast_multiply_fusion
  20.0 31.5 %all-to-all-done.tiles_ref = bf16[128,9,8,128]{3,2,1,0:T(8,128)(2,1)S(1)} async-done(((bf16[128,9,8,128]{3,2,1,0:T(8,128)(2,1)}), bf16[128,9,8,128]{3,2,1,0:T(8,128)(2,1)S(1)}, u32[]{:S(2)}, u32[]{:S(2)}) %all-to-all-start) | async-done | bytes 2359328 | tf_op jit(solution)/shard_map/all_to_all | solution.py:283
  51.6 15.4 %shard_map.82 = (bf16[24,1152]{1,0:T(8,128)(2,1)S(1)}, bf16[24,1152]{1,0:T(8,128)(2,1)S(1)}, bf16[24,128]{1,0:T(8,128)(2,1)S(1)}) custom-call(s32[128,4]{1,0:T(8,128)S(1)} %bitcast.26, s32[1]{0:T(128)} %bitcast.5.core_ref, bf16[128,9,8,128]{3,2,1,0:T(8,128)(2,1)S(1)} %all-to-all-done.tiles_ref), custom_call_target="tpu_custom_call" | custom-call | tf_op jit(solution)/shard_map/pallas_call | solution.py:122
  67.0 3.2 %collective-permute-start.2 = (bf16[24,128]{1,0:T(8,128)(2,1)S(1)}, bf16[24,128]{1,0:T(8,128)(2,1)S(1)}, u32[]{:S(2)}, u32[]{:S(2)}) collective-permute-start(bf16[24,128]{1,0:T(8,128)(2,1)S(1)} %get-tuple-element.10), channel_id=1, source_target_pairs={{1,32},{3,34},{5,36},{7,38},{9,40},{11,42},{13,44},{15,46},{17,48}... | collective-permute-start | bytes 18440 | tf_op jit(solution)/shard_map/ppermute | solution.py:293
  70.2 0.7 collective-permute-start.1
  70.9 1.1 collective-permute-start
  72.0 0.7 pad_maximum_fusion.2.even1_ref
  72.7 0.6 pad.34
  73.3 0.7 pad.35
  74.0 19.6 %all_gather.3.grid_ref = bf16[384,1152]{1,0:T(8,128)(2,1)} all-gather(bf16[24,1152]{1,0:T(8,128)(2,1)S(1)} %pad_add_fusion), channel_id=1, replica_groups={{0,2,4,6,8,10,12,14,16,18,20,22,24,26,28,30},{1,3,5,7,9,11,13,15,17,19,..., dimensions={0}, use_global_device_ids=true | all-gather | bytes 940032 | tf_op jit(solution)/shard_map/all_gather | solution.py:298
  93.6 13.9 %shard_map.83 = bf16[8,384,512]{2,1,0:T(8,128)(2,1)} custom-call(s32[1]{0:T(128)} %bitcast.top_ref, bf16[384,1152]{1,0:T(8,128)(2,1)} %all_gather.3.grid_ref, bf16[128,256]{1,0:T(8,128)(2,1)} %bitcast.32, bf16[256,256]{1,0:T(8,128)(2,1)} %bitcast.28, bf16[256,256]{1,0:T(8,128)(2,1)} %pad_maximum_fusion.2.even1_ref, ...), custom_call_target="tpu_custom_call" | custom-call | tf_op jit(solution)/shard_map/pallas_call | solution.py:216
  107.5 5.0 %collective-permute-start.3 = (bf16[8,384,512]{2,1,0:T(8,128)(2,1)}, bf16[8,384,512]{2,1,0:T(8,128)(2,1)S(1)}, u32[]{:S(2)}, u32[]{:S(2)}) collective-permute-start(bf16[8,384,512]{2,1,0:T(8,128)(2,1)} %shard_map.83), channel_id=1, source_target_pairs={{0,1},{1,0},{2,3},{3,2},{4,5},{5,4},{6,7},{7,6},{8,9},{9,8},{10,11... | collective-permute-start | bytes 9437192 | tf_op jit(solution)/shard_map/ppermute | solution.py:310
  112.5 5.5 %collective-permute-done.3 = bf16[8,384,512]{2,1,0:T(8,128)(2,1)S(1)} collective-permute-done((bf16[8,384,512]{2,1,0:T(8,128)(2,1)}, bf16[8,384,512]{2,1,0:T(8,128)(2,1)S(1)}, u32[]{:S(2)}, u32[]{:S(2)}) %collective-permute-start.3) | collective-permute-done | bytes 3145760 | tf_op jit(solution)/shard_map/ppermute | solution.py:310
  118.0 2.3 %broadcast_select_fusion.1 = (bf16[8,384,512]{2,1,0:T(8,128)(2,1)S(1)}, bf16[8,384,512]{2,1,0:T(8,128)(2,1)S(1)}) fusion(bf16[8,384,512]{2,1,0:T(8,128)(2,1)} %shard_map.83, bf16[8,384,512]{2,1,0:T(8,128)(2,1)S(1)} %collective-permute-done.3, pred[]{:T(512)S(6)} %eq.16), kind=kLoop, calls=%fused_computation.7 | loop fusion | flops 3145728 | bytes 12582913 | tf_op jit(solution)/shard_map/jit(_where)/select_n | solution.py:313
  120.3 3.2 %pad_maximum_fusion = bf16[16,384,512]{2,1,0:T(8,128)(2,1)} fusion(bf16[8,384,512]{2,1,0:T(8,128)(2,1)S(1)} %get-tuple-element.12, bf16[8,384,512]{2,1,0:T(8,128)(2,1)S(1)} %get-tuple-element.11), kind=kLoop, calls=%fused_computation | loop fusion | flops 3145728 | bytes 12582912 | tf_op jit(solution)/shard_map/concatenate | solution.py:312
  (23 shorter events, 0.3 us)
Async XLA Ops:
  0.0 18.4 %copy-start = (bf16[6,23]{1,0:T(8,128)(2,1)S(1)}, bf16[6,23]{1,0:T(8,128)(2,1)}, u32[]{:S(2)}) copy-start(bf16[6,23]{1,0:T(8,128)(2,1)} %param.11) | copy-start | bytes 832
  6.7 11.5 %copy-start.1 = (bf16[9,24,256]{2,1,0:T(8,128)(2,1)S(1)}, bf16[9,24,256]{2,1,0:T(8,128)(2,1)}, u32[]{:S(2)}) copy-start(bf16[9,24,256]{2,1,0:T(8,128)(2,1)} %param.12) | copy-start | bytes 331780
  6.7 12.7 %copy-start.2 = (f32[256]{0:T(256)S(1)}, f32[256]{0:T(256)}, u32[]{:S(2)}) copy-start(f32[256]{0:T(256)} %param.13) | copy-start | bytes 3076
  6.7 44.8 %all-to-all-start = ((bf16[128,9,8,128]{3,2,1,0:T(8,128)(2,1)}), bf16[128,9,8,128]{3,2,1,0:T(8,128)(2,1)S(1)}, u32[]{:S(2)}, u32[]{:S(2)}) async-start(bf16[128,9,8,128]{3,2,1,0:T(8,128)(2,1)} %fusion.3), calls=%async_computation | async-start | bytes 4718592 | tf_op jit(solution)/shard_map/all_to_all | solution.py:283
  67.0 6.9 %collective-permute-start.2 = (bf16[24,128]{1,0:T(8,128)(2,1)S(1)}, bf16[24,128]{1,0:T(8,128)(2,1)S(1)}, u32[]{:S(2)}, u32[]{:S(2)}) collective-permute-start(bf16[24,128]{1,0:T(8,128)(2,1)S(1)} %get-tuple-element.10), channel_id=1, source_target_pairs={{1,32},{3,34},{5,36},{7,38},{9,40},{11,42},{13,44},{15,46},{17,48}... | collective-permute-start | bytes 18440 | tf_op jit(solution)/shard_map/ppermute | solution.py:293
  70.2 3.7 %collective-permute-start.1 = (bf16[24,128]{1,0:T(8,128)(2,1)S(1)}, bf16[24,128]{1,0:T(8,128)(2,1)S(1)}, u32[]{:S(2)}, u32[]{:S(2)}) collective-permute-start(bf16[24,128]{1,0:T(8,128)(2,1)S(1)} %get-tuple-element.10), channel_id=1, source_target_pairs={{0,32},{2,34},{4,36},{6,38},{8,40},{10,42},{12,44},{14,46},{16,48}... | collective-permute-start | bytes 18440 | tf_op jit(solution)/shard_map/ppermute | solution.py:293
  70.9 3.1 %collective-permute-start = (bf16[24,1152]{1,0:T(8,128)(2,1)S(1)}, bf16[24,1152]{1,0:T(8,128)(2,1)S(1)}, u32[]{:S(2)}, u32[]{:S(2)}) collective-permute-start(bf16[24,1152]{1,0:T(8,128)(2,1)S(1)} %get-tuple-element.9), channel_id=1, source_target_pairs={{0,1},{1,0},{2,3},{3,2},{4,5},{5,4},{6,7},{7,6},{8,9},{9,8},{10,11... | collective-permute-start | bytes 165896 | tf_op jit(solution)/shard_map/ppermute | solution.py:288
  107.5 10.5 %collective-permute-start.3 = (bf16[8,384,512]{2,1,0:T(8,128)(2,1)}, bf16[8,384,512]{2,1,0:T(8,128)(2,1)S(1)}, u32[]{:S(2)}, u32[]{:S(2)}) collective-permute-start(bf16[8,384,512]{2,1,0:T(8,128)(2,1)} %shard_map.83), channel_id=1, source_target_pairs={{0,1},{1,0},{2,3},{3,2},{4,5},{5,4},{6,7},{7,6},{8,9},{9,8},{10,11... | collective-permute-start | bytes 9437192 | tf_op jit(solution)/shard_map/ppermute | solution.py:310

commit v2 on v1

--- a/solution.py
+++ b/solution.py
@@ -42,7 +42,12 @@
     def add_tile(source, slot, total):
         tile = jnp.concatenate([tiles_ref[source, slot], tiles_ref[source, slot + CAP]], axis=1)
         place = tile.astype(jnp.float32)
-        off_row = center_row - place[0:1] * ROOT_HALF_LOG2E
+        notes = tiles_ref[source, 2 * CAP]
+        live = jnp.concatenate(
+            [notes[2 * slot : 2 * slot + 1], notes[2 * slot + 1 : 2 * slot + 2]], axis=1
+        )
+        place_row = jnp.where(live.astype(jnp.float32) > 0.0, place[0:1], FAR)
+        off_row = center_row - place_row * ROOT_HALF_LOG2E
         off_col = center_col - place[1:2] * ROOT_HALF_LOG2E
         along_row = jnp.exp2(-(off_row * off_row)).astype(jnp.bfloat16)
         along_col = jnp.exp2(-(off_col * off_col)).astype(jnp.bfloat16)
@@ -140,13 +145,15 @@
 
 
 def conv_kernel(
-    top_ref, grid_ref, odd1_ref, odd2_ref, even1_ref, even2_ref, bias1_ref, weight2_ref,
-    bias2_ref, out_ref, moved_ref, even_rows, odd_rows,
+    place_ref, near_ref, east1_ref, east2_ref, east3_ref, odd1_ref, odd2_ref, even1_ref, even2_ref,
+    bias1_ref, weight2_ref, bias2_ref, *rest,
 ):
+    out_ref, send_ref, grid_ref, moved_ref, even_rows, odd_rows = rest[-6:]
     step = pl.program_id(0)
     columns = grid_ref.shape[0]
-
-    def first_row(t, step_rows):
+    quarter = near_ref.shape[0]
+
+    def first_row(t):
         block = t // 2
         if t % 2 == 0:
             here = grid_ref[:, 128 * block : 128 * block + 128]
@@ -169,7 +176,7 @@
         odd = activate(odd)
         even = activate(even)
         if t == 0:
-            live = top_ref[0].astype(jnp.float32)
+            live = place_ref[2].astype(jnp.float32)
             odd = odd * live
             even = even * live
         before = pltpu.roll(odd, 1, axis=0)
@@ -190,47 +197,66 @@
                 preferred_element_type=jnp.float32,
             )
             total = part if total is None else total + part
-        total = (total + bias2_ref[...]).astype(jnp.bfloat16)
-        out_ref[...] = total.reshape(out_ref.shape)
+        total = (total + bias2_ref[...]).astype(jnp.bfloat16).reshape(out_ref.shape)
+        out_ref[...] = total
+        send_ref[...] = total
 
     @pl.when(step == 0)
     def _():
+        for k, piece in enumerate((near_ref, east1_ref, east2_ref, east3_ref)):
+            at = pl.multiple_of((place_ref[1] + k) % 4 * quarter, quarter)
+            grid_ref[pl.ds(at, quarter), :] = piece[...]
         moved_ref[...] = pltpu.roll(grid_ref[...].astype(jnp.float32), 1, axis=0).astype(
             jnp.bfloat16
         )
-        first_row(0, 0)
-
-    for pair in range(4):
-
-        @pl.when(step == pair)
-        def _(pair=pair):
-            for t in range(4 * pair + 1, 4 * pair + 5):
-                first_row(t, 0)
-            second_rows(pair)
-
-
-def convolutions(top, gathered, weights1, bias1, weights2, bias2):
-    columns = gathered.shape[0]
+        for t in range(5):
+            first_row(t)
+        second_rows(0)
+
+    @pl.when(step == 1)
+    def _():
+        for t in range(5, 9):
+            first_row(t)
+        second_rows(1)
+
+
+def convolutions(part, place, pieces, weights1, bias1, weights2, bias2, whole):
+    columns = 4 * pieces[0].shape[0]
+    lanes = pieces[0].shape[1]
     full = lambda a: pl.BlockSpec(a.shape, lambda i, *_: (0,) * a.ndim)
-    operands = [gathered, *weights1, bias1, weights2, bias2]
+    operands = [*pieces, *weights1, bias1, weights2, bias2]
+    specs = [full(a) for a in operands]
+    aliases = {}
+    if whole is not None:
+        aliases = {1 + len(operands): 0}
+        operands.append(whole)
+        specs.append(pl.BlockSpec(memory_space=pl.ANY))
     return pl.pallas_call(
         conv_kernel,
         grid_spec=pltpu.PrefetchScalarGridSpec(
             num_scalar_prefetch=1,
-            grid=(4,),
-            in_specs=[full(a) for a in operands],
-            out_specs=pl.BlockSpec((2, columns, C2), lambda i, *_: (i, 0, 0)),
+            grid=(2,),
+            in_specs=specs,
+            out_specs=[
+                pl.BlockSpec((2, columns, C2), lambda i, place: (place[0] * 4 + 2 * part + i, 0, 0)),
+                pl.BlockSpec((2, columns, C2), lambda i, *_: (i, 0, 0)),
+            ],
             scratch_shapes=[
-                pltpu.VMEM(gathered.shape, jnp.bfloat16),
-                pltpu.VMEM((9 * columns, 3 * C1), jnp.bfloat16),
-                pltpu.VMEM((8 * columns, 3 * C1), jnp.bfloat16),
+                pltpu.VMEM((columns, lanes), jnp.bfloat16),
+                pltpu.VMEM((columns, lanes), jnp.bfloat16),
+                pltpu.VMEM((5 * columns, 3 * C1), jnp.bfloat16),
+                pltpu.VMEM((4 * columns, 3 * C1), jnp.bfloat16),
             ],
         ),
-        out_shape=jax.ShapeDtypeStruct((8, columns, C2), jnp.bfloat16),
+        out_shape=[
+            jax.ShapeDtypeStruct((16, columns, C2), jnp.bfloat16),
+            jax.ShapeDtypeStruct((4, columns, C2), jnp.bfloat16),
+        ],
+        input_output_aliases=aliases,
         compiler_params=pltpu.CompilerParams(
             dimension_semantics=("arbitrary",), vmem_limit_bytes=56 << 20
         ),
-    )(top, *operands)
+    )(place, *operands)
 
 
 def first_weights(embed_weight, conv1_weight):
@@ -274,14 +300,12 @@
     core = lax.axis_index("lon") % 2
 
     tiles = obs_tiles[0]
-    dead = iota(tiles.shape, 3) >= tile_rows[0][:, :, None, None]
-    tiles = jnp.where(dead & (iota(tiles.shape, 2) == 0), jnp.bfloat16(FAR), tiles)
-    notes = jnp.pad(
-        tile_block[0].astype(jnp.bfloat16)[:, None, None, :], ((0, 0), (0, 0), (0, 7), (0, 124))
-    )
-    leaving = jnp.concatenate([tiles[..., :128], tiles[..., 128:], notes], axis=1)
+    lanes = iota((blocks, 2 * CAP, 128), 2) + 128 * (iota((blocks, 2 * CAP, 128), 1) % 2)
+    twice = lambda a: jnp.repeat(a[0], 2, axis=1)[:, :, None]
+    notes = jnp.where(lanes < twice(tile_rows), twice(tile_block) + 1, 0).astype(jnp.bfloat16)
+    leaving = jnp.concatenate([tiles[..., :128], tiles[..., 128:], notes[:, None]], axis=1)
     arrived = lax.all_to_all(leaving, ("lat", "lon"), 0, 0, tiled=True)
-    subs = arrived[:, 2 * CAP, 0, :CAP].astype(jnp.int32)
+    subs = jnp.maximum(arrived[:, 2 * CAP, ::2, 0].astype(jnp.int32) - 1, 0)
     mine, send, tail = set_convolution(subs, core.reshape(1), arrived)
 
     pairs = [(i, i ^ 1) for i in range(n_lon)]
@@ -294,24 +318,43 @@
         tail, ("lat", "lon"), from_other
     )
     joined = mine + other + jnp.pad(halo, ((0, 0), (0, HALF_LANES - 128)))
-    groups = [[2 * k + c for k in range(n_lon // 2)] for c in range(2)]
-    gathered = lax.all_gather(joined, "lon", axis=0, tiled=True, axis_index_groups=groups)
-
     weights1 = first_weights(embed_weight, conv1_weight)
-    top = jnp.where((lax.axis_index("lat") == 0) & (core == 0), 0, 1).reshape(1)
-    half = convolutions(
-        top,
-        gathered,
-        weights1,
-        0.5 * conv1_bias[None],
-        conv2_weight.reshape(3, 3 * C1, C2),
-        conv2_bias[None],
-    )
-    swapped = lax.ppermute(half, "lon", pairs)
-    first = core == 0
-    return jnp.concatenate(
-        [jnp.where(first, half, swapped), jnp.where(first, swapped, half)], axis=0
-    )
+
+    def ring(value, stride, size):
+        def behind(i, k):
+            at = i // stride % size
+            return i + ((at - k) % size - at) * stride
+
+        return [lax.ppermute(value, "lon", [(i, behind(i, k)) for i in range(n_lon)]) for k in (1, 2, 3)]
+
+    lon = lax.axis_index("lon")
+    at_x, at_y = lon // 8, lon // 2 % 4
+    top = jnp.where((lax.axis_index("lat") == 0) & (core == 0), 0, 1)
+    whole = None
+    swapped = []
+    for part in range(2):
+        near = joined[:, 512 * part : 512 * part + 640]
+        ys = [near] + ring(near, 2, 4)
+        line = jnp.stack(ys + ys[:3])
+        quarter = lax.dynamic_slice_in_dim(line, (4 - at_y) % 4, 4).reshape(-1, line.shape[2])
+        pieces = [quarter] + ring(quarter, 8, 4)
+        place = jnp.stack([core, at_x, top if part == 0 else jnp.ones_like(top)]).astype(jnp.int32)
+        whole, half = convolutions(
+            part,
+            place,
+            pieces,
+            weights1,
+            0.5 * conv1_bias[None],
+            conv2_weight.reshape(3, 3 * C1, C2),
+            conv2_bias[None],
+            whole,
+        )
+        swapped.append(lax.ppermute(half, "lon", pairs))
+    for part in range(2):
+        whole = lax.dynamic_update_slice_in_dim(
+            whole, swapped[part], (1 - core) * 8 + 4 * part, axis=0
+        )
+    return whole
 
 
 def solution(mesh):

time: 124 us -> 133 us (1.073)
  blocking collectives: 19.6 us -> 0 us
  waiting for transfers between devices: 37 us -> 48.2 us
  starting transfers between devices: 21.4 us -> 32.2 us
  local copies, waits for them, and re-layouts: 2.71 us -> 11.4 us
  other arithmetic: 13.1 us -> 6.07 us
  Pallas kernels: 29.3 us -> 34.1 us
    all_gather x1 -> x0, blocking collectives: 19.6 us -> none  [shards(): lax.all_gather(joined, 'lon', axis=0, tiled=True, axis_index_groups=groups)]
    ppermute x1 -> x14, waiting for transfers between devices: 5.5 us -> 17.3 us  [the longest x12 15.3 us: ring(): lax.ppermute(value, 'lon', [(i, behind(i, k)) for i in range(n_lon)])]
    ppermute x1 -> x14, starting transfers between devices: 4.97 us -> 15.5 us  [the longest x12 10.5 us: ring(): lax.ppermute(value, 'lon', [(i, behind(i, k)) for i in range(n_lon)])]
    select_n x2 -> x0, other arithmetic: 5.35 us -> none  [the longest x1 3.05 us: shards(): jnp.where(dead & (iota(tiles.shape, 2) == 0), jnp.bfloat16(FAR), tiles)]
    pallas_call x1 -> x2, Pallas kernels: 13.9 us -> 18.6 us  [convolutions(): pl.pallas_call(conv_kernel, grid_spec=pltpu.PrefetchScalarGridSpec(num_sc...]
    concatenate x2 -> x1, other arithmetic: 4.93 us -> 1.69 us  [shards(): jnp.concatenate([tiles[..., :128], tiles[..., 128:], notes[:, None]], axi...]
    slice x0 -> x2, local copies, waits for them, and re-layouts: none -> 3.04 us  [the longest x1 3.03 us: shards(): subs = jnp.maximum(arrived[:, 2 * CAP, ::2, 0].astype(jnp.int32) - 1, 0)]
    dynamic_update_slice x0 -> x2, local copies, waits for them, and re-layouts: none -> 2.49 us  [shards(): lax.dynamic_update_slice_in_dim(whole, swapped[part], (1 - core) * 8 + 4...]
  transfers between devices with their start and end apart: 5 -> 18, of which waited for: 2 -> 10; matrix products, arithmetic and copies ran while one was open for 3% -> 5% of each run, Pallas kernels for 0% -> 7%
where the time goes in v2:
time: 133 us; the launch traced here: 132 us
  waiting for transfers between devices  48.2 us (36%)
  Pallas kernels  34.1 us (26%)
  starting transfers between devices  32.2 us (24%)
  local copies, waits for them, and re-layouts  11.4 us (9%)
  other arithmetic  6.07 us (5%)
    all_to_all x1, waiting for transfers between devices, shards(): arrived = lax.all_to_all(leaving, ('lat', 'lon'), 0, 0, tiled=True)  30.9 us
    pallas_call x2, Pallas kernels, convolutions(): pl.pallas_call(conv_kernel, grid_spec=pltpu.PrefetchScalarGridSpec(num_sc...  18.6 us
    pallas_call x1, Pallas kernels, set_convolution(): pl.pallas_call(setconv_kernel, grid_spec=pltpu.PrefetchScalarGridSpec(num...  15.5 us
    ppermute x12, waiting for transfers between devices, ring(): lax.ppermute(value, 'lon', [(i, behind(i, k)) for i in range(n_lon)])  15.3 us
    all_to_all x1, starting transfers between devices, shards(): arrived = lax.all_to_all(leaving, ('lat', 'lon'), 0, 0, tiled=True)  11.5 us
    ppermute x12, starting transfers between devices, ring(): lax.ppermute(value, 'lon', [(i, behind(i, k)) for i in range(n_lon)])  10.5 us
    ppermute x2, starting transfers between devices, shards(): swapped.append(lax.ppermute(half, 'lon', pairs))  4.94 us
    ppermute x1, starting transfers between devices, shards(): lax.ppermute(tail, ('lat', 'lon'), from_other)  4.47 us
  transfers between devices with their start and end apart: 18, of which 10 were waited for; matrix products, arithmetic and copies ran while one was open for 5% of the time, Pallas kernels for 7%

profile of v2, /device:TPU:1, one launch (start us, length us, event | category | flops | bytes accessed | tf_op | source)
XLA Modules:
  0.0 132.5 jit_solution(10538565318372263203)
XLA Ops:
  1.6 1.9 %fusion.4 = (bf16[128,4,8,128]{3,2,1,0:T(8,128)(2,1)S(1)}, bf16[128,4,8,128]{3,2,1,0:T(8,128)(2,1)S(1)}) fusion(bf16[128,4,8,256]{3,2,1,0:T(8,128)(2,1)} %bitcast.54), kind=kLoop, calls=%fused_computation.38 | loop fusion | bytes 4194304 | tf_op jit(solution)/shard_map/slice | solution.py:306
  3.9 1.7 %pad_maximum_fusion = bf16[128,9,8,128]{3,2,1,0:T(8,128)(2,1)} fusion(bf16[128,1,8,128]{3,2,1,0:T(8,128)(2,1)S(1)} %select_convert_fusion, bf16[128,4,8,128]{3,2,1,0:T(8,128)(2,1)S(1)} %get-tuple-element.20, bf16[128,4,8,128]{3,2,1,0:T(8,128)(2,1)S(1)} %get-tuple-element.19), kind=kLoop, calls=%fused_computation | loop fusion | flops 2359296 | bytes 4718592 | tf_op jit(solution)/shard_map/concatenate | solution.py:306
  5.6 11.5 %all-to-all-start = ((bf16[128,9,8,128]{3,2,1,0:T(8,128)(2,1)}), bf16[128,9,8,128]{3,2,1,0:T(8,128)(2,1)S(1)}, u32[]{:S(2)}, u32[]{:S(2)}) async-start(bf16[128,9,8,128]{3,2,1,0:T(8,128)(2,1)} %pad_maximum_fusion), calls=%async_computation | async-start | bytes 4718592 | tf_op jit(solution)/shard_map/all_to_all | solution.py:307
  19.5 30.9 %all-to-all-done.tiles_ref = bf16[128,9,8,128]{3,2,1,0:T(8,128)(2,1)S(1)} async-done(((bf16[128,9,8,128]{3,2,1,0:T(8,128)(2,1)}), bf16[128,9,8,128]{3,2,1,0:T(8,128)(2,1)S(1)}, u32[]{:S(2)}, u32[]{:S(2)}) %all-to-all-start) | async-done | bytes 2359328 | tf_op jit(solution)/shard_map/all_to_all | solution.py:307
  50.4 3.0 %slice.32 = bf16[128,1,4,1]{3,2,1,0:T(4,128)(2,1)S(1)} slice(bf16[128,9,8,128]{3,2,1,0:T(8,128)(2,1)S(1)} %all-to-all-done.tiles_ref), slice={[0:128:1], [8:9:1], [0:8:2], [0:1:1]} | slice | bytes 2048 | tf_op jit(solution)/shard_map/slice | solution.py:308
  53.8 15.5 %shard_map.82 = (bf16[24,1152]{1,0:T(8,128)(2,1)S(1)}, bf16[24,1152]{1,0:T(8,128)(2,1)S(1)}, bf16[24,128]{1,0:T(8,128)(2,1)S(1)}) custom-call(s32[128,4]{1,0:T(8,128)S(1)} %copy.19.sub_ref, s32[1]{0:T(128)} %bitcast.core_ref, bf16[128,9,8,128]{3,2,1,0:T(8,128)(2,1)S(1)} %all-to-all-done.tiles_ref), custom_call_target="tpu_custom_call" | custom-call | tf_op jit(solution)/shard_map/pallas_call | solution.py:127
  69.9 4.5 %collective-permute-start.2 = (bf16[24,128]{1,0:T(8,128)(2,1)S(1)}, bf16[24,128]{1,0:T(8,128)(2,1)S(1)}, u32[]{:S(2)}, u32[]{:S(2)}) collective-permute-start(bf16[24,128]{1,0:T(8,128)(2,1)S(1)} %get-tuple-element.14), channel_id=1, source_target_pairs={{1,32},{3,34},{5,36},{7,38},{9,40},{11,42},{13,44},{15,46},{17,48}... | collective-permute-start | bytes 18440 | tf_op jit(solution)/shard_map/ppermute | solution.py:317
  78.2 2.2 %collective-permute-start.9 = (bf16[24,640]{1,0:T(8,128)(2,1)S(1)}, bf16[24,640]{1,0:T(8,128)(2,1)S(1)}, u32[]{:S(2)}, u32[]{:S(2)}) collective-permute-start(bf16[24,640]{1,0:T(8,128)(2,1)S(1)} %get-tuple-element.23), channel_id=1, source_target_pairs={{0,6},{1,7},{2,0},{3,1},{4,2},{5,3},{6,4},{7,5},{8,14},{9,15},{10,... | collective-permute-start | bytes 92168 | tf_op jit(solution)/shard_map/ppermute | solution.py:328
  80.5 1.2 collective-permute-start.10
  82.5 2.2 %collective-permute-done.10 = bf16[24,640]{1,0:T(8,128)(2,1)S(1)} collective-permute-done((bf16[24,640]{1,0:T(8,128)(2,1)S(1)}, bf16[24,640]{1,0:T(8,128)(2,1)S(1)}, u32[]{:S(2)}, u32[]{:S(2)}) %collective-permute-start.10) | collective-permute-done | bytes 30752 | tf_op jit(solution)/shard_map/ppermute | solution.py:328
  86.6 1.3 collective-permute-start.13
  88.0 1.5 %collective-permute-done.12.east1_ref = bf16[96,640]{1,0:T(8,128)(2,1)S(1)} collective-permute-done((bf16[96,640]{1,0:T(8,128)(2,1)S(1)}, bf16[96,640]{1,0:T(8,128)(2,1)S(1)}, u32[]{:S(2)}, u32[]{:S(2)}) %collective-permute-start.12) | collective-permute-done | bytes 122912 | tf_op jit(solution)/shard_map/ppermute | solution.py:328
  89.5 2.4 %collective-permute-done.13.east2_ref = bf16[96,640]{1,0:T(8,128)(2,1)S(1)} collective-permute-done((bf16[96,640]{1,0:T(8,128)(2,1)S(1)}, bf16[96,640]{1,0:T(8,128)(2,1)S(1)}, u32[]{:S(2)}, u32[]{:S(2)}) %collective-permute-start.13) | collective-permute-done | bytes 122912 | tf_op jit(solution)/shard_map/ppermute | solution.py:328
  91.9 1.3 collective-permute-done.14.east3_ref
  93.8 9.3 %shard_map.83 = (bf16[16,384,512]{2,1,0:T(8,128)(2,1)}, bf16[4,384,512]{2,1,0:T(8,128)(2,1)}) custom-call(s32[3]{0:T(128)} %pad_add_fusion.3.place_ref, bf16[96,640]{1,0:T(8,128)(2,1)} %bitcast.64, bf16[96,640]{1,0:T(8,128)(2,1)} %copy-done.4, bf16[96,640]{1,0:T(8,128)(2,1)} %copy-done.5, bf16[96,640]{1,0:T(8,128)(2,1)} %copy-done.6, ...), custom_call_target="tpu_custom_call" | custom-call | tf_op jit(solution)/shard_map/pallas_call | solution.py:234
  103.1 4.5 %collective-permute-start.15 = (bf16[4,384,512]{2,1,0:T(8,128)(2,1)}, bf16[4,384,512]{2,1,0:T(8,128)(2,1)S(1)}, u32[]{:S(2)}, u32[]{:S(2)}) collective-permute-start(bf16[4,384,512]{2,1,0:T(8,128)(2,1)} %get-tuple-element.17), channel_id=1, source_target_pairs={{0,1},{1,0},{2,3},{3,2},{4,5},{5,4},{6,7},{7,6},{8,9},{9,8},{10,11... | collective-permute-start | bytes 4718600 | tf_op jit(solution)/shard_map/ppermute | solution.py:352
  108.1 1.2 collective-permute-start.7
  110.4 2.2 %collective-permute-done.6.east1_ref = bf16[96,640]{1,0:T(8,128)(2,1)S(1)} collective-permute-done((bf16[96,640]{1,0:T(8,128)(2,1)S(1)}, bf16[96,640]{1,0:T(8,128)(2,1)S(1)}, u32[]{:S(2)}, u32[]{:S(2)}) %collective-permute-start.6) | collective-permute-done | bytes 122912 | tf_op jit(solution)/shard_map/ppermute | solution.py:328
  112.6 1.6 %collective-permute-done.7.east2_ref = bf16[96,640]{1,0:T(8,128)(2,1)S(1)} collective-permute-done((bf16[96,640]{1,0:T(8,128)(2,1)S(1)}, bf16[96,640]{1,0:T(8,128)(2,1)S(1)}, u32[]{:S(2)}, u32[]{:S(2)}) %collective-permute-start.7) | collective-permute-done | bytes 122912 | tf_op jit(solution)/shard_map/ppermute | solution.py:328
  114.3 3.3 %collective-permute-done.8.east3_ref = bf16[96,640]{1,0:T(8,128)(2,1)S(1)} collective-permute-done((bf16[96,640]{1,0:T(8,128)(2,1)S(1)}, bf16[96,640]{1,0:T(8,128)(2,1)S(1)}, u32[]{:S(2)}, u32[]{:S(2)}) %collective-permute-start.8) | collective-permute-done | bytes 122912 | tf_op jit(solution)/shard_map/ppermute | solution.py:328
  118.2 9.3 %shard_map.84 = (bf16[16,384,512]{2,1,0:T(8,128)(2,1)}, bf16[4,384,512]{2,1,0:T(8,128)(2,1)}) custom-call(s32[3]{0:T(128)} %pad_add_fusion.1.place_ref, bf16[96,640]{1,0:T(8,128)(2,1)} %bitcast.68, bf16[96,640]{1,0:T(8,128)(2,1)} %copy-done.7, bf16[96,640]{1,0:T(8,128)(2,1)} %copy-done.8, ...), custom_call_target="tpu_custom_call", output_to_operand_aliasing={{0}: (12, {})} | custom-call | tf_op jit(solution)/shard_map/pallas_call | solution.py:234
  128.0 1.2 constant_dynamic-update-slice_fusion.15
  129.2 2.0 %collective-permute-done.16 = bf16[4,384,512]{2,1,0:T(8,128)(2,1)S(1)} collective-permute-done((bf16[4,384,512]{2,1,0:T(8,128)(2,1)}, bf16[4,384,512]{2,1,0:T(8,128)(2,1)S(1)}, u32[]{:S(2)}, u32[]{:S(2)}) %collective-permute-start.16) | collective-permute-done | bytes 1572896 | tf_op jit(solution)/shard_map/ppermute | solution.py:352
  131.2 1.2 constant_dynamic-update-slice_fusion.14
  (88 shorter events, 15.3 us)
Async XLA Ops:
  0.0 17.2 %copy-start = (bf16[6,23]{1,0:T(8,128)(2,1)S(1)}, bf16[6,23]{1,0:T(8,128)(2,1)}, u32[]{:S(2)}) copy-start(bf16[6,23]{1,0:T(8,128)(2,1)} %param.11) | copy-start | bytes 832
  5.5 11.5 %copy-start.3 = (bf16[9,24,256]{2,1,0:T(8,128)(2,1)S(1)}, bf16[9,24,256]{2,1,0:T(8,128)(2,1)}, u32[]{:S(2)}) copy-start(bf16[9,24,256]{2,1,0:T(8,128)(2,1)} %param.12) | copy-start | bytes 331780
  5.5 13.4 %copy-start.10 = (f32[256]{0:T(256)S(1)}, f32[256]{0:T(256)}, u32[]{:S(2)}) copy-start(f32[256]{0:T(256)} %param.13) | copy-start | bytes 3076
  5.6 44.8 %all-to-all-start = ((bf16[128,9,8,128]{3,2,1,0:T(8,128)(2,1)}), bf16[128,9,8,128]{3,2,1,0:T(8,128)(2,1)S(1)}, u32[]{:S(2)}, u32[]{:S(2)}) async-start(bf16[128,9,8,128]{3,2,1,0:T(8,128)(2,1)} %pad_maximum_fusion), calls=%async_computation | async-start | bytes 4718592 | tf_op jit(solution)/shard_map/all_to_all | solution.py:307
  69.3 7.1 %collective-permute-start.1 = (bf16[24,128]{1,0:T(8,128)(2,1)S(1)}, bf16[24,128]{1,0:T(8,128)(2,1)S(1)}, u32[]{:S(2)}, u32[]{:S(2)}) collective-permute-start(bf16[24,128]{1,0:T(8,128)(2,1)S(1)} %get-tuple-element.14), channel_id=1, source_target_pairs={{0,32},{2,34},{4,36},{6,38},{8,40},{10,42},{12,44},{14,46},{16,48}... | collective-permute-start | bytes 18440 | tf_op jit(solution)/shard_map/ppermute | solution.py:317
  69.9 6.5 %collective-permute-start.2 = (bf16[24,128]{1,0:T(8,128)(2,1)S(1)}, bf16[24,128]{1,0:T(8,128)(2,1)S(1)}, u32[]{:S(2)}, u32[]{:S(2)}) collective-permute-start(bf16[24,128]{1,0:T(8,128)(2,1)S(1)} %get-tuple-element.14), channel_id=1, source_target_pairs={{1,32},{3,34},{5,36},{7,38},{9,40},{11,42},{13,44},{15,46},{17,48}... | collective-permute-start | bytes 18440 | tf_op jit(solution)/shard_map/ppermute | solution.py:317
  74.4 2.0 %collective-permute-start = (bf16[24,1152]{1,0:T(8,128)(2,1)S(1)}, bf16[24,1152]{1,0:T(8,128)(2,1)S(1)}, u32[]{:S(2)}, u32[]{:S(2)}) collective-permute-start(bf16[24,1152]{1,0:T(8,128)(2,1)S(1)} %get-tuple-element.13), channel_id=1, source_target_pairs={{0,1},{1,0},{2,3},{3,2},{4,5},{5,4},{6,7},{7,6},{8,9},{9,8},{10,11... | collective-permute-start | bytes 165896 | tf_op jit(solution)/shard_map/ppermute | solution.py:312
  76.5 5.2 %collective-permute-start.3 = (bf16[24,640]{1,0:T(8,128)(2,1)S(1)}, bf16[24,640]{1,0:T(8,128)(2,1)S(1)}, u32[]{:S(2)}, u32[]{:S(2)}) collective-permute-start(bf16[24,640]{1,0:T(8,128)(2,1)S(1)} %get-tuple-element.24), channel_id=1, source_target_pairs={{0,6},{1,7},{2,0},{3,1},{4,2},{5,3},{6,4},{7,5},{8,14},{9,15},{10,... | collective-permute-start | bytes 92168 | tf_op jit(solution)/shard_map/ppermute | solution.py:328
  77.2 5.3 %collective-permute-start.4 = (bf16[24,640]{1,0:T(8,128)(2,1)S(1)}, bf16[24,640]{1,0:T(8,128)(2,1)S(1)}, u32[]{:S(2)}, u32[]{:S(2)}) collective-permute-start(bf16[24,640]{1,0:T(8,128)(2,1)S(1)} %get-tuple-element.24), channel_id=1, source_target_pairs={{0,4},{1,5},{2,6},{3,7},{4,0},{5,1},{6,2},{7,3},{8,12},{9,13},{10,... | collective-permute-start | bytes 92168 | tf_op jit(solution)/shard_map/ppermute | solution.py:328
  77.8 4.7 %collective-permute-start.5 = (bf16[24,640]{1,0:T(8,128)(2,1)S(1)}, bf16[24,640]{1,0:T(8,128)(2,1)S(1)}, u32[]{:S(2)}, u32[]{:S(2)}) collective-permute-start(bf16[24,640]{1,0:T(8,128)(2,1)S(1)} %get-tuple-element.24), channel_id=1, source_target_pairs={{0,2},{1,3},{2,4},{3,5},{4,6},{5,7},{6,0},{7,1},{8,10},{9,11},{10,... | collective-permute-start | bytes 92168 | tf_op jit(solution)/shard_map/ppermute | solution.py:328
  78.2 4.3 %collective-permute-start.9 = (bf16[24,640]{1,0:T(8,128)(2,1)S(1)}, bf16[24,640]{1,0:T(8,128)(2,1)S(1)}, u32[]{:S(2)}, u32[]{:S(2)}) collective-permute-start(bf16[24,640]{1,0:T(8,128)(2,1)S(1)} %get-tuple-element.23), channel_id=1, source_target_pairs={{0,6},{1,7},{2,0},{3,1},{4,2},{5,3},{6,4},{7,5},{8,14},{9,15},{10,... | collective-permute-start | bytes 92168 | tf_op jit(solution)/shard_map/ppermute | solution.py:328
  80.5 4.2 %collective-permute-start.10 = (bf16[24,640]{1,0:T(8,128)(2,1)S(1)}, bf16[24,640]{1,0:T(8,128)(2,1)S(1)}, u32[]{:S(2)}, u32[]{:S(2)}) collective-permute-start(bf16[24,640]{1,0:T(8,128)(2,1)S(1)} %get-tuple-element.23), channel_id=1, source_target_pairs={{0,4},{1,5},{2,6},{3,7},{4,0},{5,1},{6,2},{7,3},{8,12},{9,13},{10,... | collective-permute-start | bytes 92168 | tf_op jit(solution)/shard_map/ppermute | solution.py:328
  81.6 4.0 %collective-permute-start.11 = (bf16[24,640]{1,0:T(8,128)(2,1)S(1)}, bf16[24,640]{1,0:T(8,128)(2,1)S(1)}, u32[]{:S(2)}, u32[]{:S(2)}) collective-permute-start(bf16[24,640]{1,0:T(8,128)(2,1)S(1)} %get-tuple-element.23), channel_id=1, source_target_pairs={{0,2},{1,3},{2,4},{3,5},{4,6},{5,7},{6,0},{7,1},{8,10},{9,11},{10,... | collective-permute-start | bytes 92168 | tf_op jit(solution)/shard_map/ppermute | solution.py:328
  85.7 7.5 %copy-start.1 = (bf16[4,24,640]{2,1,0:T(8,128)(2,1)}, bf16[4,24,640]{2,1,0:T(8,128)(2,1)S(1)}, u32[]{:S(2)}) copy-start(bf16[4,24,640]{2,1,0:T(8,128)(2,1)S(1)} %constant_dynamic-slice_fusion) | copy-start | bytes 368644
  85.7 3.8 %collective-permute-start.12 = (bf16[96,640]{1,0:T(8,128)(2,1)S(1)}, bf16[96,640]{1,0:T(8,128)(2,1)S(1)}, u32[]{:S(2)}, u32[]{:S(2)}) collective-permute-start(bf16[96,640]{1,0:T(8,128)(2,1)S(1)} %bitcast.61), channel_id=1, source_target_pairs={{0,24},{1,25},{2,26},{3,27},{4,28},{5,29},{6,30},{7,31},{8,0},{9,1... | collective-permute-start | bytes 368648 | tf_op jit(solution)/shard_map/ppermute | solution.py:328
  86.6 5.3 %collective-permute-start.13 = (bf16[96,640]{1,0:T(8,128)(2,1)S(1)}, bf16[96,640]{1,0:T(8,128)(2,1)S(1)}, u32[]{:S(2)}, u32[]{:S(2)}) collective-permute-start(bf16[96,640]{1,0:T(8,128)(2,1)S(1)} %bitcast.62), channel_id=1, source_target_pairs={{0,16},{1,17},{2,18},{3,19},{4,20},{5,21},{6,22},{7,23},{8,24},{9,... | collective-permute-start | bytes 368648 | tf_op jit(solution)/shard_map/ppermute | solution.py:328
  87.9 5.2 %collective-permute-start.14 = (bf16[96,640]{1,0:T(8,128)(2,1)S(1)}, bf16[96,640]{1,0:T(8,128)(2,1)S(1)}, u32[]{:S(2)}, u32[]{:S(2)}) collective-permute-start(bf16[96,640]{1,0:T(8,128)(2,1)S(1)} %bitcast.63), channel_id=1, source_target_pairs={{0,8},{1,9},{2,10},{3,11},{4,12},{5,13},{6,14},{7,15},{8,16},{9,17... | collective-permute-start | bytes 368648 | tf_op jit(solution)/shard_map/ppermute | solution.py:328
  103.1 24.8 %collective-permute-start.15 = (bf16[4,384,512]{2,1,0:T(8,128)(2,1)}, bf16[4,384,512]{2,1,0:T(8,128)(2,1)S(1)}, u32[]{:S(2)}, u32[]{:S(2)}) collective-permute-start(bf16[4,384,512]{2,1,0:T(8,128)(2,1)} %get-tuple-element.17), channel_id=1, source_target_pairs={{0,1},{1,0},{2,3},{3,2},{4,5},{5,4},{6,7},{7,6},{8,9},{9,8},{10,11... | collective-permute-start | bytes 4718600 | tf_op jit(solution)/shard_map/ppermute | solution.py:352
  107.6 9.9 %copy-start.2 = (bf16[4,24,640]{2,1,0:T(8,128)(2,1)}, bf16[4,24,640]{2,1,0:T(8,128)(2,1)S(1)}, u32[]{:S(2)}) copy-start(bf16[4,24,640]{2,1,0:T(8,128)(2,1)S(1)} %constant_dynamic-slice_fusion.1) | copy-start | bytes 368644
  107.6 5.0 %collective-permute-start.6 = (bf16[96,640]{1,0:T(8,128)(2,1)S(1)}, bf16[96,640]{1,0:T(8,128)(2,1)S(1)}, u32[]{:S(2)}, u32[]{:S(2)}) collective-permute-start(bf16[96,640]{1,0:T(8,128)(2,1)S(1)} %bitcast.65), channel_id=1, source_target_pairs={{0,24},{1,25},{2,26},{3,27},{4,28},{5,29},{6,30},{7,31},{8,0},{9,1... | collective-permute-start | bytes 368648 | tf_op jit(solution)/shard_map/ppermute | solution.py:328
  108.1 6.1 %collective-permute-start.7 = (bf16[96,640]{1,0:T(8,128)(2,1)S(1)}, bf16[96,640]{1,0:T(8,128)(2,1)S(1)}, u32[]{:S(2)}, u32[]{:S(2)}) collective-permute-start(bf16[96,640]{1,0:T(8,128)(2,1)S(1)} %bitcast.66), channel_id=1, source_target_pairs={{0,16},{1,17},{2,18},{3,19},{4,20},{5,21},{6,22},{7,23},{8,24},{9,... | collective-permute-start | bytes 368648 | tf_op jit(solution)/shard_map/ppermute | solution.py:328
  109.3 8.2 %collective-permute-start.8 = (bf16[96,640]{1,0:T(8,128)(2,1)S(1)}, bf16[96,640]{1,0:T(8,128)(2,1)S(1)}, u32[]{:S(2)}, u32[]{:S(2)}) collective-permute-start(bf16[96,640]{1,0:T(8,128)(2,1)S(1)} %bitcast.67), channel_id=1, source_target_pairs={{0,8},{1,9},{2,10},{3,11},{4,12},{5,13},{6,14},{7,15},{8,16},{9,17... | collective-permute-start | bytes 368648 | tf_op jit(solution)/shard_map/ppermute | solution.py:328
  112.6 4.9 %copy-start.7 = (bf16[96,640]{1,0:T(8,128)(2,1)}, bf16[96,640]{1,0:T(8,128)(2,1)S(1)}, u32[]{:S(2)}) copy-start(bf16[96,640]{1,0:T(8,128)(2,1)S(1)} %collective-permute-done.6.east1_ref) | copy-start | bytes 368644
  127.5 3.7 %collective-permute-start.16 = (bf16[4,384,512]{2,1,0:T(8,128)(2,1)}, bf16[4,384,512]{2,1,0:T(8,128)(2,1)S(1)}, u32[]{:S(2)}, u32[]{:S(2)}) collective-permute-start(bf16[4,384,512]{2,1,0:T(8,128)(2,1)} %get-tuple-element.18), channel_id=1, source_target_pairs={{0,1},{1,0},{2,3},{3,2},{4,5},{5,4},{6,7},{7,6},{8,9},{9,8},{10,11... | collective-permute-start | bytes 4718600 | tf_op jit(solution)/shard_map/ppermute | solution.py:352
  (5 other events, 9.6 us)

commit v3 on v2

v3 whole, which is shorter than its diff:
```python
import functools

import jax
import jax.numpy as jnp
from jax import lax
from jax.experimental import pallas as pl
from jax.experimental.pallas import tpu as pltpu
from jax.sharding import PartitionSpec as P

BX = 64
BY = 48
SB = 16
TILE = 256
CAP = 4
FEAT = 8
C1 = 256
C2 = 512
SUBS = 12
PHASES = 4
QUADS = BY // PHASES
ROW_LANES = PHASES * FEAT
FAR = 8192.0
ROOT_HALF_LOG2E = (0.5 * 1.4426950408889634) ** 0.5
SOURCES = 16


def iota(shape, axis):
    return lax.broadcasted_iota(jnp.int32, shape, axis)


def setconv_kernel(note_ref, tiles_ref, out_ref, *sums):
    step = pl.program_id(0)

    @pl.when(step == 0)
    def _():
        for total in sums:
            total[...] = jnp.zeros_like(total)

    row = iota((SB, 1), 0)
    lane = iota((1, TILE), 1)
    center_row = (row.astype(jnp.float32) + 0.5) * ROOT_HALF_LOG2E
    center_col = ((row % 4 * 4 + row // 4).astype(jnp.float32) + 0.5) * ROOT_HALF_LOG2E

    def add_tile(source, slot, total):
        tile = jnp.concatenate([tiles_ref[source, slot], tiles_ref[source, slot + CAP]], axis=1)
        place = tile.astype(jnp.float32)
        live = lane < note_ref[step * SOURCES + source, CAP + slot]
        place_row = jnp.where(live, place[0:1], FAR)
        off_row = center_row - place_row * ROOT_HALF_LOG2E
        off_col = center_col - place[1:2] * ROOT_HALF_LOG2E
        along_row = jnp.exp2(-(off_row * off_row)).astype(jnp.bfloat16)
        along_col = jnp.exp2(-(off_col * off_col)).astype(jnp.bfloat16)
        weighted = [along_row, jnp.zeros_like(along_row)]
        weighted += [tile[k : k + 1] * along_row for k in range(2, FEAT)]
        part = lax.dot_general(
            along_col,
            jnp.concatenate(weighted, axis=0),
            (((1,), (1,)), ((), ())),
            preferred_element_type=jnp.float32,
        )
        sub = note_ref[step * SOURCES + source, slot]
        total[sub] = total[sub] + part

    def add_sources(m, carry):
        for k in range(4):
            for slot in range(CAP):
                add_tile(4 * m + k, slot, sums[slot])
        return carry

    lax.fori_loop(0, SOURCES // 4, add_sources, 0)

    @pl.when(step == pl.num_programs(0) - 1)
    def _():
        total = sums[0][...]
        for more in sums[1:]:
            total = total + more[...]
        total = total.reshape(SUBS * SB, FEAT * SB)
        pick = (iota((128, 128), 0) == iota((128, 128), 1) % SB).astype(jnp.float32)
        density = jnp.dot(
            total, pick, precision=lax.Precision.HIGHEST, preferred_element_type=jnp.float32
        )
        lane = iota((SUBS * SB, 128), 1)
        grid = jnp.where(lane < SB, jnp.log1p(density), total / (1.0 + density))
        grid = grid.astype(jnp.bfloat16)
        target = iota((4 * SB, SUBS * SB), 0)
        source = iota((4 * SB, SUBS * SB), 1)
        quad = target % SB
        wanted = target // SB * BY + quad // 4 * SB + quad % 4
        parts = []
        for phase in range(PHASES):
            take = ((quad < QUADS) & (source == wanted + 4 * phase)).astype(jnp.bfloat16)
            parts.append(
                jnp.dot(take, grid, preferred_element_type=jnp.float32).astype(jnp.bfloat16)
            )
        spread = jnp.concatenate(parts, axis=1)
        lane_in = iota((512, 512), 0)
        lane_out = iota((512, 512), 1)
        moved = (
            lane_in % SB * ROW_LANES + lane_in // 128 * FEAT + lane_in % 128 // SB == lane_out
        ).astype(jnp.bfloat16)
        ordered = jnp.dot(spread, moved, preferred_element_type=jnp.float32).astype(jnp.bfloat16)
        to = iota((8 * QUADS, 4 * SB), 0)
        start = iota((8 * QUADS, 4 * SB), 1)
        for half in range(2):
            rows = None
            for k in range(4):
                take = (to // QUADS % 4 == k) & (
                    start == (2 * half + to // (4 * QUADS)) * SB + to % QUADS
                )
                part = jnp.dot(
                    take.astype(jnp.bfloat16),
                    ordered[:, 128 * k : 128 * k + 128],
                    preferred_element_type=jnp.float32,
                )
                rows = part if rows is None else rows + part
            rows = rows.astype(jnp.bfloat16)
            for k in range(out_ref.shape[0] // 2):
                out_ref[2 * k + half] = rows


def set_convolution(notes, arrived, copies):
    out = jax.ShapeDtypeStruct((copies, 8 * QUADS, 128), jnp.bfloat16)
    return pl.pallas_call(
        setconv_kernel,
        grid_spec=pltpu.PrefetchScalarGridSpec(
            num_scalar_prefetch=1,
            grid=(arrived.shape[0] // SOURCES,),
            in_specs=[pl.BlockSpec((SOURCES,) + arrived.shape[1:], lambda i, *_: (i, 0, 0, 0))],
            out_specs=pl.BlockSpec(out.shape, lambda i, *_: (0, 0, 0)),
            scratch_shapes=[pltpu.VMEM((SUBS, SB, FEAT * SB), jnp.float32)] * CAP,
        ),
        out_shape=out,
        compiler_params=pltpu.CompilerParams(
            dimension_semantics=("arbitrary",), vmem_limit_bytes=24 << 20
        ),
    )(notes, arrived)


def leave_kernel(tiles_ref, notes_ref, out_ref):
    out_ref[:, :CAP] = tiles_ref[:, :, :, :128]
    out_ref[:, CAP : 2 * CAP] = tiles_ref[:, :, :, 128:]
    out_ref[:, 2 * CAP] = notes_ref[...]


def leaving_tiles(tiles, notes):
    count = tiles.shape[0]
    return pl.pallas_call(
        leave_kernel,
        grid=(count // SOURCES,),
        in_specs=[
            pl.BlockSpec((SOURCES,) + tiles.shape[1:], lambda i: (i, 0, 0, 0)),
            pl.BlockSpec((SOURCES,) + notes.shape[1:], lambda i: (i, 0, 0)),
        ],
        out_specs=pl.BlockSpec((SOURCES, 2 * CAP + 1, FEAT, 128), lambda i: (i, 0, 0, 0)),
        out_shape=jax.ShapeDtypeStruct((count, 2 * CAP + 1, FEAT, 128), jnp.bfloat16),
        compiler_params=pltpu.CompilerParams(vmem_limit_bytes=60 << 20),
    )(tiles, notes)


def conv_kernel(first_block, *refs):
    (flag_ref, *halo, own_ref, odd1_ref, odd2_ref, even1_ref, even2_ref, bias1_ref, weight2_hbm,
     bias2_ref) = refs[: 9 + (first_block == 0)]
    out_ref, send_ref, wide_ref, grid_ref, moved_ref, even_rows, odd_rows, weight2_ref, sem = refs[-9:]
    step = pl.program_id(0)
    columns = grid_ref.shape[0]
    load = pltpu.make_async_copy(weight2_hbm, weight2_ref, sem)

    def first_row(t):
        block = t // 2
        if t % 2 == 0:
            here = grid_ref[:, 128 * block : 128 * block + 128]
            left = moved_ref[:, 128 * block : 128 * block + 128]
            odd = jnp.dot(here, odd1_ref[...], preferred_element_type=jnp.float32)
            weights = even1_ref
        else:
            here = grid_ref[:, 128 * block : 128 * block + 256]
            left = moved_ref[:, 128 * block : 128 * block + 256]
            odd = jnp.dot(here, odd2_ref[...], preferred_element_type=jnp.float32)
            weights = even2_ref
        even = jnp.dot(
            jnp.concatenate([here, left], axis=1), weights[...], preferred_element_type=jnp.float32
        )

        def activate(half):
            half = half + bias1_ref[...]
            return half * jnp.tanh(half) + half

        odd = activate(odd)
        even = activate(even)
        if t == 0:
            live = flag_ref[1].astype(jnp.float32)
            odd = odd * live
            even = even * live
        before = pltpu.roll(odd, 1, axis=0)
        store = even_rows if t % 2 == 0 else odd_rows
        at = pl.ds(block * columns, columns)
        store[at, 0:C1] = before.astype(jnp.bfloat16)
        store[at, C1 : 2 * C1] = even.astype(jnp.bfloat16)
        store[at, 2 * C1 :] = odd.astype(jnp.bfloat16)

    def second_rows(pair):
        total = None
        for tap, (store, at) in enumerate(
            [(even_rows, 2 * pair), (odd_rows, 2 * pair), (even_rows, 2 * pair + 1)]
        ):
            part = jnp.dot(
                store[at * columns : (at + 2) * columns, :],
                weight2_ref[tap],
                preferred_element_type=jnp.float32,
            )
            total = part if total is None else total + part
        total = (total + bias2_ref[...]).astype(jnp.bfloat16).reshape(out_ref.shape)
        out_ref[...] = total
        send_ref[...] = total

    @pl.when(step == 0)
    def _():
        load.start()
        for source in range(own_ref.shape[0]):
            own = own_ref[source].astype(jnp.float32)
            parts = [own[QUADS * k : QUADS * (k + 1)] for k in range(first_block, first_block + 4)]
            if first_block == 0:
                parts = [halo[0][source].astype(jnp.float32)[SB - QUADS :]] + parts
            else:
                parts = [own[QUADS * (first_block - 1) : QUADS * first_block]] + parts
            for k, part in enumerate(parts):
                wide_ref[QUADS * source : QUADS * (source + 1), 128 * k : 128 * (k + 1)] = part
        grid_ref[...] = wide_ref[...].astype(jnp.bfloat16)
        moved_ref[...] = pltpu.roll(wide_ref[...], 1, axis=0).astype(jnp.bfloat16)
        for t in range(5):
            first_row(t)
        load.wait()
        second_rows(0)

    @pl.when(step == 1)
    def _():
        for t in range(5, 9):
            first_row(t)
        second_rows(1)


def convolutions(part, flags, halo, own, weights1, bias1, weights2, bias2, whole):
    columns = QUADS * own.shape[0]
    full = lambda a: pl.BlockSpec(a.shape, lambda i, *_: (0,) * a.ndim)
    anywhere = pl.BlockSpec(memory_space=pl.ANY)
    operands = [own, *weights1, bias1, weights2, bias2]
    if part == 0:
        operands = [halo] + operands
    specs = [anywhere if a is weights2 else full(a) for a in operands]
    aliases = {}
    if whole is not None:
        aliases = {1 + len(operands): 0}
        operands.append(whole)
        specs.append(anywhere)
    return pl.pallas_call(
        functools.partial(conv_kernel, 4 * part),
        grid_spec=pltpu.PrefetchScalarGridSpec(
            num_scalar_prefetch=1,
            grid=(2,),
            in_specs=specs,
            out_specs=[
                pl.BlockSpec((2, columns, C2), lambda i, flags: (flags[0] * 4 + 2 * part + i, 0, 0)),
                pl.BlockSpec((2, columns, C2), lambda i, *_: (i, 0, 0)),
            ],
            scratch_shapes=[
                pltpu.VMEM((columns, 640), jnp.float32),
                pltpu.VMEM((columns, 640), jnp.bfloat16),
                pltpu.VMEM((columns, 640), jnp.bfloat16),
                pltpu.VMEM((5 * columns, 3 * C1), jnp.bfloat16),
                pltpu.VMEM((4 * columns, 3 * C1), jnp.bfloat16),
                pltpu.VMEM(weights2.shape, jnp.bfloat16),
                pltpu.SemaphoreType.DMA,
            ],
        ),
        out_shape=[
            jax.ShapeDtypeStruct((16, columns, C2), jnp.bfloat16),
            jax.ShapeDtypeStruct((4, columns, C2), jnp.bfloat16),
        ],
        input_output_aliases=aliases,
        cost_estimate=pl.CostEstimate(
            flops=9_000_000_000, transcendentals=1_800_000, bytes_accessed=12_000_000
        ),
        compiler_params=pltpu.CompilerParams(
            dimension_semantics=("arbitrary",), vmem_limit_bytes=61 << 20
        ),
    )(flags, *operands)


def first_weights(embed_weight, conv1_weight):
    channels = conv1_weight.astype(jnp.float32)
    values = jnp.einsum(
        "vc,tco->tvo",
        embed_weight.astype(jnp.float32),
        channels[:, 1:],
        precision=lax.Precision.HIGHEST,
    )
    taps = jnp.concatenate([channels[:, :1], jnp.zeros_like(channels[:, :1]), values], axis=1)
    taps = (0.5 * taps).astype(jnp.bfloat16).reshape(3, 3, FEAT, C1)

    def placed(part, above, below, phase):
        pads = ((above, below), (phase, PHASES - phase - part.shape[1]), (0, 0), (0, 0))
        return jnp.pad(part, pads).reshape(-1, C1)

    odd = [placed(taps, above, below, 1) for above, below in ((1, 0), (3, 2))]
    even = [
        jnp.concatenate(
            [placed(taps[:, 1:], above, below, 0), placed(taps[:, :1], above, below, 3)], axis=0
        )
        for above, below in ((1, 0), (3, 2))
    ]
    return odd + even


def shards(
    obs_tiles,
    tile_block,
    tile_rows,
    embed_weight,
    conv1_weight,
    conv1_bias,
    conv2_weight,
    conv2_bias,
):
    n_lon = lax.axis_size("lon")
    n_lat = lax.axis_size("lat")
    core = lax.axis_index("lon") % 2

    notes = jnp.concatenate([tile_block[0], tile_rows[0]], axis=1).astype(jnp.bfloat16)
    notes = jnp.pad(notes[:, None], ((0, 0), (0, 7), (0, 120)))
    arrived = lax.all_to_all(leaving_tiles(obs_tiles[0], notes), ("lat", "lon"), 0, 0, tiled=True)
    notes = arrived[:, 2 * CAP, 0, : 2 * CAP].astype(jnp.int32)

    own = lax.all_to_all(set_convolution(notes, arrived, n_lon), "lon", 0, 0, tiled=True)
    last = own[:, 8 * QUADS - SB :]
    south = [(z * n_lon + i, z * n_lon + i + 1) for z in range(n_lat) for i in range(0, n_lon, 2)]
    south += [(b, b + n_lon - 1) for _, b in south if b + n_lon < n_lat * n_lon]
    halo = lax.ppermute(last, ("lat", "lon"), south)

    weights1 = first_weights(embed_weight, conv1_weight)
    top = jnp.where((lax.axis_index("lat") == 0) & (core == 0), 0, 1)
    pairs = [(i, i ^ 1) for i in range(n_lon)]
    whole = None
    swapped = []
    for part in (1, 0):
        flags = jnp.stack([core, top if part == 0 else jnp.ones_like(top)]).astype(jnp.int32)
        whole, half = convolutions(
            part,
            flags,
            halo,
            own,
            weights1,
            0.5 * conv1_bias[None],
            conv2_weight.reshape(3, 3 * C1, C2),
            conv2_bias[None],
            whole,
        )
        swapped.append((part, lax.ppermute(half, "lon", pairs)))
    for part, rows in swapped:
        whole = lax.dynamic_update_slice_in_dim(whole, rows, (1 - core) * 8 + 4 * part, axis=0)
    return whole


def solution(mesh):
    placed = (
        P(("lat", "lon"), None, None, None, None),
        P(("lat", "lon"), None, None),
        P(("lat", "lon"), None, None),
        P(),
        P(),
        P(),
        P(),
        P(),
    )
    return jax.shard_map(
        shards, mesh=mesh, in_specs=placed, out_specs=P("lat", None, None), check_vma=False
    )
```

time: 133 us -> 117 us (0.88)
  starting transfers between devices: 32.2 us -> 18.9 us
  Pallas kernels: 34.1 us -> 41.4 us
  local copies, waits for them, and re-layouts: 11.4 us -> 6.92 us
  waiting for transfers between devices: 48.2 us -> 45.1 us
  other arithmetic: 6.07 us -> 4.04 us
    ppermute x17 -> x3, starting transfers between devices: 20.7 us -> 2.74 us  [the longest x1 2.07 us: shards(): halo = lax.ppermute(last, ('lat', 'lon'), south)]
    ppermute x17 -> x3, waiting for transfers between devices: 17.3 us -> 2.36 us  [the longest x2 2.36 us: shards(): swapped.append((part, lax.ppermute(half, 'lon', pairs)))]
    all_to_all x1 -> x2, waiting for transfers between devices: 30.9 us -> 42.7 us  [the longest x1 33 us: shards(): lax.all_to_all(leaving_tiles(obs_tiles[0], notes), ('lat', 'lon'), 0, 0,...]
    pallas_call x2 -> x3, Pallas kernels: 18.6 us -> 24.9 us  [the longest x2 19 us: convolutions(): pl.pallas_call(functools.partial(conv_kernel, 4 * part), grid_spec=pltpu....]
    slice x3 -> x1, local copies, waits for them, and re-layouts: 4.94 us -> 0.01 us  [shards(): last = own[:, 8 * QUADS - SB:]]
    all_to_all x1 -> x2, starting transfers between devices: 11.5 us -> 16.2 us  [the longest x1 11.5 us: shards(): lax.all_to_all(leaving_tiles(obs_tiles[0], notes), ('lat', 'lon'), 0, 0,...]
    dynamic_update_slice x2, local copies, waits for them, and re-layouts: 2.49 us -> 3.9 us  [shards(): lax.dynamic_update_slice_in_dim(whole, rows, (1 - core) * 8 + 4 * part, a...]
  transfers between devices with their start and end apart: 18 -> 5, of which waited for: 10 -> 3; matrix products, arithmetic and copies ran while one was open for 5% -> 5% of each run, Pallas kernels for 7% -> 16%
where the time goes in v3:
time: 117 us
  waiting for transfers between devices  45.1 us (39%)
  Pallas kernels  41.4 us (35%)
  starting transfers between devices  18.9 us (16%)
  local copies, waits for them, and re-layouts  6.92 us (6%)
  other arithmetic  4.04 us (3%)
    all_to_all x1, waiting for transfers between devices, shards(): lax.all_to_all(leaving_tiles(obs_tiles[0], notes), ('lat', 'lon'), 0, 0,...  33 us
    pallas_call x2, Pallas kernels, convolutions(): pl.pallas_call(functools.partial(conv_kernel, 4 * part), grid_spec=pltpu....  19 us
    pallas_call x1, Pallas kernels, set_convolution(): pl.pallas_call(setconv_kernel, grid_spec=pltpu.PrefetchScalarGridSpec(num...  16.5 us
    all_to_all x1, starting transfers between devices, shards(): lax.all_to_all(leaving_tiles(obs_tiles[0], notes), ('lat', 'lon'), 0, 0,...  11.5 us
    all_to_all x1, waiting for transfers between devices, shards(): lax.all_to_all(set_convolution(notes, arrived, n_lon), 'lon', 0, 0, tiled...  9.67 us
    pallas_call x1, Pallas kernels, leaving_tiles(): pl.pallas_call(leave_kernel, grid=(count // SOURCES,), in_specs=[pl.Block...  5.81 us
    all_to_all x1, starting transfers between devices, shards(): lax.all_to_all(set_convolution(notes, arrived, n_lon), 'lon', 0, 0, tiled...  4.67 us
    dynamic_update_slice x2, local copies, waits for them, and re-layouts, shards(): lax.dynamic_update_slice_in_dim(whole, rows, (1 - core) * 8 + 4 * part, a...  3.9 us
  transfers between devices with their start and end apart: 5, of which 3 were waited for; matrix products, arithmetic and copies ran while one was open for 5% of the time, Pallas kernels for 16%

profile of v3, /device:TPU:1, one launch (start us, length us, event | category | flops | bytes accessed | tf_op | source)
XLA Modules:
  0.0 116.6 jit_solution(13087860975642998988)
XLA Ops:
  0.0 0.7 convert_bitcast_fusion
  0.9 0.8 pad.28.notes_ref
  1.6 5.8 %shard_map.82 = bf16[128,9,8,128]{3,2,1,0:T(8,128)(2,1)} custom-call(bf16[128,4,8,256]{3,2,1,0:T(8,128)(2,1)} %bitcast.27, bf16[128,8,128]{2,1,0:T(8,128)(2,1)} %pad.28.notes_ref), custom_call_target="tpu_custom_call" | custom-call | tf_op jit(solution)/shard_map/pallas_call | solution.py:147
  7.4 11.5 %all-to-all-start = ((bf16[128,9,8,128]{3,2,1,0:T(8,128)(2,1)}), bf16[128,9,8,128]{3,2,1,0:T(8,128)(2,1)S(1)}, u32[]{:S(2)}, u32[]{:S(2)}) async-start(bf16[128,9,8,128]{3,2,1,0:T(8,128)(2,1)} %shard_map.82), calls=%async_computation | async-start | bytes 4718592 | tf_op jit(solution)/shard_map/all_to_all | solution.py:330
  19.2 33.0 %all-to-all-done.tiles_ref = bf16[128,9,8,128]{3,2,1,0:T(8,128)(2,1)S(1)} async-done(((bf16[128,9,8,128]{3,2,1,0:T(8,128)(2,1)}), bf16[128,9,8,128]{3,2,1,0:T(8,128)(2,1)S(1)}, u32[]{:S(2)}, u32[]{:S(2)}) %all-to-all-start) | async-done | bytes 2359328 | tf_op jit(solution)/shard_map/all_to_all | solution.py:330
  52.3 16.5 %shard_map.83 = bf16[32,96,128]{2,1,0:T(8,128)(2,1)} custom-call(s32[128,8]{1,0:T(8,128)S(1)} %bitcast.26, bf16[128,9,8,128]{3,2,1,0:T(8,128)(2,1)S(1)} %all-to-all-done.tiles_ref), custom_call_target="tpu_custom_call" | custom-call | tf_op jit(solution)/shard_map/pallas_call | solution.py:123
  68.9 4.7 %all-to-all-start.1 = ((bf16[32,96,128]{2,1,0:T(8,128)(2,1)}), bf16[32,96,128]{2,1,0:T(8,128)(2,1)S(1)}, u32[]{:S(2)}, u32[]{:S(2)}) async-start(bf16[32,96,128]{2,1,0:T(8,128)(2,1)} %shard_map.83), calls=%async_computation.1 | async-start | bytes 1572864 | tf_op jit(solution)/shard_map/all_to_all | solution.py:333
  73.7 0.7 pad.30
  74.4 0.6 pad.29
  75.0 0.7 pad_add_fusion.1.refs_0_
  75.7 0.6 pad_add_fusion.refs_0_
  76.2 0.7 pad_maximum_fusion.1.refs_4_.refs_5_
  76.9 0.7 pad_maximum_fusion.refs_5_.refs_6_
  77.6 0.6 broadcast_multiply_fusion
  78.2 9.7 %all-to-all-done.1.refs_1_.refs_2_ = bf16[32,96,128]{2,1,0:T(8,128)(2,1)S(1)} async-done(((bf16[32,96,128]{2,1,0:T(8,128)(2,1)}), bf16[32,96,128]{2,1,0:T(8,128)(2,1)S(1)}, u32[]{:S(2)}, u32[]{:S(2)}) %all-to-all-start.1) | async-done | bytes 786464 | tf_op jit(solution)/shard_map/all_to_all | solution.py:333
  87.9 2.1 %collective-permute-start = (bf16[32,16,128]{2,1,0:T(8,128)(2,1)S(1)}, bf16[32,16,128]{2,1,0:T(8,128)(2,1)S(1)}, u32[]{:S(2)}, u32[]{:S(2)}) collective-permute-start(bf16[32,16,128]{2,1,0:T(8,128)(2,1)S(1)} %slice.28), channel_id=1, source_target_pairs={{0,1},{2,3},{4,5},{6,7},{8,9},{10,11},{12,13},{14,15},{16,17},{18,... | collective-permute-start | bytes 393224 | tf_op jit(solution)/shard_map/ppermute | solution.py:337
  90.0 9.5 %shard_map.84 = (bf16[16,384,512]{2,1,0:T(8,128)(2,1)}, bf16[4,384,512]{2,1,0:T(8,128)(2,1)}) custom-call(s32[2]{0:T(128)} %pad_add_fusion.1.refs_0_, bf16[32,96,128]{2,1,0:T(8,128)(2,1)} %copy-done.1, bf16[128,256]{1,0:T(8,128)(2,1)} %bitcast.35, bf16[256,256]{1,0:T(8,128)(2,1)} %bitcast.33, bf16[256,256]{1,0:T(8,128)(2,1)} %pad_maximum_fusion.1.refs_4_.refs_5_, ...), custom_call_target="tpu_custom_call" | custom-call | flops 8999999488 | bytes 12000000 | tf_op jit(solution)/shard_map/pallas_call | solution.py:255
  99.5 0.4 collective-permute-start.1
  100.0 0.7 copy-done.4
  100.6 9.5 %shard_map.85 = (bf16[16,384,512]{2,1,0:T(8,128)(2,1)}, bf16[4,384,512]{2,1,0:T(8,128)(2,1)}) custom-call(s32[2]{0:T(128)} %pad_add_fusion.refs_0_, bf16[32,16,128]{2,1,0:T(8,128)(2,1)} %copy-done.4, bf16[32,96,128]{2,1,0:T(8,128)(2,1)} %copy-done.1, bf16[128,256]{1,0:T(8,128)(2,1)} %bitcast.36, ...), custom_call_target="tpu_custom_call", output_to_operand_aliasing={{0}: (10, {})} | custom-call | flops 8999999488 | bytes 12000000 | tf_op jit(solution)/shard_map/pallas_call | solution.py:255
  110.1 0.2 collective-permute-start.2
  110.4 1.2 %constant_dynamic-update-slice_fusion.1 = bf16[16,384,512]{2,1,0:T(8,128)(2,1)} fusion(bf16[16,384,512]{2,1,0:T(8,128)(2,1)} %get-tuple-element.10, bf16[4,384,512]{2,1,0:T(8,128)(2,1)S(1)} %collective-permute-done.1, s32[]{:T(128)S(6)} %select_n.19), kind=kLoop, calls=%fused_computation.15 | loop fusion | bytes 3145732 | tf_op jit(solution)/shard_map/dynamic_update_slice | solution.py:359
  111.6 2.4 %collective-permute-done.2 = bf16[4,384,512]{2,1,0:T(8,128)(2,1)} collective-permute-done((bf16[4,384,512]{2,1,0:T(8,128)(2,1)}, bf16[4,384,512]{2,1,0:T(8,128)(2,1)}, u32[]{:S(2)}, u32[]{:S(2)}) %collective-permute-start.2) | collective-permute-done | bytes 1572896 | tf_op jit(solution)/shard_map/ppermute | solution.py:357
  114.0 2.7 %constant_dynamic-update-slice_fusion = bf16[16,384,512]{2,1,0:T(8,128)(2,1)} fusion(bf16[16,384,512]{2,1,0:T(8,128)(2,1)} %constant_dynamic-update-slice_fusion.1, bf16[4,384,512]{2,1,0:T(8,128)(2,1)} %collective-permute-done.2, s32[]{:T(128)S(6)} %select_n.20), kind=kLoop, calls=%fused_computation.14 | loop fusion | bytes 3145732 | tf_op jit(solution)/shard_map/dynamic_update_slice | solution.py:359
  (26 shorter events, 0.6 us)
Async XLA Ops:
  0.0 19.1 %copy-start = (bf16[6,23]{1,0:T(8,128)(2,1)S(1)}, bf16[6,23]{1,0:T(8,128)(2,1)}, u32[]{:S(2)}) copy-start(bf16[6,23]{1,0:T(8,128)(2,1)} %param.11) | copy-start | bytes 832
  7.4 11.5 %copy-start.2 = (bf16[9,24,256]{2,1,0:T(8,128)(2,1)S(1)}, bf16[9,24,256]{2,1,0:T(8,128)(2,1)}, u32[]{:S(2)}) copy-start(bf16[9,24,256]{2,1,0:T(8,128)(2,1)} %param.12) | copy-start | bytes 331780
  7.4 44.8 %all-to-all-start = ((bf16[128,9,8,128]{3,2,1,0:T(8,128)(2,1)}), bf16[128,9,8,128]{3,2,1,0:T(8,128)(2,1)S(1)}, u32[]{:S(2)}, u32[]{:S(2)}) async-start(bf16[128,9,8,128]{3,2,1,0:T(8,128)(2,1)} %shard_map.82), calls=%async_computation | async-start | bytes 4718592 | tf_op jit(solution)/shard_map/all_to_all | solution.py:330
  68.9 8.8 %copy-start.3 = (f32[256]{0:T(256)S(1)}, f32[256]{0:T(256)}, u32[]{:S(2)}) copy-start(f32[256]{0:T(256)} %param.13) | copy-start | bytes 3076
  68.9 19.0 %all-to-all-start.1 = ((bf16[32,96,128]{2,1,0:T(8,128)(2,1)}), bf16[32,96,128]{2,1,0:T(8,128)(2,1)S(1)}, u32[]{:S(2)}, u32[]{:S(2)}) async-start(bf16[32,96,128]{2,1,0:T(8,128)(2,1)} %shard_map.83), calls=%async_computation.1 | async-start | bytes 1572864 | tf_op jit(solution)/shard_map/all_to_all | solution.py:333
  87.9 2.1 %copy-start.1 = (bf16[32,96,128]{2,1,0:T(8,128)(2,1)}, bf16[32,96,128]{2,1,0:T(8,128)(2,1)S(1)}, u32[]{:S(2)}) copy-start(bf16[32,96,128]{2,1,0:T(8,128)(2,1)S(1)} %all-to-all-done.1.refs_1_.refs_2_) | copy-start | bytes 2359300
  87.9 12.1 %collective-permute-start = (bf16[32,16,128]{2,1,0:T(8,128)(2,1)S(1)}, bf16[32,16,128]{2,1,0:T(8,128)(2,1)S(1)}, u32[]{:S(2)}, u32[]{:S(2)}) collective-permute-start(bf16[32,16,128]{2,1,0:T(8,128)(2,1)S(1)} %slice.28), channel_id=1, source_target_pairs={{0,1},{2,3},{4,5},{6,7},{8,9},{10,11},{12,13},{14,15},{16,17},{18,... | collective-permute-start | bytes 393224 | tf_op jit(solution)/shard_map/ppermute | solution.py:337
  99.5 10.9 %collective-permute-start.1 = (bf16[4,384,512]{2,1,0:T(8,128)(2,1)}, bf16[4,384,512]{2,1,0:T(8,128)(2,1)S(1)}, u32[]{:S(2)}, u32[]{:S(2)}) collective-permute-start(bf16[4,384,512]{2,1,0:T(8,128)(2,1)} %get-tuple-element.11), channel_id=1, source_target_pairs={{0,1},{1,0},{2,3},{3,2},{4,5},{5,4},{6,7},{7,6},{8,9},{9,8},{10,11... | collective-permute-start | bytes 4718600 | tf_op jit(solution)/shard_map/ppermute | solution.py:357
  100.0 0.7 copy-start.4
  110.1 3.8 %collective-permute-start.2 = (bf16[4,384,512]{2,1,0:T(8,128)(2,1)}, bf16[4,384,512]{2,1,0:T(8,128)(2,1)}, u32[]{:S(2)}, u32[]{:S(2)}) collective-permute-start(bf16[4,384,512]{2,1,0:T(8,128)(2,1)} %get-tuple-element.12), channel_id=1, source_target_pairs={{0,1},{1,0},{2,3},{3,2},{4,5},{5,4},{6,7},{7,6},{8,9},{9,8},{10,11... | collective-permute-start | bytes 4718600 | tf_op jit(solution)/shard_map/ppermute | solution.py:357

commit v4 on v3

--- a/solution.py
+++ b/solution.py
@@ -13,6 +13,7 @@
 TILE = 256
 CAP = 4
 FEAT = 8
+KEPT = 7
 C1 = 256
 C2 = 512
 SUBS = 12
@@ -50,7 +51,7 @@
         off_col = center_col - place[1:2] * ROOT_HALF_LOG2E
         along_row = jnp.exp2(-(off_row * off_row)).astype(jnp.bfloat16)
         along_col = jnp.exp2(-(off_col * off_col)).astype(jnp.bfloat16)
-        weighted = [along_row, jnp.zeros_like(along_row)]
+        weighted = [along_row]
         weighted += [tile[k : k + 1] * along_row for k in range(2, FEAT)]
         part = lax.dot_general(
             along_col,
@@ -61,20 +62,17 @@
         sub = note_ref[step * SOURCES + source, slot]
         total[sub] = total[sub] + part
 
-    def add_sources(m, carry):
-        for k in range(4):
-            for slot in range(CAP):
-                add_tile(4 * m + k, slot, sums[slot])
-        return carry
-
-    lax.fori_loop(0, SOURCES // 4, add_sources, 0)
+    for k in range(SOURCES):
+        for slot in range(CAP):
+            add_tile(k, slot, sums[slot])
 
     @pl.when(step == pl.num_programs(0) - 1)
     def _():
         total = sums[0][...]
         for more in sums[1:]:
             total = total + more[...]
-        total = total.reshape(SUBS * SB, FEAT * SB)
+        total = total.reshape(SUBS * SB, KEPT * SB)
+        total = jnp.concatenate([total, jnp.zeros((SUBS * SB, SB), jnp.float32)], axis=1)
         pick = (iota((128, 128), 0) == iota((128, 128), 1) % SB).astype(jnp.float32)
         density = jnp.dot(
             total, pick, precision=lax.Precision.HIGHEST, preferred_element_type=jnp.float32
@@ -127,7 +125,7 @@
             grid=(arrived.shape[0] // SOURCES,),
             in_specs=[pl.BlockSpec((SOURCES,) + arrived.shape[1:], lambda i, *_: (i, 0, 0, 0))],
             out_specs=pl.BlockSpec(out.shape, lambda i, *_: (0, 0, 0)),
-            scratch_shapes=[pltpu.VMEM((SUBS, SB, FEAT * SB), jnp.float32)] * CAP,
+            scratch_shapes=[pltpu.VMEM((SUBS, SB, KEPT * SB), jnp.float32)] * CAP,
         ),
         out_shape=out,
         compiler_params=pltpu.CompilerParams(
@@ -136,25 +134,39 @@
     )(notes, arrived)
 
 
-def leave_kernel(tiles_ref, notes_ref, out_ref):
+def leave_kernel(sub_ref, rows_ref, tiles_ref, out_ref, notes_ref):
+    step = pl.program_id(0)
+    count = tiles_ref.shape[0]
+
+    @pl.when(step == 0)
+    def _():
+        both = jnp.concatenate([sub_ref[...], rows_ref[...]], axis=0).astype(jnp.float32)
+        blank = jnp.zeros((128 - 2 * CAP, both.shape[1]), jnp.float32)
+        notes_ref[...] = jnp.concatenate([both, blank], axis=0).T
+
+    notes = notes_ref[pl.ds(step * count, count), :]
+    notes = jnp.broadcast_to(notes[:, None, :], (count, FEAT, 128)).astype(jnp.bfloat16)
     out_ref[:, :CAP] = tiles_ref[:, :, :, :128]
     out_ref[:, CAP : 2 * CAP] = tiles_ref[:, :, :, 128:]
-    out_ref[:, 2 * CAP] = notes_ref[...]
-
-
-def leaving_tiles(tiles, notes):
+    out_ref[:, 2 * CAP] = notes
+
+
+def leaving_tiles(tiles, subs, rows):
     count = tiles.shape[0]
+    part = count // 2
     return pl.pallas_call(
         leave_kernel,
-        grid=(count // SOURCES,),
+        grid=(2,),
         in_specs=[
-            pl.BlockSpec((SOURCES,) + tiles.shape[1:], lambda i: (i, 0, 0, 0)),
-            pl.BlockSpec((SOURCES,) + notes.shape[1:], lambda i: (i, 0, 0)),
+            pl.BlockSpec(subs.shape, lambda i: (0, 0)),
+            pl.BlockSpec(rows.shape, lambda i: (0, 0)),
+            pl.BlockSpec((part,) + tiles.shape[1:], lambda i: (i, 0, 0, 0)),
         ],
-        out_specs=pl.BlockSpec((SOURCES, 2 * CAP + 1, FEAT, 128), lambda i: (i, 0, 0, 0)),
+        out_specs=pl.BlockSpec((part, 2 * CAP + 1, FEAT, 128), lambda i: (i, 0, 0, 0)),
         out_shape=jax.ShapeDtypeStruct((count, 2 * CAP + 1, FEAT, 128), jnp.bfloat16),
+        scratch_shapes=[pltpu.VMEM((count, 128), jnp.float32)],
         compiler_params=pltpu.CompilerParams(vmem_limit_bytes=60 << 20),
-    )(tiles, notes)
+    )(subs, rows, tiles)
 
 
 def conv_kernel(first_block, *refs):
@@ -163,7 +175,13 @@
     out_ref, send_ref, wide_ref, grid_ref, moved_ref, even_rows, odd_rows, weight2_ref, sem = refs[-9:]
     step = pl.program_id(0)
     columns = grid_ref.shape[0]
-    load = pltpu.make_async_copy(weight2_hbm, weight2_ref, sem)
+    loads = [
+        pltpu.make_async_copy(
+            weight2_hbm.at[tap, pl.ds(C1 * k, C1)], weight2_ref.at[tap, pl.ds(C1 * k, C1)], sem.at[tap, k]
+        )
+        for tap in range(3)
+        for k in range(3)
+    ]
 
     def first_row(t):
         block = t // 2
@@ -198,13 +216,13 @@
         store[at, C1 : 2 * C1] = even.astype(jnp.bfloat16)
         store[at, 2 * C1 :] = odd.astype(jnp.bfloat16)
 
-    def second_rows(pair):
+    def second_row(row):
         total = None
         for tap, (store, at) in enumerate(
-            [(even_rows, 2 * pair), (odd_rows, 2 * pair), (even_rows, 2 * pair + 1)]
+            [(even_rows, row), (odd_rows, row), (even_rows, row + 1)]
         ):
             part = jnp.dot(
-                store[at * columns : (at + 2) * columns, :],
+                store[at * columns : (at + 1) * columns, :],
                 weight2_ref[tap],
                 preferred_element_type=jnp.float32,
             )
@@ -215,7 +233,8 @@
 
     @pl.when(step == 0)
     def _():
-        load.start()
+        for load in loads:
+            load.start()
         for source in range(own_ref.shape[0]):
             own = own_ref[source].astype(jnp.float32)
             parts = [own[QUADS * k : QUADS * (k + 1)] for k in range(first_block, first_block + 4)]
@@ -227,16 +246,19 @@
                 wide_ref[QUADS * source : QUADS * (source + 1), 128 * k : 128 * (k + 1)] = part
         grid_ref[...] = wide_ref[...].astype(jnp.bfloat16)
         moved_ref[...] = pltpu.roll(wide_ref[...], 1, axis=0).astype(jnp.bfloat16)
-        for t in range(5):
+        for t in range(3):
             first_row(t)
-        load.wait()
-        second_rows(0)
-
-    @pl.when(step == 1)
-    def _():
-        for t in range(5, 9):
-            first_row(t)
-        second_rows(1)
+        for load in loads:
+            load.wait()
+        second_row(0)
+
+    for row in range(1, 4):
+
+        @pl.when(step == row)
+        def _(row=row):
+            first_row(2 * row + 1)
+            first_row(2 * row + 2)
+            second_row(row)
 
 
 def convolutions(part, flags, halo, own, weights1, bias1, weights2, bias2, whole):
@@ -256,11 +278,11 @@
         functools.partial(conv_kernel, 4 * part),
         grid_spec=pltpu.PrefetchScalarGridSpec(
             num_scalar_prefetch=1,
-            grid=(2,),
+            grid=(4,),
             in_specs=specs,
             out_specs=[
-                pl.BlockSpec((2, columns, C2), lambda i, flags: (flags[0] * 4 + 2 * part + i, 0, 0)),
-                pl.BlockSpec((2, columns, C2), lambda i, *_: (i, 0, 0)),
+                pl.BlockSpec((1, columns, C2), lambda i, flags: (flags[0] * 8 + 4 * part + i, 0, 0)),
+                pl.BlockSpec((1, columns, C2), lambda i, *_: (i, 0, 0)),
             ],
             scratch_shapes=[
                 pltpu.VMEM((columns, 640), jnp.float32),
@@ -269,7 +291,7 @@
                 pltpu.VMEM((5 * columns, 3 * C1), jnp.bfloat16),
                 pltpu.VMEM((4 * columns, 3 * C1), jnp.bfloat16),
                 pltpu.VMEM(weights2.shape, jnp.bfloat16),
-                pltpu.SemaphoreType.DMA,
+                pltpu.SemaphoreType.DMA((3, 3)),
             ],
         ),
         out_shape=[
@@ -281,7 +303,7 @@
             flops=9_000_000_000, transcendentals=1_800_000, bytes_accessed=12_000_000
         ),
         compiler_params=pltpu.CompilerParams(
-            dimension_semantics=("arbitrary",), vmem_limit_bytes=61 << 20
+            dimension_semantics=("arbitrary",), vmem_limit_bytes=40 << 20
         ),
     )(flags, *operands)
 
@@ -294,7 +316,7 @@
         channels[:, 1:],
         precision=lax.Precision.HIGHEST,
     )
-    taps = jnp.concatenate([channels[:, :1], jnp.zeros_like(channels[:, :1]), values], axis=1)
+    taps = jnp.concatenate([channels[:, :1], values, jnp.zeros_like(channels[:, :1])], axis=1)
     taps = (0.5 * taps).astype(jnp.bfloat16).reshape(3, 3, FEAT, C1)
 
     def placed(part, above, below, phase):
@@ -325,9 +347,8 @@
     n_lat = lax.axis_size("lat")
     core = lax.axis_index("lon") % 2
 
-    notes = jnp.concatenate([tile_block[0], tile_rows[0]], axis=1).astype(jnp.bfloat16)
-    notes = jnp.pad(notes[:, None], ((0, 0), (0, 7), (0, 120)))
-    arrived = lax.all_to_all(leaving_tiles(obs_tiles[0], notes), ("lat", "lon"), 0, 0, tiled=True)
+    leaving = leaving_tiles(obs_tiles[0], tile_block[0].T, tile_rows[0].T)
+    arrived = lax.all_to_all(leaving, ("lat", "lon"), 0, 0, tiled=True)
     notes = arrived[:, 2 * CAP, 0, : 2 * CAP].astype(jnp.int32)
 
     own = lax.all_to_all(set_convolution(notes, arrived, n_lon), "lon", 0, 0, tiled=True)

time: 117 us -> 106 us (0.906)
  Pallas kernels: 41.4 us -> 30.8 us
  other arithmetic: 4.04 us -> 0.33 us
  waiting for transfers between devices: 45.1 us -> 47.9 us
    pallas_call x1, Pallas kernels: 16.5 us -> 12.2 us  [set_convolution(): pl.pallas_call(setconv_kernel, grid_spec=pltpu.PrefetchScalarGridSpec(num...]
    all_to_all x1, waiting for transfers between devices: 9.67 us -> 13.9 us  [shards(): lax.all_to_all(set_convolution(notes, arrived, n_lon), 'lon', 0, 0, tiled...]
    pallas_call x2, Pallas kernels: 19 us -> 15.7 us  [convolutions(): pl.pallas_call(functools.partial(conv_kernel, 4 * part), grid_spec=pltpu....]
    pallas_call x1, Pallas kernels: 5.81 us -> 2.96 us  [leaving_tiles(): pl.pallas_call(leave_kernel, grid=(2,), in_specs=[pl.BlockSpec(subs.shape...]
    ppermute x2, waiting for transfers between devices: 2.36 us -> 0.95 us  [shards(): swapped.append((part, lax.ppermute(half, 'lon', pairs)))]
    dynamic_update_slice x2, local copies, waits for them, and re-layouts: 3.9 us -> 5.3 us  [shards(): lax.dynamic_update_slice_in_dim(whole, rows, (1 - core) * 8 + 4 * part, a...]
    concatenate x2, other arithmetic: 1.38 us -> 0.03 us  [first_weights(): jnp.concatenate([placed(taps[:, 1:], above, below, 0), placed(taps[:, :1]...]
    pad x6, local copies, waits for them, and re-layouts: 1.34 us -> 0.06 us  [placed(): return jnp.pad(part, pads).reshape(-1, C1)]
  transfers between devices with their start and end apart: 5 -> 5, of which waited for: 3 -> 3; matrix products, arithmetic and copies ran while one was open for 5% -> 3% of each run, Pallas kernels for 16% -> 15%
where the time goes in v4:
time: 106 us
  waiting for transfers between devices  47.9 us (45%)
  Pallas kernels  30.8 us (29%)
  starting transfers between devices  19.1 us (18%)
  local copies, waits for them, and re-layouts  7.14 us (7%)
    all_to_all x1, waiting for transfers between devices, shards(): arrived = lax.all_to_all(leaving, ('lat', 'lon'), 0, 0, tiled=True)  33 us
    pallas_call x2, Pallas kernels, convolutions(): pl.pallas_call(functools.partial(conv_kernel, 4 * part), grid_spec=pltpu....  15.7 us
    all_to_all x1, waiting for transfers between devices, shards(): lax.all_to_all(set_convolution(notes, arrived, n_lon), 'lon', 0, 0, tiled...  13.9 us
    pallas_call x1, Pallas kernels, set_convolution(): pl.pallas_call(setconv_kernel, grid_spec=pltpu.PrefetchScalarGridSpec(num...  12.2 us
    all_to_all x1, starting transfers between devices, shards(): arrived = lax.all_to_all(leaving, ('lat', 'lon'), 0, 0, tiled=True)  11.5 us
    dynamic_update_slice x2, local copies, waits for them, and re-layouts, shards(): lax.dynamic_update_slice_in_dim(whole, rows, (1 - core) * 8 + 4 * part, a...  5.3 us
    all_to_all x1, starting transfers between devices, shards(): lax.all_to_all(set_convolution(notes, arrived, n_lon), 'lon', 0, 0, tiled...  4.67 us
    pallas_call x1, Pallas kernels, leaving_tiles(): pl.pallas_call(leave_kernel, grid=(2,), in_specs=[pl.BlockSpec(subs.shape...  2.96 us
  transfers between devices with their start and end apart: 5, of which 3 were waited for; matrix products, arithmetic and copies ran while one was open for 3% of the time, Pallas kernels for 15%

profile of v4, /device:TPU:1, one launch (start us, length us, event | category | flops | bytes accessed | tf_op | source)
XLA Modules:
  0.0 105.5 jit_solution(17059739049662824167)
XLA Ops:
  0.0 3.0 %shard_map.82 = bf16[128,9,8,128]{3,2,1,0:T(8,128)(2,1)} custom-call(s32[4,128]{1,0:T(4,128)} %bitcast.46, s32[4,128]{1,0:T(4,128)} %bitcast.47, bf16[128,4,8,256]{3,2,1,0:T(8,128)(2,1)} %bitcast.39), custom_call_target="tpu_custom_call" | custom-call | tf_op jit(solution)/shard_map/pallas_call | solution.py:157
  3.0 11.5 %all-to-all-start = ((bf16[128,9,8,128]{3,2,1,0:T(8,128)(2,1)}), bf16[128,9,8,128]{3,2,1,0:T(8,128)(2,1)S(1)}, u32[]{:S(2)}, u32[]{:S(2)}) async-start(bf16[128,9,8,128]{3,2,1,0:T(8,128)(2,1)} %shard_map.82), calls=%async_computation | async-start | bytes 4718592 | tf_op jit(solution)/shard_map/all_to_all | solution.py:351
  14.5 0.1 pad.38.clone
  14.6 0.1 fusion
  14.7 33.0 %all-to-all-done.tiles_ref = bf16[128,9,8,128]{3,2,1,0:T(8,128)(2,1)S(1)} async-done(((bf16[128,9,8,128]{3,2,1,0:T(8,128)(2,1)}), bf16[128,9,8,128]{3,2,1,0:T(8,128)(2,1)S(1)}, u32[]{:S(2)}, u32[]{:S(2)}) %all-to-all-start) | async-done | bytes 2359328 | tf_op jit(solution)/shard_map/all_to_all | solution.py:351
  47.8 0.1 slice_convert_fusion
  47.8 12.2 %shard_map.83 = bf16[32,96,128]{2,1,0:T(8,128)(2,1)} custom-call(s32[128,8]{1,0:T(8,128)S(1)} %bitcast.28, bf16[128,9,8,128]{3,2,1,0:T(8,128)(2,1)S(1)} %all-to-all-done.tiles_ref), custom_call_target="tpu_custom_call" | custom-call | tf_op jit(solution)/shard_map/pallas_call | solution.py:121
  60.0 4.7 %all-to-all-start.1 = ((bf16[32,96,128]{2,1,0:T(8,128)(2,1)}), bf16[32,96,128]{2,1,0:T(8,128)(2,1)S(1)}, u32[]{:S(2)}, u32[]{:S(2)}) async-start(bf16[32,96,128]{2,1,0:T(8,128)(2,1)} %shard_map.83), calls=%async_computation.1 | async-start | bytes 1572864 | tf_op jit(solution)/shard_map/all_to_all | solution.py:354
  64.7 0.1 fusion.2
  64.9 0.1 pad_add_fusion.1.refs_0_
  65.0 0.1 pad_add_fusion.refs_0_
  65.1 13.9 %all-to-all-done.1.refs_1_.refs_2_ = bf16[32,96,128]{2,1,0:T(8,128)(2,1)S(1)} async-done(((bf16[32,96,128]{2,1,0:T(8,128)(2,1)}), bf16[32,96,128]{2,1,0:T(8,128)(2,1)S(1)}, u32[]{:S(2)}, u32[]{:S(2)}) %all-to-all-start.1) | async-done | bytes 786464 | tf_op jit(solution)/shard_map/all_to_all | solution.py:354
  79.0 2.1 %collective-permute-start = (bf16[32,16,128]{2,1,0:T(8,128)(2,1)S(1)}, bf16[32,16,128]{2,1,0:T(8,128)(2,1)S(1)}, u32[]{:S(2)}, u32[]{:S(2)}) collective-permute-start(bf16[32,16,128]{2,1,0:T(8,128)(2,1)S(1)} %slice.28), channel_id=1, source_target_pairs={{0,1},{2,3},{4,5},{6,7},{8,9},{10,11},{12,13},{14,15},{16,17},{18,... | collective-permute-start | bytes 393224 | tf_op jit(solution)/shard_map/ppermute | solution.py:358
  81.1 0.0 copy-start.1
  81.1 1.7 %copy-done.1 = bf16[9,256,512]{2,1,0:T(8,128)(2,1)S(1)} copy-done((bf16[9,256,512]{2,1,0:T(8,128)(2,1)S(1)}, bf16[9,256,512]{2,1,0:T(8,128)(2,1)}, u32[]{:S(2)}) %copy-start.1) | copy-done | bytes 2359320
  82.8 7.7 %shard_map.84 = (bf16[16,384,512]{2,1,0:T(8,128)(2,1)}, bf16[4,384,512]{2,1,0:T(8,128)(2,1)S(1)}) custom-call(s32[2]{0:T(128)S(1)} %pad_add_fusion.1.refs_0_, bf16[32,96,128]{2,1,0:T(8,128)(2,1)S(1)} %all-to-all-done.1.refs_1_.refs_2_, bf16[128,256]{1,0:T(8,128)(2,1)S(1)} %bitcast.31, bf16[256,256]{1,0:T(8,128)(2,1)S(1)} %bitcast.29, ...), custom_call_target="tpu_custom_call" | custom-call | flops 8999999488 | bytes 12000000 | tf_op jit(solution)/shard_map/pallas_call | solution.py:277
  90.5 0.6 collective-permute-start.1
  91.1 0.0 collective-permute-done.refs_1_
  91.1 7.9 %shard_map.85 = (bf16[16,384,512]{2,1,0:T(8,128)(2,1)}, bf16[4,384,512]{2,1,0:T(8,128)(2,1)}) custom-call(s32[2]{0:T(128)S(1)} %pad_add_fusion.refs_0_, bf16[32,16,128]{2,1,0:T(8,128)(2,1)S(1)} %collective-permute-done.refs_1_, bf16[32,96,128]{2,1,0:T(8,128)(2,1)S(1)} %all-to-all-done.1.refs_1_.refs_2_, ...), custom_call_target="tpu_custom_call", output_to_operand_aliasing={{0}: (10, {})} | custom-call | flops 8999999488 | bytes 12000000 | tf_op jit(solution)/shard_map/pallas_call | solution.py:277
  99.1 0.2 collective-permute-start.2
  99.3 0.0 collective-permute-done.1
  99.3 2.7 %constant_dynamic-update-slice_fusion.1 = bf16[16,384,512]{2,1,0:T(8,128)(2,1)} fusion(bf16[16,384,512]{2,1,0:T(8,128)(2,1)} %get-tuple-element.10, bf16[4,384,512]{2,1,0:T(8,128)(2,1)} %collective-permute-done.1, s32[]{:T(128)S(6)} %select_n.19), kind=kLoop, calls=%fused_computation.12 | loop fusion | bytes 3145732 | tf_op jit(solution)/shard_map/dynamic_update_slice | solution.py:380
  102.0 0.9 collective-permute-done.2
  102.9 2.7 %constant_dynamic-update-slice_fusion = bf16[16,384,512]{2,1,0:T(8,128)(2,1)} fusion(bf16[16,384,512]{2,1,0:T(8,128)(2,1)} %constant_dynamic-update-slice_fusion.1, bf16[4,384,512]{2,1,0:T(8,128)(2,1)} %collective-permute-done.2, s32[]{:T(128)S(6)} %select_n.20), kind=kLoop, calls=%fused_computation.11 | loop fusion | bytes 3145732 | tf_op jit(solution)/shard_map/dynamic_update_slice | solution.py:380
  (22 shorter events, 0.1 us)
Async XLA Ops:
  0.0 14.6 %copy-start = (bf16[6,23]{1,0:T(8,128)(2,1)S(1)}, bf16[6,23]{1,0:T(8,128)(2,1)}, u32[]{:S(2)}) copy-start(bf16[6,23]{1,0:T(8,128)(2,1)} %param.11) | copy-start | bytes 832
  3.0 11.5 %copy-start.3 = (bf16[9,24,256]{2,1,0:T(8,128)(2,1)S(1)}, bf16[9,24,256]{2,1,0:T(8,128)(2,1)}, u32[]{:S(2)}) copy-start(bf16[9,24,256]{2,1,0:T(8,128)(2,1)} %param.12) | copy-start | bytes 331780
  3.0 44.8 %all-to-all-start = ((bf16[128,9,8,128]{3,2,1,0:T(8,128)(2,1)}), bf16[128,9,8,128]{3,2,1,0:T(8,128)(2,1)S(1)}, u32[]{:S(2)}, u32[]{:S(2)}) async-start(bf16[128,9,8,128]{3,2,1,0:T(8,128)(2,1)} %shard_map.82), calls=%async_computation | async-start | bytes 4718592 | tf_op jit(solution)/shard_map/all_to_all | solution.py:351
  60.0 5.1 %copy-start.4 = (f32[256]{0:T(256)S(1)}, f32[256]{0:T(256)}, u32[]{:S(2)}) copy-start(f32[256]{0:T(256)} %param.13) | copy-start | bytes 3076
  60.0 21.1 %copy-start.2 = (f32[512]{0:T(512)S(1)}, f32[512]{0:T(512)}, u32[]{:S(2)}) copy-start(f32[512]{0:T(512)} %param.15) | copy-start | bytes 6148
  60.0 19.0 %all-to-all-start.1 = ((bf16[32,96,128]{2,1,0:T(8,128)(2,1)}), bf16[32,96,128]{2,1,0:T(8,128)(2,1)S(1)}, u32[]{:S(2)}, u32[]{:S(2)}) async-start(bf16[32,96,128]{2,1,0:T(8,128)(2,1)} %shard_map.83), calls=%async_computation.1 | async-start | bytes 1572864 | tf_op jit(solution)/shard_map/all_to_all | solution.py:354
  79.0 12.1 %collective-permute-start = (bf16[32,16,128]{2,1,0:T(8,128)(2,1)S(1)}, bf16[32,16,128]{2,1,0:T(8,128)(2,1)S(1)}, u32[]{:S(2)}, u32[]{:S(2)}) collective-permute-start(bf16[32,16,128]{2,1,0:T(8,128)(2,1)S(1)} %slice.28), channel_id=1, source_target_pairs={{0,1},{2,3},{4,5},{6,7},{8,9},{10,11},{12,13},{14,15},{16,17},{18,... | collective-permute-start | bytes 393224 | tf_op jit(solution)/shard_map/ppermute | solution.py:358
  81.1 1.7 %copy-start.1 = (bf16[9,256,512]{2,1,0:T(8,128)(2,1)S(1)}, bf16[9,256,512]{2,1,0:T(8,128)(2,1)}, u32[]{:S(2)}) copy-start(bf16[9,256,512]{2,1,0:T(8,128)(2,1)} %param.14) | copy-start | bytes 7077892
  90.5 8.8 %collective-permute-start.1 = (bf16[4,384,512]{2,1,0:T(8,128)(2,1)S(1)}, bf16[4,384,512]{2,1,0:T(8,128)(2,1)}, u32[]{:S(2)}, u32[]{:S(2)}) collective-permute-start(bf16[4,384,512]{2,1,0:T(8,128)(2,1)S(1)} %get-tuple-element.11), channel_id=1, source_target_pairs={{0,1},{1,0},{2,3},{3,2},{4,5},{5,4},{6,7},{7,6},{8,9},{9,8},{10,11... | collective-permute-start | bytes 4718600 | tf_op jit(solution)/shard_map/ppermute | solution.py:378
  99.1 3.8 %collective-permute-start.2 = (bf16[4,384,512]{2,1,0:T(8,128)(2,1)}, bf16[4,384,512]{2,1,0:T(8,128)(2,1)}, u32[]{:S(2)}, u32[]{:S(2)}) collective-permute-start(bf16[4,384,512]{2,1,0:T(8,128)(2,1)} %get-tuple-element.12), channel_id=1, source_target_pairs={{0,1},{1,0},{2,3},{3,2},{4,5},{5,4},{6,7},{7,6},{8,9},{9,8},{10,11... | collective-permute-start | bytes 4718600 | tf_op jit(solution)/shard_map/ppermute | solution.py:378

commit v5 on v4

--- a/solution.py
+++ b/solution.py
@@ -22,7 +22,7 @@
 ROW_LANES = PHASES * FEAT
 FAR = 8192.0
 ROOT_HALF_LOG2E = (0.5 * 1.4426950408889634) ** 0.5
-SOURCES = 16
+SOURCES = 32
 
 
 def iota(shape, axis):
@@ -212,9 +212,9 @@
         before = pltpu.roll(odd, 1, axis=0)
         store = even_rows if t % 2 == 0 else odd_rows
         at = pl.ds(block * columns, columns)
-        store[at, 0:C1] = before.astype(jnp.bfloat16)
+        store[at, 0:C1] = odd.astype(jnp.bfloat16)
         store[at, C1 : 2 * C1] = even.astype(jnp.bfloat16)
-        store[at, 2 * C1 :] = odd.astype(jnp.bfloat16)
+        store[at, 2 * C1 :] = before.astype(jnp.bfloat16)
 
     def second_row(row):
         total = None
@@ -303,7 +303,7 @@
             flops=9_000_000_000, transcendentals=1_800_000, bytes_accessed=12_000_000
         ),
         compiler_params=pltpu.CompilerParams(
-            dimension_semantics=("arbitrary",), vmem_limit_bytes=40 << 20
+            dimension_semantics=("arbitrary",), vmem_limit_bytes=(40 if part else 40) << 20
         ),
     )(flags, *operands)
 
@@ -358,6 +358,7 @@
     halo = lax.ppermute(last, ("lat", "lon"), south)
 
     weights1 = first_weights(embed_weight, conv1_weight)
+    weights2 = conv2_weight.reshape(3, 3, C1, C2)[:, ::-1].reshape(3, 3 * C1, C2)
     top = jnp.where((lax.axis_index("lat") == 0) & (core == 0), 0, 1)
     pairs = [(i, i ^ 1) for i in range(n_lon)]
     whole = None
@@ -371,7 +372,7 @@
             own,
             weights1,
             0.5 * conv1_bias[None],
-            conv2_weight.reshape(3, 3 * C1, C2),
+            weights2,
             conv2_bias[None],
             whole,
         )

time: 106 us -> 105 us (level)
  waiting for transfers between devices: 47.9 us -> 41.1 us
  local copies, waits for them, and re-layouts: 7.14 us -> 10.2 us
  other arithmetic: 0.33 us -> 3.14 us
    all_to_all x1, waiting for transfers between devices: 13.9 us -> 7.31 us  [shards(): lax.all_to_all(set_convolution(notes, arrived, n_lon), 'lon', 0, 0, tiled...]
    pad x6, local copies, waits for them, and re-layouts: 0.06 us -> 1.98 us  [placed(): return jnp.pad(part, pads).reshape(-1, C1)]
    rev x0 -> x1, local copies, waits for them, and re-layouts: none -> 1.91 us  [shards(): conv2_weight.reshape(3, 3, C1, C2)[:, ::-1].reshape(3, 3 * C1, C2)]
    concatenate x2, other arithmetic: 0.03 us -> 1.64 us  [first_weights(): jnp.concatenate([placed(taps[:, 1:], above, below, 0), placed(taps[:, :1]...]
    dynamic_update_slice x2, local copies, waits for them, and re-layouts: 5.3 us -> 3.9 us  [shards(): lax.dynamic_update_slice_in_dim(whole, rows, (1 - core) * 8 + 4 * part, a...]
    unnamed x10 -> x12, local copies, waits for them, and re-layouts: 1.68 us -> 2.36 us
  transfers between devices with their start and end apart: 5 -> 5, of which waited for: 3 -> 3; matrix products, arithmetic and copies ran while one was open for 3% -> 9% of each run, Pallas kernels for 15% -> 15%
where the time goes in v5:
time: 105 us; the launch traced here: 104 us
  waiting for transfers between devices  41.1 us (39%)
  Pallas kernels  30.4 us (29%)
  starting transfers between devices  19 us (18%)
  local copies, waits for them, and re-layouts  10.2 us (10%)
  other arithmetic  3.14 us (3%)
    all_to_all x1, waiting for transfers between devices, shards(): arrived = lax.all_to_all(leaving, ('lat', 'lon'), 0, 0, tiled=True)  33 us
    pallas_call x2, Pallas kernels, convolutions(): pl.pallas_call(functools.partial(conv_kernel, 4 * part), grid_spec=pltpu....  15.8 us
    pallas_call x1, Pallas kernels, set_convolution(): pl.pallas_call(setconv_kernel, grid_spec=pltpu.PrefetchScalarGridSpec(num...  11.6 us
    all_to_all x1, starting transfers between devices, shards(): arrived = lax.all_to_all(leaving, ('lat', 'lon'), 0, 0, tiled=True)  11.5 us
    all_to_all x1, waiting for transfers between devices, shards(): lax.all_to_all(set_convolution(notes, arrived, n_lon), 'lon', 0, 0, tiled...  7.31 us
    all_to_all x1, starting transfers between devices, shards(): lax.all_to_all(set_convolution(notes, arrived, n_lon), 'lon', 0, 0, tiled...  4.53 us
    dynamic_update_slice x2, local copies, waits for them, and re-layouts, shards(): lax.dynamic_update_slice_in_dim(whole, rows, (1 - core) * 8 + 4 * part, a...  3.9 us
    pallas_call x1, Pallas kernels, leaving_tiles(): pl.pallas_call(leave_kernel, grid=(2,), in_specs=[pl.BlockSpec(subs.shape...  2.96 us
  transfers between devices with their start and end apart: 5, of which 3 were waited for; matrix products, arithmetic and copies ran while one was open for 9% of the time, Pallas kernels for 15%

profile of v5, /device:TPU:1, one launch (start us, length us, event | category | flops | bytes accessed | tf_op | source)
XLA Modules:
  0.0 104.2 jit_solution(998852650878248369)
XLA Ops:
  0.0 3.0 %shard_map.82 = bf16[128,9,8,128]{3,2,1,0:T(8,128)(2,1)} custom-call(s32[4,128]{1,0:T(4,128)} %bitcast.48, s32[4,128]{1,0:T(4,128)} %bitcast.49, bf16[128,4,8,256]{3,2,1,0:T(8,128)(2,1)} %bitcast.41), custom_call_target="tpu_custom_call" | custom-call | tf_op jit(solution)/shard_map/pallas_call | solution.py:157
  3.0 11.5 %all-to-all-start = ((bf16[128,9,8,128]{3,2,1,0:T(8,128)(2,1)}), bf16[128,9,8,128]{3,2,1,0:T(8,128)(2,1)S(1)}, u32[]{:S(2)}, u32[]{:S(2)}) async-start(bf16[128,9,8,128]{3,2,1,0:T(8,128)(2,1)} %shard_map.82), calls=%async_computation | async-start | bytes 4718592 | tf_op jit(solution)/shard_map/all_to_all | solution.py:351
  14.7 33.0 %all-to-all-done.tiles_ref = bf16[128,9,8,128]{3,2,1,0:T(8,128)(2,1)S(1)} async-done(((bf16[128,9,8,128]{3,2,1,0:T(8,128)(2,1)}), bf16[128,9,8,128]{3,2,1,0:T(8,128)(2,1)S(1)}, u32[]{:S(2)}, u32[]{:S(2)}) %all-to-all-start) | async-done | bytes 2359328 | tf_op jit(solution)/shard_map/all_to_all | solution.py:351
  47.8 11.6 %shard_map.83 = bf16[32,96,128]{2,1,0:T(8,128)(2,1)} custom-call(s32[128,8]{1,0:T(8,128)S(1)} %bitcast.31, bf16[128,9,8,128]{3,2,1,0:T(8,128)(2,1)S(1)} %all-to-all-done.tiles_ref), custom_call_target="tpu_custom_call" | custom-call | tf_op jit(solution)/shard_map/pallas_call | solution.py:121
  59.4 4.5 %all-to-all-start.1 = ((bf16[32,96,128]{2,1,0:T(8,128)(2,1)}), bf16[32,96,128]{2,1,0:T(8,128)(2,1)S(1)}, u32[]{:S(2)}, u32[]{:S(2)}) async-start(bf16[32,96,128]{2,1,0:T(8,128)(2,1)} %shard_map.83), calls=%async_computation.1 | async-start | bytes 1572864 | tf_op jit(solution)/shard_map/all_to_all | solution.py:354
  64.1 0.7 pad.28
  64.7 0.7 pad.29
  65.4 0.6 pad.24
  66.1 1.9 %rev.3 = bf16[3,3,256,512]{3,2,1,0:T(8,128)(2,1)S(1)} reverse(bf16[3,3,256,512]{3,2,1,0:T(8,128)(2,1)} %bitcast.40), dimensions={1} | reverse | bytes 4718592 | tf_op jit(solution)/shard_map/rev | solution.py:361
  68.0 0.6 pad_add_fusion.1.refs_0_
  68.7 0.7 pad_maximum_fusion.1.refs_4_.refs_5_
  69.3 1.0 pad_maximum_fusion.refs_5_.refs_6_
  70.3 0.7 broadcast_multiply_fusion
  71.0 7.3 %all-to-all-done.1.refs_1_.refs_2_ = bf16[32,96,128]{2,1,0:T(8,128)(2,1)S(1)} async-done(((bf16[32,96,128]{2,1,0:T(8,128)(2,1)}), bf16[32,96,128]{2,1,0:T(8,128)(2,1)S(1)}, u32[]{:S(2)}, u32[]{:S(2)}) %all-to-all-start.1) | async-done | bytes 786464 | tf_op jit(solution)/shard_map/all_to_all | solution.py:354
  78.3 2.1 %collective-permute-start = (bf16[32,16,128]{2,1,0:T(8,128)(2,1)S(1)}, bf16[32,16,128]{2,1,0:T(8,128)(2,1)S(1)}, u32[]{:S(2)}, u32[]{:S(2)}) collective-permute-start(bf16[32,16,128]{2,1,0:T(8,128)(2,1)S(1)} %slice.28), channel_id=1, source_target_pairs={{0,1},{2,3},{4,5},{6,7},{8,9},{10,11},{12,13},{14,15},{16,17},{18,... | collective-permute-start | bytes 393224 | tf_op jit(solution)/shard_map/ppermute | solution.py:358
  80.4 0.9 copy-done.1
  81.3 0.8 copy-done.2
  82.2 0.6 copy-done.4
  82.8 7.9 %shard_map.84 = (bf16[16,384,512]{2,1,0:T(8,128)(2,1)}, bf16[4,384,512]{2,1,0:T(8,128)(2,1)}) custom-call(s32[2]{0:T(128)S(1)} %copy-done.4, bf16[32,96,128]{2,1,0:T(8,128)(2,1)S(1)} %all-to-all-done.1.refs_1_.refs_2_, bf16[128,256]{1,0:T(8,128)(2,1)S(1)} %bitcast.34, bf16[256,256]{1,0:T(8,128)(2,1)S(1)} %bitcast.32, bf16[256,256]{1,0:T(8,128)(2,1)S(1)} %copy-done.1, ...), custom_call_target="tpu_custom_call" | custom-call | flops 8999999488 | bytes 12000000 | tf_op jit(solution)/shard_map/pallas_call | solution.py:277
  90.7 0.6 collective-permute-start.1
  91.3 7.9 %shard_map.85 = (bf16[16,384,512]{2,1,0:T(8,128)(2,1)}, bf16[4,384,512]{2,1,0:T(8,128)(2,1)}) custom-call(s32[2]{0:T(128)S(1)} %pad_add_fusion.refs_0_, bf16[32,16,128]{2,1,0:T(8,128)(2,1)S(1)} %collective-permute-done.refs_1_, bf16[32,96,128]{2,1,0:T(8,128)(2,1)S(1)} %all-to-all-done.1.refs_1_.refs_2_, ...), custom_call_target="tpu_custom_call", output_to_operand_aliasing={{0}: (10, {})} | custom-call | flops 8999999488 | bytes 12000000 | tf_op jit(solution)/shard_map/pallas_call | solution.py:277
  99.5 2.7 %constant_dynamic-update-slice_fusion.1 = bf16[16,384,512]{2,1,0:T(8,128)(2,1)} fusion(bf16[16,384,512]{2,1,0:T(8,128)(2,1)} %get-tuple-element.10, bf16[4,384,512]{2,1,0:T(8,128)(2,1)} %collective-permute-done.1, s32[]{:T(128)S(6)} %select_n.19), kind=kLoop, calls=%fused_computation.12 | loop fusion | bytes 3145732 | tf_op jit(solution)/shard_map/dynamic_update_slice | solution.py:381
  102.1 0.8 collective-permute-done.2
  102.9 1.2 %constant_dynamic-update-slice_fusion = bf16[16,384,512]{2,1,0:T(8,128)(2,1)} fusion(bf16[16,384,512]{2,1,0:T(8,128)(2,1)} %constant_dynamic-update-slice_fusion.1, bf16[4,384,512]{2,1,0:T(8,128)(2,1)S(1)} %collective-permute-done.2, s32[]{:T(128)S(6)} %select_n.20), kind=kLoop, calls=%fused_computation.11 | loop fusion | bytes 3145732 | tf_op jit(solution)/shard_map/dynamic_update_slice | solution.py:381
  (25 shorter events, 0.8 us)
Async XLA Ops:
  0.0 14.6 %copy-start = (bf16[6,23]{1,0:T(8,128)(2,1)S(1)}, bf16[6,23]{1,0:T(8,128)(2,1)}, u32[]{:S(2)}) copy-start(bf16[6,23]{1,0:T(8,128)(2,1)} %param.11) | copy-start | bytes 832
  3.0 11.5 %copy-start.5 = (bf16[9,24,256]{2,1,0:T(8,128)(2,1)S(1)}, bf16[9,24,256]{2,1,0:T(8,128)(2,1)}, u32[]{:S(2)}) copy-start(bf16[9,24,256]{2,1,0:T(8,128)(2,1)} %param.12) | copy-start | bytes 331780
  3.0 44.8 %all-to-all-start = ((bf16[128,9,8,128]{3,2,1,0:T(8,128)(2,1)}), bf16[128,9,8,128]{3,2,1,0:T(8,128)(2,1)S(1)}, u32[]{:S(2)}, u32[]{:S(2)}) async-start(bf16[128,9,8,128]{3,2,1,0:T(8,128)(2,1)} %shard_map.82), calls=%async_computation | async-start | bytes 4718592 | tf_op jit(solution)/shard_map/all_to_all | solution.py:351
  59.4 18.9 %all-to-all-start.1 = ((bf16[32,96,128]{2,1,0:T(8,128)(2,1)}), bf16[32,96,128]{2,1,0:T(8,128)(2,1)S(1)}, u32[]{:S(2)}, u32[]{:S(2)}) async-start(bf16[32,96,128]{2,1,0:T(8,128)(2,1)} %shard_map.83), calls=%async_computation.1 | async-start | bytes 1572864 | tf_op jit(solution)/shard_map/all_to_all | solution.py:354
  66.1 14.4 %copy-start.3 = (f32[512]{0:T(512)S(1)}, f32[512]{0:T(512)}, u32[]{:S(2)}) copy-start(f32[512]{0:T(512)} %param.15) | copy-start | bytes 6148
  78.3 13.0 %collective-permute-start = (bf16[32,16,128]{2,1,0:T(8,128)(2,1)S(1)}, bf16[32,16,128]{2,1,0:T(8,128)(2,1)S(1)}, u32[]{:S(2)}, u32[]{:S(2)}) collective-permute-start(bf16[32,16,128]{2,1,0:T(8,128)(2,1)S(1)} %slice.28), channel_id=1, source_target_pairs={{0,1},{2,3},{4,5},{6,7},{8,9},{10,11},{12,13},{14,15},{16,17},{18,... | collective-permute-start | bytes 393224 | tf_op jit(solution)/shard_map/ppermute | solution.py:358
  80.4 0.9 copy-start.1
  81.3 0.8 copy-start.2
  82.2 0.6 copy-start.4
  90.7 8.8 %collective-permute-start.1 = (bf16[4,384,512]{2,1,0:T(8,128)(2,1)}, bf16[4,384,512]{2,1,0:T(8,128)(2,1)}, u32[]{:S(2)}, u32[]{:S(2)}) collective-permute-start(bf16[4,384,512]{2,1,0:T(8,128)(2,1)} %get-tuple-element.11), channel_id=1, source_target_pairs={{0,1},{1,0},{2,3},{3,2},{4,5},{5,4},{6,7},{7,6},{8,9},{9,8},{10,11... | collective-permute-start | bytes 4718600 | tf_op jit(solution)/shard_map/ppermute | solution.py:379
  99.2 3.7 %collective-permute-start.2 = (bf16[4,384,512]{2,1,0:T(8,128)(2,1)}, bf16[4,384,512]{2,1,0:T(8,128)(2,1)S(1)}, u32[]{:S(2)}, u32[]{:S(2)}) collective-permute-start(bf16[4,384,512]{2,1,0:T(8,128)(2,1)} %get-tuple-element.12), channel_id=1, source_target_pairs={{0,1},{1,0},{2,3},{3,2},{4,5},{5,4},{6,7},{7,6},{8,9},{9,8},{10,11... | collective-permute-start | bytes 4718600 | tf_op jit(solution)/shard_map/ppermute | solution.py:379

commit v6 on v5

--- a/solution.py
+++ b/solution.py
@@ -169,10 +169,25 @@
     )(subs, rows, tiles)
 
 
+def placed(params, count, above, shift, low, high):
+    lane = iota((count, params.shape[0]), 0)
+    row_tap = lane // ROW_LANES - above
+    col_tap = lane // FEAT % PHASES + shift
+    wanted = (3 * row_tap + col_tap) * FEAT + lane % FEAT
+    inside = (row_tap >= 0) & (row_tap < 3) & (col_tap >= low) & (col_tap < high)
+    take = (inside & (iota(lane.shape, 1) == wanted)).astype(jnp.bfloat16)
+    return jnp.dot(take, params, preferred_element_type=jnp.float32).astype(jnp.bfloat16)
+
+
 def conv_kernel(first_block, *refs):
-    (flag_ref, *halo, own_ref, odd1_ref, odd2_ref, even1_ref, even2_ref, bias1_ref, weight2_hbm,
-     bias2_ref) = refs[: 9 + (first_block == 0)]
-    out_ref, send_ref, wide_ref, grid_ref, moved_ref, even_rows, odd_rows, weight2_ref, sem = refs[-9:]
+    flag_ref, *halo, own_ref, params_ref, weight2_hbm = refs[: 4 + (first_block == 0)]
+    (out_ref, send_ref, wide_ref, grid_ref, moved_ref, even_rows, odd_rows, weight2_ref, odd1_ref,
+     odd2_ref, even1_ref, even2_ref, sem) = refs[-13:]
+    bias1 = params_ref[9 * FEAT : 9 * FEAT + 1, :]
+    bias2 = jnp.concatenate(
+        [params_ref[9 * FEAT + 1 : 9 * FEAT + 2, :], params_ref[9 * FEAT + 2 : 9 * FEAT + 3, :]],
+        axis=1,
+    )
     step = pl.program_id(0)
     columns = grid_ref.shape[0]
     loads = [
@@ -200,7 +215,7 @@
         )
 
         def activate(half):
-            half = half + bias1_ref[...]
+            half = half + bias1
             return half * jnp.tanh(half) + half
 
         odd = activate(odd)
@@ -227,7 +242,7 @@
                 preferred_element_type=jnp.float32,
             )
             total = part if total is None else total + part
-        total = (total + bias2_ref[...]).astype(jnp.bfloat16).reshape(out_ref.shape)
+        total = (total + bias2).astype(jnp.bfloat16).reshape(out_ref.shape)
         out_ref[...] = total
         send_ref[...] = total
 
@@ -235,6 +250,13 @@
     def _():
         for load in loads:
             load.start()
+        params = params_ref[...].astype(jnp.bfloat16)
+        odd1_ref[...] = placed(params, 128, 1, -1, 0, 3)
+        odd2_ref[...] = placed(params, 256, 3, -1, 0, 3)
+        even1_ref[0:128, :] = placed(params, 128, 1, 1, 1, 3)
+        even1_ref[128:256, :] = placed(params, 128, 1, -3, 0, 1)
+        even2_ref[0:256, :] = placed(params, 256, 3, 1, 1, 3)
+        even2_ref[256:512, :] = placed(params, 256, 3, -3, 0, 1)
         for source in range(own_ref.shape[0]):
             own = own_ref[source].astype(jnp.float32)
             parts = [own[QUADS * k : QUADS * (k + 1)] for k in range(first_block, first_block + 4)]
@@ -261,11 +283,11 @@
             second_row(row)
 
 
-def convolutions(part, flags, halo, own, weights1, bias1, weights2, bias2, whole):
+def convolutions(part, flags, halo, own, params, weights2, whole):
     columns = QUADS * own.shape[0]
     full = lambda a: pl.BlockSpec(a.shape, lambda i, *_: (0,) * a.ndim)
     anywhere = pl.BlockSpec(memory_space=pl.ANY)
-    operands = [own, *weights1, bias1, weights2, bias2]
+    operands = [own, params, weights2]
     if part == 0:
         operands = [halo] + operands
     specs = [anywhere if a is weights2 else full(a) for a in operands]
@@ -291,6 +313,10 @@
                 pltpu.VMEM((5 * columns, 3 * C1), jnp.bfloat16),
                 pltpu.VMEM((4 * columns, 3 * C1), jnp.bfloat16),
                 pltpu.VMEM(weights2.shape, jnp.bfloat16),
+                pltpu.VMEM((128, C1), jnp.bfloat16),
+                pltpu.VMEM((256, C1), jnp.bfloat16),
+                pltpu.VMEM((256, C1), jnp.bfloat16),
+                pltpu.VMEM((512, C1), jnp.bfloat16),
                 pltpu.SemaphoreType.DMA((3, 3)),
             ],
         ),
@@ -317,20 +343,7 @@
         precision=lax.Precision.HIGHEST,
     )
     taps = jnp.concatenate([channels[:, :1], values, jnp.zeros_like(channels[:, :1])], axis=1)
-    taps = (0.5 * taps).astype(jnp.bfloat16).reshape(3, 3, FEAT, C1)
-
-    def placed(part, above, below, phase):
-        pads = ((above, below), (phase, PHASES - phase - part.shape[1]), (0, 0), (0, 0))
-        return jnp.pad(part, pads).reshape(-1, C1)
-
-    odd = [placed(taps, above, below, 1) for above, below in ((1, 0), (3, 2))]
-    even = [
-        jnp.concatenate(
-            [placed(taps[:, 1:], above, below, 0), placed(taps[:, :1], above, below, 3)], axis=0
-        )
-        for above, below in ((1, 0), (3, 2))
-    ]
-    return odd + even
+    return 0.5 * taps.reshape(9 * FEAT, C1)
 
 
 def shards(
@@ -351,13 +364,23 @@
     arrived = lax.all_to_all(leaving, ("lat", "lon"), 0, 0, tiled=True)
     notes = arrived[:, 2 * CAP, 0, : 2 * CAP].astype(jnp.int32)
 
-    own = lax.all_to_all(set_convolution(notes, arrived, n_lon), "lon", 0, 0, tiled=True)
+    halves = set_convolution(notes, arrived, n_lon)
+    halves, conv2_weight = lax.optimization_barrier((halves, conv2_weight))
+    own = lax.all_to_all(halves, "lon", 0, 0, tiled=True)
     last = own[:, 8 * QUADS - SB :]
     south = [(z * n_lon + i, z * n_lon + i + 1) for z in range(n_lat) for i in range(0, n_lon, 2)]
     south += [(b, b + n_lon - 1) for _, b in south if b + n_lon < n_lat * n_lon]
     halo = lax.ppermute(last, ("lat", "lon"), south)
 
-    weights1 = first_weights(embed_weight, conv1_weight)
+    params = jnp.concatenate(
+        [
+            first_weights(embed_weight, conv1_weight),
+            0.5 * conv1_bias[None],
+            conv2_bias.reshape(2, C1),
+            jnp.zeros((5, C1), jnp.float32),
+        ],
+        axis=0,
+    )
     weights2 = conv2_weight.reshape(3, 3, C1, C2)[:, ::-1].reshape(3, 3 * C1, C2)
     top = jnp.where((lax.axis_index("lat") == 0) & (core == 0), 0, 1)
     pairs = [(i, i ^ 1) for i in range(n_lon)]
@@ -370,10 +393,8 @@
             flags,
             halo,
             own,
-            weights1,
-            0.5 * conv1_bias[None],
+            params,
             weights2,
-            conv2_bias[None],
             whole,
         )
         swapped.append((part, lax.ppermute(half, "lon", pairs)))

time: 105 us -> 102 us (0.971)
  waiting for transfers between devices: 41.1 us -> 46 us
  local copies, waits for them, and re-layouts: 10.2 us -> 5.91 us
  other arithmetic: 3.14 us -> 0.37 us
    all_to_all x1, waiting for transfers between devices: 7.31 us -> 12.1 us  [shards(): own = lax.all_to_all(halves, 'lon', 0, 0, tiled=True)]
    unnamed x12 -> x8, local copies, waits for them, and re-layouts: 2.36 us -> 0.02 us
    pad x6 -> x0, local copies, waits for them, and re-layouts: 1.98 us -> none  [placed(): return jnp.pad(part, pads).reshape(-1, C1)]
    concatenate x3 -> x1, other arithmetic: 1.66 us -> 0.08 us  [shards(): jnp.concatenate([first_weights(embed_weight, conv1_weight), 0.5 * conv1_b...]
  transfers between devices with their start and end apart: 5 -> 5, of which waited for: 3 -> 3; matrix products, arithmetic and copies ran while one was open for 9% -> 5% of each run, Pallas kernels for 15% -> 16%
where the time goes in v6:
time: 102 us
  waiting for transfers between devices  46 us (45%)
  Pallas kernels  30.7 us (30%)
  starting transfers between devices  19 us (19%)
  local copies, waits for them, and re-layouts  5.91 us (6%)
    all_to_all x1, waiting for transfers between devices, shards(): arrived = lax.all_to_all(leaving, ('lat', 'lon'), 0, 0, tiled=True)  33 us
    pallas_call x2, Pallas kernels, convolutions(): pl.pallas_call(functools.partial(conv_kernel, 4 * part), grid_spec=pltpu....  16.1 us
    all_to_all x1, waiting for transfers between devices, shards(): own = lax.all_to_all(halves, 'lon', 0, 0, tiled=True)  12.1 us
    pallas_call x1, Pallas kernels, set_convolution(): pl.pallas_call(setconv_kernel, grid_spec=pltpu.PrefetchScalarGridSpec(num...  11.6 us
    all_to_all x1, starting transfers between devices, shards(): arrived = lax.all_to_all(leaving, ('lat', 'lon'), 0, 0, tiled=True)  11.5 us
    all_to_all x1, starting transfers between devices, shards(): own = lax.all_to_all(halves, 'lon', 0, 0, tiled=True)  4.53 us
    dynamic_update_slice x2, local copies, waits for them, and re-layouts, shards(): lax.dynamic_update_slice_in_dim(whole, rows, (1 - core) * 8 + 4 * part, a...  3.9 us
    pallas_call x1, Pallas kernels, leaving_tiles(): pl.pallas_call(leave_kernel, grid=(2,), in_specs=[pl.BlockSpec(subs.shape...  2.96 us
  transfers between devices with their start and end apart: 5, of which 3 were waited for; matrix products, arithmetic and copies ran while one was open for 5% of the time, Pallas kernels for 16%

profile of v6, /device:TPU:1, one launch (start us, length us, event | category | flops | bytes accessed | tf_op | source)
XLA Modules:
  0.0 102.1 jit_solution(7850278182524756228)
XLA Ops:
  0.0 3.0 %shard_map.82 = bf16[128,9,8,128]{3,2,1,0:T(8,128)(2,1)} custom-call(s32[4,128]{1,0:T(4,128)} %bitcast.27, s32[4,128]{1,0:T(4,128)} %bitcast.28, bf16[128,4,8,256]{3,2,1,0:T(8,128)(2,1)} %bitcast.25), custom_call_target="tpu_custom_call" | custom-call | tf_op jit(solution)/shard_map/pallas_call | solution.py:157
  3.0 11.5 %all-to-all-start = ((bf16[128,9,8,128]{3,2,1,0:T(8,128)(2,1)}), bf16[128,9,8,128]{3,2,1,0:T(8,128)(2,1)S(1)}, u32[]{:S(2)}, u32[]{:S(2)}) async-start(bf16[128,9,8,128]{3,2,1,0:T(8,128)(2,1)} %shard_map.82), calls=%async_computation | async-start | bytes 4718592 | tf_op jit(solution)/shard_map/all_to_all | solution.py:364
  14.5 0.1 pad.8.clone
  14.6 0.1 pad.5.clone
  14.7 0.1 pad_add_fusion.1.refs_0_
  14.8 33.0 %all-to-all-done.tiles_ref = bf16[128,9,8,128]{3,2,1,0:T(8,128)(2,1)S(1)} async-done(((bf16[128,9,8,128]{3,2,1,0:T(8,128)(2,1)}), bf16[128,9,8,128]{3,2,1,0:T(8,128)(2,1)S(1)}, u32[]{:S(2)}, u32[]{:S(2)}) %all-to-all-start) | async-done | bytes 2359328 | tf_op jit(solution)/shard_map/all_to_all | solution.py:364
  47.8 0.1 slice_convert_fusion
  47.8 11.6 %shard_map.83 = bf16[32,96,128]{2,1,0:T(8,128)(2,1)} custom-call(s32[128,8]{1,0:T(8,128)S(1)} %bitcast.23, bf16[128,9,8,128]{3,2,1,0:T(8,128)(2,1)S(1)} %all-to-all-done.tiles_ref), custom_call_target="tpu_custom_call" | custom-call | tf_op jit(solution)/shard_map/pallas_call | solution.py:121
  59.5 4.5 %all-to-all-start.1 = ((bf16[32,96,128]{2,1,0:T(8,128)(2,1)}), bf16[32,96,128]{2,1,0:T(8,128)(2,1)S(1)}, u32[]{:S(2)}, u32[]{:S(2)}) async-start(bf16[32,96,128]{2,1,0:T(8,128)(2,1)} %shard_map.83), calls=%async_computation.1 | async-start | bytes 1572864 | tf_op jit(solution)/shard_map/all_to_all | solution.py:369
  64.0 0.1 pad_add_fusion.refs_0_
  64.1 0.1 convolution_bitcast_fusion
  64.2 0.1 fusion.1
  64.3 0.1 maximum_maximum_fusion.refs_2_.refs_3_
  64.4 1.8 %rev.3 = bf16[3,3,256,512]{3,2,1,0:T(8,128)(2,1)S(1)} reverse(bf16[3,3,256,512]{3,2,1,0:T(8,128)(2,1)} %bitcast.24), dimensions={1} | reverse | bytes 4718592 | tf_op jit(solution)/shard_map/rev | solution.py:384
  66.2 12.1 %all-to-all-done.1.refs_1_.refs_2_ = bf16[32,96,128]{2,1,0:T(8,128)(2,1)S(1)} async-done(((bf16[32,96,128]{2,1,0:T(8,128)(2,1)}), bf16[32,96,128]{2,1,0:T(8,128)(2,1)S(1)}, u32[]{:S(2)}, u32[]{:S(2)}) %all-to-all-start.1) | async-done | bytes 786464 | tf_op jit(solution)/shard_map/all_to_all | solution.py:369
  78.4 2.1 %collective-permute-start = (bf16[32,16,128]{2,1,0:T(8,128)(2,1)S(1)}, bf16[32,16,128]{2,1,0:T(8,128)(2,1)S(1)}, u32[]{:S(2)}, u32[]{:S(2)}) collective-permute-start(bf16[32,16,128]{2,1,0:T(8,128)(2,1)S(1)} %slice.21), channel_id=1, source_target_pairs={{0,1},{2,3},{4,5},{6,7},{8,9},{10,11},{12,13},{14,15},{16,17},{18,... | collective-permute-start | bytes 393224 | tf_op jit(solution)/shard_map/ppermute | solution.py:373
  80.4 8.1 %shard_map.84 = (bf16[16,384,512]{2,1,0:T(8,128)(2,1)}, bf16[4,384,512]{2,1,0:T(8,128)(2,1)}) custom-call(s32[2]{0:T(128)S(1)} %pad_add_fusion.1.refs_0_, bf16[32,96,128]{2,1,0:T(8,128)(2,1)S(1)} %all-to-all-done.1.refs_1_.refs_2_, f32[80,256]{1,0:T(8,128)S(1)} %maximum_maximum_fusion.refs_2_.refs_3_, bf16[3,768,512]{2,1,0:T(8,128)(2,1)S(1)} %bitcast.21), custom_call_target="tpu_custom_call" | custom-call | flops 8999999488 | bytes 12000000 | tf_op jit(solution)/shard_map/pallas_call | solution.py:299
  88.5 0.6 collective-permute-start.1
  89.1 0.0 collective-permute-done.refs_1_
  89.1 8.0 %shard_map.85 = (bf16[16,384,512]{2,1,0:T(8,128)(2,1)}, bf16[4,384,512]{2,1,0:T(8,128)(2,1)}) custom-call(s32[2]{0:T(128)S(1)} %pad_add_fusion.refs_0_, bf16[32,16,128]{2,1,0:T(8,128)(2,1)S(1)} %collective-permute-done.refs_1_, bf16[32,96,128]{2,1,0:T(8,128)(2,1)S(1)} %all-to-all-done.1.refs_1_.refs_2_, ...), custom_call_target="tpu_custom_call", output_to_operand_aliasing={{0}: (5, {})} | custom-call | flops 8999999488 | bytes 12000000 | tf_op jit(solution)/shard_map/pallas_call | solution.py:299
  97.2 0.2 collective-permute-start.2
  97.4 2.7 %constant_dynamic-update-slice_fusion.1 = bf16[16,384,512]{2,1,0:T(8,128)(2,1)} fusion(bf16[16,384,512]{2,1,0:T(8,128)(2,1)} %get-tuple-element.14, bf16[4,384,512]{2,1,0:T(8,128)(2,1)} %collective-permute-done.1, s32[]{:T(128)S(6)} %select_n.19), kind=kLoop, calls=%fused_computation.12 | loop fusion | bytes 3145732 | tf_op jit(solution)/shard_map/dynamic_update_slice | solution.py:402
  100.1 0.8 collective-permute-done.2
  100.9 1.2 %constant_dynamic-update-slice_fusion = bf16[16,384,512]{2,1,0:T(8,128)(2,1)} fusion(bf16[16,384,512]{2,1,0:T(8,128)(2,1)} %constant_dynamic-update-slice_fusion.1, bf16[4,384,512]{2,1,0:T(8,128)(2,1)S(1)} %collective-permute-done.2, s32[]{:T(128)S(6)} %select_n.20), kind=kLoop, calls=%fused_computation.11 | loop fusion | bytes 3145732 | tf_op jit(solution)/shard_map/dynamic_update_slice | solution.py:402
  (14 shorter events, 0.1 us)
Async XLA Ops:
  0.0 64.1 %copy-start = (bf16[6,23]{1,0:T(8,128)(2,1)S(1)}, bf16[6,23]{1,0:T(8,128)(2,1)}, u32[]{:S(2)}) copy-start(bf16[6,23]{1,0:T(8,128)(2,1)} %param.11) | copy-start | bytes 832
  3.0 11.5 %copy-start.2 = (f32[512]{0:T(512)S(1)}, f32[512]{0:T(512)}, u32[]{:S(2)}) copy-start(f32[512]{0:T(512)} %param.15) | copy-start | bytes 6148
  3.0 11.8 %copy-start.3 = (f32[256]{0:T(256)S(1)}, f32[256]{0:T(256)}, u32[]{:S(2)}) copy-start(f32[256]{0:T(256)} %param.13) | copy-start | bytes 3076
  3.0 11.8 %copy-start.1 = (bf16[9,24,256]{2,1,0:T(8,128)(2,1)S(1)}, bf16[9,24,256]{2,1,0:T(8,128)(2,1)}, u32[]{:S(2)}) copy-start(bf16[9,24,256]{2,1,0:T(8,128)(2,1)} %param.12) | copy-start | bytes 331780
  3.0 44.8 %all-to-all-start = ((bf16[128,9,8,128]{3,2,1,0:T(8,128)(2,1)}), bf16[128,9,8,128]{3,2,1,0:T(8,128)(2,1)S(1)}, u32[]{:S(2)}, u32[]{:S(2)}) async-start(bf16[128,9,8,128]{3,2,1,0:T(8,128)(2,1)} %shard_map.82), calls=%async_computation | async-start | bytes 4718592 | tf_op jit(solution)/shard_map/all_to_all | solution.py:364
  59.5 18.9 %all-to-all-start.1 = ((bf16[32,96,128]{2,1,0:T(8,128)(2,1)}), bf16[32,96,128]{2,1,0:T(8,128)(2,1)S(1)}, u32[]{:S(2)}, u32[]{:S(2)}) async-start(bf16[32,96,128]{2,1,0:T(8,128)(2,1)} %shard_map.83), calls=%async_computation.1 | async-start | bytes 1572864 | tf_op jit(solution)/shard_map/all_to_all | solution.py:369
  78.4 10.8 %collective-permute-start = (bf16[32,16,128]{2,1,0:T(8,128)(2,1)S(1)}, bf16[32,16,128]{2,1,0:T(8,128)(2,1)S(1)}, u32[]{:S(2)}, u32[]{:S(2)}) collective-permute-start(bf16[32,16,128]{2,1,0:T(8,128)(2,1)S(1)} %slice.21), channel_id=1, source_target_pairs={{0,1},{2,3},{4,5},{6,7},{8,9},{10,11},{12,13},{14,15},{16,17},{18,... | collective-permute-start | bytes 393224 | tf_op jit(solution)/shard_map/ppermute | solution.py:373
  88.5 8.9 %collective-permute-start.1 = (bf16[4,384,512]{2,1,0:T(8,128)(2,1)}, bf16[4,384,512]{2,1,0:T(8,128)(2,1)}, u32[]{:S(2)}, u32[]{:S(2)}) collective-permute-start(bf16[4,384,512]{2,1,0:T(8,128)(2,1)} %get-tuple-element.15), channel_id=1, source_target_pairs={{0,1},{1,0},{2,3},{3,2},{4,5},{5,4},{6,7},{7,6},{8,9},{9,8},{10,11... | collective-permute-start | bytes 4718600 | tf_op jit(solution)/shard_map/ppermute | solution.py:400
  97.2 3.7 %collective-permute-start.2 = (bf16[4,384,512]{2,1,0:T(8,128)(2,1)}, bf16[4,384,512]{2,1,0:T(8,128)(2,1)S(1)}, u32[]{:S(2)}, u32[]{:S(2)}) collective-permute-start(bf16[4,384,512]{2,1,0:T(8,128)(2,1)} %get-tuple-element.16), channel_id=1, source_target_pairs={{0,1},{1,0},{2,3},{3,2},{4,5},{5,4},{6,7},{7,6},{8,9},{9,8},{10,11... | collective-permute-start | bytes 4718600 | tf_op jit(solution)/shard_map/ppermute | solution.py:400

commit v7 on v6

--- a/solution.py
+++ b/solution.py
@@ -29,8 +29,14 @@
     return lax.broadcasted_iota(jnp.int32, shape, axis)
 
 
-def setconv_kernel(note_ref, tiles_ref, out_ref, *sums):
+def setconv_kernel(note_ref, place_ref, tiles_ref, out_ref, *sums):
     step = pl.program_id(0)
+
+    def note_row(source):
+        index = (place_ref[0] - step + 4) % 4
+        for axis, at in ((1, source // 8), (2, source // 2 % 4)):
+            index = index * 4 + (place_ref[axis] - at + 4) % 4
+        return index * 2 + (place_ref[3] - source % 2 + 2) % 2
 
     @pl.when(step == 0)
     def _():
@@ -42,10 +48,10 @@
     center_row = (row.astype(jnp.float32) + 0.5) * ROOT_HALF_LOG2E
     center_col = ((row % 4 * 4 + row // 4).astype(jnp.float32) + 0.5) * ROOT_HALF_LOG2E
 
-    def add_tile(source, slot, total):
-        tile = jnp.concatenate([tiles_ref[source, slot], tiles_ref[source, slot + CAP]], axis=1)
+    def add_tile(source, slot, note, total):
+        tile = tiles_ref[source, slot]
         place = tile.astype(jnp.float32)
-        live = lane < note_ref[step * SOURCES + source, CAP + slot]
+        live = lane < note_ref[note, CAP + slot]
         place_row = jnp.where(live, place[0:1], FAR)
         off_row = center_row - place_row * ROOT_HALF_LOG2E
         off_col = center_col - place[1:2] * ROOT_HALF_LOG2E
@@ -59,12 +65,13 @@
             (((1,), (1,)), ((), ())),
             preferred_element_type=jnp.float32,
         )
-        sub = note_ref[step * SOURCES + source, slot]
+        sub = note_ref[note, slot]
         total[sub] = total[sub] + part
 
     for k in range(SOURCES):
+        note = note_row(k)
         for slot in range(CAP):
-            add_tile(k, slot, sums[slot])
+            add_tile(k, slot, note, sums[slot])
 
     @pl.when(step == pl.num_programs(0) - 1)
     def _():
@@ -116,12 +123,12 @@
                 out_ref[2 * k + half] = rows
 
 
-def set_convolution(notes, arrived, copies):
+def set_convolution(notes, place, arrived, copies):
     out = jax.ShapeDtypeStruct((copies, 8 * QUADS, 128), jnp.bfloat16)
     return pl.pallas_call(
         setconv_kernel,
         grid_spec=pltpu.PrefetchScalarGridSpec(
-            num_scalar_prefetch=1,
+            num_scalar_prefetch=2,
             grid=(arrived.shape[0] // SOURCES,),
             in_specs=[pl.BlockSpec((SOURCES,) + arrived.shape[1:], lambda i, *_: (i, 0, 0, 0))],
             out_specs=pl.BlockSpec(out.shape, lambda i, *_: (0, 0, 0)),
@@ -131,42 +138,7 @@
         compiler_params=pltpu.CompilerParams(
             dimension_semantics=("arbitrary",), vmem_limit_bytes=24 << 20
         ),
-    )(notes, arrived)
-
-
-def leave_kernel(sub_ref, rows_ref, tiles_ref, out_ref, notes_ref):
-    step = pl.program_id(0)
-    count = tiles_ref.shape[0]
-
-    @pl.when(step == 0)
-    def _():
-        both = jnp.concatenate([sub_ref[...], rows_ref[...]], axis=0).astype(jnp.float32)
-        blank = jnp.zeros((128 - 2 * CAP, both.shape[1]), jnp.float32)
-        notes_ref[...] = jnp.concatenate([both, blank], axis=0).T
-
-    notes = notes_ref[pl.ds(step * count, count), :]
-    notes = jnp.broadcast_to(notes[:, None, :], (count, FEAT, 128)).astype(jnp.bfloat16)
-    out_ref[:, :CAP] = tiles_ref[:, :, :, :128]
-    out_ref[:, CAP : 2 * CAP] = tiles_ref[:, :, :, 128:]
-    out_ref[:, 2 * CAP] = notes
-
-
-def leaving_tiles(tiles, subs, rows):
-    count = tiles.shape[0]
-    part = count // 2
-    return pl.pallas_call(
-        leave_kernel,
-        grid=(2,),
-        in_specs=[
-            pl.BlockSpec(subs.shape, lambda i: (0, 0)),
-            pl.BlockSpec(rows.shape, lambda i: (0, 0)),
-            pl.BlockSpec((part,) + tiles.shape[1:], lambda i: (i, 0, 0, 0)),
-        ],
-        out_specs=pl.BlockSpec((part, 2 * CAP + 1, FEAT, 128), lambda i: (i, 0, 0, 0)),
-        out_shape=jax.ShapeDtypeStruct((count, 2 * CAP + 1, FEAT, 128), jnp.bfloat16),
-        scratch_shapes=[pltpu.VMEM((count, 128), jnp.float32)],
-        compiler_params=pltpu.CompilerParams(vmem_limit_bytes=60 << 20),
-    )(subs, rows, tiles)
+    )(notes, place, arrived)
 
 
 def placed(params, count, above, shift, low, high):
@@ -360,11 +332,38 @@
     n_lat = lax.axis_size("lat")
     core = lax.axis_index("lon") % 2
 
-    leaving = leaving_tiles(obs_tiles[0], tile_block[0].T, tile_rows[0].T)
-    arrived = lax.all_to_all(leaving, ("lat", "lon"), 0, 0, tiled=True)
-    notes = arrived[:, 2 * CAP, 0, : 2 * CAP].astype(jnp.int32)
-
-    halves = set_convolution(notes, arrived, n_lon)
+    arrived = lax.all_to_all(obs_tiles[0], ("lat", "lon"), 0, 0, tiled=True)
+
+    lon = lax.axis_index("lon")
+    place = [lax.axis_index("lat"), lon // 8, lon // 2 % 4, core]
+    notes = jnp.concatenate([tile_block[0], tile_rows[0]], axis=1).astype(jnp.bfloat16)
+    notes = notes.reshape(4, 4, 4, 2, 2 * CAP)
+    for axis, at in enumerate(place):
+        size = notes.shape[axis]
+        notes = lax.dynamic_slice_in_dim(
+            jnp.concatenate([notes, notes], axis=axis), at, size, axis=axis
+        )
+
+    def ahead(i, axis, k):
+        if axis == 1:
+            return (i + 8 * k) % n_lon
+        if axis == 2:
+            return i // 8 * 8 + (i + 2 * k) % 8
+        return i ^ k
+
+    for axis in range(4):
+        parts = [lax.index_in_dim(notes, k, axis) for k in range(notes.shape[axis])]
+        for k in range(1, len(parts)):
+            if axis == 0:
+                parts[k] = lax.ppermute(parts[k], "lat", [(i, (i + k) % n_lat) for i in range(n_lat)])
+            else:
+                parts[k] = lax.ppermute(
+                    parts[k], "lon", [(i, ahead(i, axis, k)) for i in range(n_lon)]
+                )
+        notes = jnp.concatenate(parts, axis=axis)
+    notes = notes.reshape(-1, 2 * CAP).astype(jnp.int32)
+
+    halves = set_convolution(notes, jnp.stack(place).astype(jnp.int32), arrived, n_lon)
     halves, conv2_weight = lax.optimization_barrier((halves, conv2_weight))
     own = lax.all_to_all(halves, "lon", 0, 0, tiled=True)
     last = own[:, 8 * QUADS - SB :]

time: 102 us -> 112 us (1.098)
  starting transfers between devices: 19 us -> 51.6 us
  waiting for transfers between devices: 46 us -> 24.5 us
  Pallas kernels: 30.7 us -> 27.8 us
    all_to_all x1, waiting for transfers between devices: 33 us -> 0.01 us  [shards(): arrived = lax.all_to_all(obs_tiles[0], ('lat', 'lon'), 0, 0, tiled=True)]
    ppermute x0 -> x10, starting transfers between devices: none -> 29.8 us  [the longest x7 24.3 us: shards(): lax.ppermute(parts[k], 'lon', [(i, ahead(i, axis, k)) for i in range(n_lo...]
    ppermute x0 -> x10, waiting for transfers between devices: none -> 11.8 us  [the longest x7 8.16 us: shards(): lax.ppermute(parts[k], 'lon', [(i, ahead(i, axis, k)) for i in range(n_lo...]
    pallas_call x1 -> x0, Pallas kernels: 2.96 us -> none  [leaving_tiles(): pl.pallas_call(leave_kernel, grid=(2,), in_specs=[pl.BlockSpec(subs.shape...]
    all_to_all x1, starting transfers between devices: 4.53 us -> 7.23 us  [shards(): own = lax.all_to_all(halves, 'lon', 0, 0, tiled=True)]
  transfers between devices with their start and end apart: 5 -> 15, of which waited for: 3 -> 9; matrix products, arithmetic and copies ran while one was open for 5% -> 6% of each run, Pallas kernels for 16% -> 14%
where the time goes in v7:
time: 112 us
  starting transfers between devices  51.6 us (46%)
  Pallas kernels  27.8 us (25%)
  waiting for transfers between devices  24.5 us (22%)
  local copies, waits for them, and re-layouts  6.27 us (6%)
  other arithmetic  1.33 us (1%)
    ppermute x7, starting transfers between devices, shards(): lax.ppermute(parts[k], 'lon', [(i, ahead(i, axis, k)) for i in range(n_lo...  24.3 us
    pallas_call x2, Pallas kernels, convolutions(): pl.pallas_call(functools.partial(conv_kernel, 4 * part), grid_spec=pltpu....  16.1 us
    all_to_all x1, waiting for transfers between devices, shards(): own = lax.all_to_all(halves, 'lon', 0, 0, tiled=True)  12 us
    pallas_call x1, Pallas kernels, set_convolution(): pl.pallas_call(setconv_kernel, grid_spec=pltpu.PrefetchScalarGridSpec(num...  11.7 us
    all_to_all x1, starting transfers between devices, shards(): arrived = lax.all_to_all(obs_tiles[0], ('lat', 'lon'), 0, 0, tiled=True)  11.5 us
    ppermute x7, waiting for transfers between devices, shards(): lax.ppermute(parts[k], 'lon', [(i, ahead(i, axis, k)) for i in range(n_lo...  8.16 us
    all_to_all x1, starting transfers between devices, shards(): own = lax.all_to_all(halves, 'lon', 0, 0, tiled=True)  7.23 us
    ppermute x3, starting transfers between devices, shards(): lax.ppermute(parts[k], 'lat', [(i, (i + k) % n_lat) for i in range(n_lat)])  5.42 us
  transfers between devices with their start and end apart: 15, of which 9 were waited for; matrix products, arithmetic and copies ran while one was open for 6% of the time, Pallas kernels for 14%

profile of v7, /device:TPU:1, one launch (start us, length us, event | category | flops | bytes accessed | tf_op | source)
XLA Modules:
  0.0 111.9 jit_solution(9142324283428099856)
XLA Ops:
  0.0 11.5 %all-to-all-start = ((bf16[128,4,8,256]{3,2,1,0:T(8,128)(2,1)}), bf16[128,4,8,256]{3,2,1,0:T(8,128)(2,1)S(1)}, u32[]{:S(2)}, u32[]{:S(2)}) async-start(bf16[128,4,8,256]{3,2,1,0:T(8,128)(2,1)} %bitcast.24), calls=%async_computation | async-start | bytes 4194304 | tf_op jit(solution)/shard_map/all_to_all | solution.py:335
  12.6 1.6 %collective-permute-start = (bf16[1,4,4,2,8]{4,3,2,1,0:T(2,128)(2,1)S(1)}, bf16[1,4,4,2,8]{4,3,2,1,0:T(2,128)(2,1)S(1)}, u32[]{:S(2)}, u32[]{:S(2)}) collective-permute-start(bf16[1,4,4,2,8]{4,3,2,1,0:T(2,128)(2,1)S(1)} %get-tuple-element.29), channel_id=1, source_target_pairs={{0,32},{32,64},{64,96},{96,0},{1,33},{33,65},{65,97},{97,1},{2,34}... | collective-permute-start | bytes 1544 | tf_op jit(solution)/shard_map/ppermute | solution.py:358
  14.1 2.9 %collective-permute-start.1 = (bf16[1,4,4,2,8]{4,3,2,1,0:T(2,128)(2,1)S(1)}, bf16[1,4,4,2,8]{4,3,2,1,0:T(2,128)(2,1)S(1)}, u32[]{:S(2)}, u32[]{:S(2)}) collective-permute-start(bf16[1,4,4,2,8]{4,3,2,1,0:T(2,128)(2,1)S(1)} %get-tuple-element.28), channel_id=1, source_target_pairs={{0,64},{32,96},{64,0},{96,32},{1,65},{33,97},{65,1},{97,33},{2,66}... | collective-permute-start | bytes 1544 | tf_op jit(solution)/shard_map/ppermute | solution.py:358
  17.1 0.9 collective-permute-start.2
  18.0 3.3 %collective-permute-done.1 = bf16[1,4,4,2,8]{4,3,2,1,0:T(2,128)(2,1)S(1)} collective-permute-done((bf16[1,4,4,2,8]{4,3,2,1,0:T(2,128)(2,1)S(1)}, bf16[1,4,4,2,8]{4,3,2,1,0:T(2,128)(2,1)S(1)}, u32[]{:S(2)}, u32[]{:S(2)}) %collective-permute-start.1) | collective-permute-done | bytes 544 | tf_op jit(solution)/shard_map/ppermute | solution.py:358
  21.8 8.0 %collective-permute-start.3 = (bf16[4,1,4,2,8]{4,3,2,1,0:T(2,128)(2,1)S(1)}, bf16[4,1,4,2,8]{4,3,2,1,0:T(2,128)(2,1)S(1)}, u32[]{:S(2)}, u32[]{:S(2)}) collective-permute-start(bf16[4,1,4,2,8]{4,3,2,1,0:T(2,128)(2,1)S(1)} %get-tuple-element.26), channel_id=1, source_target_pairs={{0,8},{1,9},{2,10},{3,11},{4,12},{5,13},{6,14},{7,15},{8,16},{9,17... | collective-permute-start | bytes 1544 | tf_op jit(solution)/shard_map/ppermute | solution.py:360
  29.8 2.5 %collective-permute-start.5 = (bf16[4,1,4,2,8]{4,3,2,1,0:T(2,128)(2,1)S(1)}, bf16[4,1,4,2,8]{4,3,2,1,0:T(2,128)(2,1)S(1)}, u32[]{:S(2)}, u32[]{:S(2)}) collective-permute-start(bf16[4,1,4,2,8]{4,3,2,1,0:T(2,128)(2,1)S(1)} %get-tuple-element.24), channel_id=1, source_target_pairs={{0,24},{1,25},{2,26},{3,27},{4,28},{5,29},{6,30},{7,31},{8,0},{9,1... | collective-permute-start | bytes 1544 | tf_op jit(solution)/shard_map/ppermute | solution.py:360
  32.3 4.4 %collective-permute-done.3 = bf16[4,1,4,2,8]{4,3,2,1,0:T(2,128)(2,1)S(1)} collective-permute-done((bf16[4,1,4,2,8]{4,3,2,1,0:T(2,128)(2,1)S(1)}, bf16[4,1,4,2,8]{4,3,2,1,0:T(2,128)(2,1)S(1)}, u32[]{:S(2)}, u32[]{:S(2)}) %collective-permute-start.3) | collective-permute-done | bytes 544 | tf_op jit(solution)/shard_map/ppermute | solution.py:360
  36.7 0.7 collective-permute-done.4
  37.5 1.3 %collective-permute-start.6 = (bf16[4,4,1,2,8]{4,3,2,1,0:T(2,128)(2,1)S(1)}, bf16[4,4,1,2,8]{4,3,2,1,0:T(2,128)(2,1)S(1)}, u32[]{:S(2)}, u32[]{:S(2)}) collective-permute-start(bf16[4,4,1,2,8]{4,3,2,1,0:T(2,128)(2,1)S(1)} %get-tuple-element.22), channel_id=1, source_target_pairs={{0,2},{1,3},{2,4},{3,5},{4,6},{5,7},{6,0},{7,1},{8,10},{9,11},{10,... | collective-permute-start | bytes 1544 | tf_op jit(solution)/shard_map/ppermute | solution.py:360
  38.7 8.6 %collective-permute-start.7 = (bf16[4,4,1,2,8]{4,3,2,1,0:T(2,128)(2,1)S(1)}, bf16[4,4,1,2,8]{4,3,2,1,0:T(2,128)(2,1)S(1)}, u32[]{:S(2)}, u32[]{:S(2)}) collective-permute-start(bf16[4,4,1,2,8]{4,3,2,1,0:T(2,128)(2,1)S(1)} %get-tuple-element.21), channel_id=1, source_target_pairs={{0,4},{1,5},{2,6},{3,7},{4,0},{5,1},{6,2},{7,3},{8,12},{9,13},{10,... | collective-permute-start | bytes 1544 | tf_op jit(solution)/shard_map/ppermute | solution.py:360
  47.4 1.0 collective-permute-done.7
  48.4 1.4 %collective-permute-done.8 = bf16[4,4,1,2,8]{4,3,2,1,0:T(2,128)(2,1)S(1)} collective-permute-done((bf16[4,4,1,2,8]{4,3,2,1,0:T(2,128)(2,1)S(1)}, bf16[4,4,1,2,8]{4,3,2,1,0:T(2,128)(2,1)S(1)}, u32[]{:S(2)}, u32[]{:S(2)}) %collective-permute-start.8) | collective-permute-done | bytes 544 | tf_op jit(solution)/shard_map/ppermute | solution.py:360
  50.0 4.0 %collective-permute-start.9 = (bf16[4,4,4,1,8]{4,3,2,1,0:T(2,128)(2,1)S(1)}, bf16[4,4,4,1,8]{4,3,2,1,0:T(2,128)(2,1)S(1)}, u32[]{:S(2)}, u32[]{:S(2)}) collective-permute-start(bf16[4,4,4,1,8]{4,3,2,1,0:T(2,128)(2,1)S(1)} %get-tuple-element.18), channel_id=1, source_target_pairs={{0,1},{1,0},{2,3},{3,2},{4,5},{5,4},{6,7},{7,6},{8,9},{9,8},{10,11... | collective-permute-start | bytes 3080 | tf_op jit(solution)/shard_map/ppermute | solution.py:360
  55.0 11.7 %shard_map.82 = bf16[32,96,128]{2,1,0:T(8,128)(2,1)} custom-call(s32[128,8]{1,0:T(8,128)S(1)} %convert.12.note_ref, s32[4]{0:T(128)S(1)} %pad_add_fusion.1.place_ref, bf16[128,4,8,256]{3,2,1,0:T(8,128)(2,1)S(1)} %all-to-all-done.tiles_ref), custom_call_target="tpu_custom_call" | custom-call | tf_op jit(solution)/shard_map/pallas_call | solution.py:128
  66.6 7.2 %all-to-all-start.1 = ((bf16[32,96,128]{2,1,0:T(8,128)(2,1)}), bf16[32,96,128]{2,1,0:T(8,128)(2,1)S(1)}, u32[]{:S(2)}, u32[]{:S(2)}) async-start(bf16[32,96,128]{2,1,0:T(8,128)(2,1)} %shard_map.82), calls=%async_computation.1 | async-start | bytes 1572864 | tf_op jit(solution)/shard_map/all_to_all | solution.py:368
  74.3 1.8 %rev.3 = bf16[3,3,256,512]{3,2,1,0:T(8,128)(2,1)S(1)} reverse(bf16[3,3,256,512]{3,2,1,0:T(8,128)(2,1)} %bitcast.23), dimensions={1} | reverse | bytes 4718592 | tf_op jit(solution)/shard_map/rev | solution.py:383
  76.1 12.0 %all-to-all-done.1.refs_1_.refs_2_ = bf16[32,96,128]{2,1,0:T(8,128)(2,1)S(1)} async-done(((bf16[32,96,128]{2,1,0:T(8,128)(2,1)}), bf16[32,96,128]{2,1,0:T(8,128)(2,1)S(1)}, u32[]{:S(2)}, u32[]{:S(2)}) %all-to-all-start.1) | async-done | bytes 786464 | tf_op jit(solution)/shard_map/all_to_all | solution.py:368
  88.1 2.4 %collective-permute-start.10 = (bf16[32,16,128]{2,1,0:T(8,128)(2,1)S(1)}, bf16[32,16,128]{2,1,0:T(8,128)(2,1)S(1)}, u32[]{:S(2)}, u32[]{:S(2)}) collective-permute-start(bf16[32,16,128]{2,1,0:T(8,128)(2,1)S(1)} %slice.86), channel_id=1, source_target_pairs={{0,1},{2,3},{4,5},{6,7},{8,9},{10,11},{12,13},{14,15},{16,17},{18,... | collective-permute-start | bytes 393224 | tf_op jit(solution)/shard_map/ppermute | solution.py:372
  90.6 8.1 %shard_map.83 = (bf16[16,384,512]{2,1,0:T(8,128)(2,1)}, bf16[4,384,512]{2,1,0:T(8,128)(2,1)}) custom-call(s32[2]{0:T(128)S(1)} %pad_add_fusion.2.refs_0_, bf16[32,96,128]{2,1,0:T(8,128)(2,1)S(1)} %all-to-all-done.1.refs_1_.refs_2_, f32[80,256]{1,0:T(8,128)S(1)} %maximum_maximum_fusion.refs_2_.refs_3_, bf16[3,768,512]{2,1,0:T(8,128)(2,1)S(1)} %bitcast.21), custom_call_target="tpu_custom_call" | custom-call | flops 8999999488 | bytes 12000000 | tf_op jit(solution)/shard_map/pallas_call | solution.py:271
  98.9 8.1 %shard_map.84 = (bf16[16,384,512]{2,1,0:T(8,128)(2,1)}, bf16[4,384,512]{2,1,0:T(8,128)(2,1)}) custom-call(s32[2]{0:T(128)S(1)} %pad_add_fusion.refs_0_, bf16[32,16,128]{2,1,0:T(8,128)(2,1)S(1)} %collective-permute-done.10.refs_1_, bf16[32,96,128]{2,1,0:T(8,128)(2,1)S(1)} %all-to-all-done.1.refs_1_.refs_2_, ...), custom_call_target="tpu_custom_call", output_to_operand_aliasing={{0}: (5, {})} | custom-call | flops 8999999488 | bytes 12000000 | tf_op jit(solution)/shard_map/pallas_call | solution.py:271
  107.4 2.7 %constant_dynamic-update-slice_fusion.1 = bf16[16,384,512]{2,1,0:T(8,128)(2,1)} fusion(bf16[16,384,512]{2,1,0:T(8,128)(2,1)} %get-tuple-element.14, bf16[4,384,512]{2,1,0:T(8,128)(2,1)} %collective-permute-done.11, s32[]{:T(128)S(6)} %select_n.49), kind=kLoop, calls=%fused_computation.27 | loop fusion | bytes 3145732 | tf_op jit(solution)/shard_map/dynamic_update_slice | solution.py:401
  110.0 0.6 collective-permute-done.12
  110.6 1.2 %constant_dynamic-update-slice_fusion = bf16[16,384,512]{2,1,0:T(8,128)(2,1)} fusion(bf16[16,384,512]{2,1,0:T(8,128)(2,1)} %constant_dynamic-update-slice_fusion.1, bf16[4,384,512]{2,1,0:T(8,128)(2,1)S(1)} %collective-permute-done.12, s32[]{:T(128)S(6)} %select_n.50), kind=kLoop, calls=%fused_computation.26 | loop fusion | bytes 3145732 | tf_op jit(solution)/shard_map/dynamic_update_slice | solution.py:401
  (54 shorter events, 3.7 us)
Async XLA Ops:
  0.0 74.0 %copy-start = (bf16[6,23]{1,0:T(8,128)(2,1)S(1)}, bf16[6,23]{1,0:T(8,128)(2,1)}, u32[]{:S(2)}) copy-start(bf16[6,23]{1,0:T(8,128)(2,1)} %param.11) | copy-start | bytes 832
  0.0 11.6 %copy-start.2 = (s32[1,128,4]{1,2,0:T(4,128)S(1)}, s32[1,128,4]{1,2,0:T(4,128)}, u32[]{:S(2)}) copy-start(s32[1,128,4]{1,2,0:T(4,128)} %param.9) | copy-start | bytes 6148
  0.0 11.7 %copy-start.3 = (s32[1,128,4]{1,2,0:T(4,128)S(1)}, s32[1,128,4]{1,2,0:T(4,128)}, u32[]{:S(2)}) copy-start(s32[1,128,4]{1,2,0:T(4,128)} %param.10) | copy-start | bytes 6148
  0.0 18.0 %copy-start.1 = (bf16[9,24,256]{2,1,0:T(8,128)(2,1)S(1)}, bf16[9,24,256]{2,1,0:T(8,128)(2,1)}, u32[]{:S(2)}) copy-start(bf16[9,24,256]{2,1,0:T(8,128)(2,1)} %param.12) | copy-start | bytes 331780
  0.0 32.3 %copy-start.5 = (f32[256]{0:T(256)S(1)}, f32[256]{0:T(256)}, u32[]{:S(2)}) copy-start(f32[256]{0:T(256)} %param.13) | copy-start | bytes 3076
  0.0 54.0 %copy-start.4 = (f32[512]{0:T(512)S(1)}, f32[512]{0:T(512)}, u32[]{:S(2)}) copy-start(f32[512]{0:T(512)} %param.15) | copy-start | bytes 6148
  0.0 54.9 %all-to-all-start = ((bf16[128,4,8,256]{3,2,1,0:T(8,128)(2,1)}), bf16[128,4,8,256]{3,2,1,0:T(8,128)(2,1)S(1)}, u32[]{:S(2)}, u32[]{:S(2)}) async-start(bf16[128,4,8,256]{3,2,1,0:T(8,128)(2,1)} %bitcast.24), calls=%async_computation | async-start | bytes 4194304 | tf_op jit(solution)/shard_map/all_to_all | solution.py:335
  12.6 5.4 %collective-permute-start = (bf16[1,4,4,2,8]{4,3,2,1,0:T(2,128)(2,1)S(1)}, bf16[1,4,4,2,8]{4,3,2,1,0:T(2,128)(2,1)S(1)}, u32[]{:S(2)}, u32[]{:S(2)}) collective-permute-start(bf16[1,4,4,2,8]{4,3,2,1,0:T(2,128)(2,1)S(1)} %get-tuple-element.29), channel_id=1, source_target_pairs={{0,32},{32,64},{64,96},{96,0},{1,33},{33,65},{65,97},{97,1},{2,34}... | collective-permute-start | bytes 1544 | tf_op jit(solution)/shard_map/ppermute | solution.py:358
  14.1 7.2 %collective-permute-start.1 = (bf16[1,4,4,2,8]{4,3,2,1,0:T(2,128)(2,1)S(1)}, bf16[1,4,4,2,8]{4,3,2,1,0:T(2,128)(2,1)S(1)}, u32[]{:S(2)}, u32[]{:S(2)}) collective-permute-start(bf16[1,4,4,2,8]{4,3,2,1,0:T(2,128)(2,1)S(1)} %get-tuple-element.28), channel_id=1, source_target_pairs={{0,64},{32,96},{64,0},{96,32},{1,65},{33,97},{65,1},{97,33},{2,66}... | collective-permute-start | bytes 1544 | tf_op jit(solution)/shard_map/ppermute | solution.py:358
  17.1 4.6 %collective-permute-start.2 = (bf16[1,4,4,2,8]{4,3,2,1,0:T(2,128)(2,1)S(1)}, bf16[1,4,4,2,8]{4,3,2,1,0:T(2,128)(2,1)S(1)}, u32[]{:S(2)}, u32[]{:S(2)}) collective-permute-start(bf16[1,4,4,2,8]{4,3,2,1,0:T(2,128)(2,1)S(1)} %get-tuple-element.30), channel_id=1, source_target_pairs={{0,96},{32,0},{64,32},{96,64},{1,97},{33,1},{65,33},{97,65},{2,98}... | collective-permute-start | bytes 1544 | tf_op jit(solution)/shard_map/ppermute | solution.py:358
  21.8 14.9 %collective-permute-start.3 = (bf16[4,1,4,2,8]{4,3,2,1,0:T(2,128)(2,1)S(1)}, bf16[4,1,4,2,8]{4,3,2,1,0:T(2,128)(2,1)S(1)}, u32[]{:S(2)}, u32[]{:S(2)}) collective-permute-start(bf16[4,1,4,2,8]{4,3,2,1,0:T(2,128)(2,1)S(1)} %get-tuple-element.26), channel_id=1, source_target_pairs={{0,8},{1,9},{2,10},{3,11},{4,12},{5,13},{6,14},{7,15},{8,16},{9,17... | collective-permute-start | bytes 1544 | tf_op jit(solution)/shard_map/ppermute | solution.py:360
  29.8 7.5 %collective-permute-start.4 = (bf16[4,1,4,2,8]{4,3,2,1,0:T(2,128)(2,1)S(1)}, bf16[4,1,4,2,8]{4,3,2,1,0:T(2,128)(2,1)S(1)}, u32[]{:S(2)}, u32[]{:S(2)}) collective-permute-start(bf16[4,1,4,2,8]{4,3,2,1,0:T(2,128)(2,1)S(1)} %get-tuple-element.25), channel_id=1, source_target_pairs={{0,16},{1,17},{2,18},{3,19},{4,20},{5,21},{6,22},{7,23},{8,24},{9,... | collective-permute-start | bytes 1544 | tf_op jit(solution)/shard_map/ppermute | solution.py:360
  29.8 7.5 %collective-permute-start.5 = (bf16[4,1,4,2,8]{4,3,2,1,0:T(2,128)(2,1)S(1)}, bf16[4,1,4,2,8]{4,3,2,1,0:T(2,128)(2,1)S(1)}, u32[]{:S(2)}, u32[]{:S(2)}) collective-permute-start(bf16[4,1,4,2,8]{4,3,2,1,0:T(2,128)(2,1)S(1)} %get-tuple-element.24), channel_id=1, source_target_pairs={{0,24},{1,25},{2,26},{3,27},{4,28},{5,29},{6,30},{7,31},{8,0},{9,1... | collective-permute-start | bytes 1544 | tf_op jit(solution)/shard_map/ppermute | solution.py:360
  37.5 9.9 %collective-permute-start.6 = (bf16[4,4,1,2,8]{4,3,2,1,0:T(2,128)(2,1)S(1)}, bf16[4,4,1,2,8]{4,3,2,1,0:T(2,128)(2,1)S(1)}, u32[]{:S(2)}, u32[]{:S(2)}) collective-permute-start(bf16[4,4,1,2,8]{4,3,2,1,0:T(2,128)(2,1)S(1)} %get-tuple-element.22), channel_id=1, source_target_pairs={{0,2},{1,3},{2,4},{3,5},{4,6},{5,7},{6,0},{7,1},{8,10},{9,11},{10,... | collective-permute-start | bytes 1544 | tf_op jit(solution)/shard_map/ppermute | solution.py:360
  38.7 9.7 %collective-permute-start.7 = (bf16[4,4,1,2,8]{4,3,2,1,0:T(2,128)(2,1)S(1)}, bf16[4,4,1,2,8]{4,3,2,1,0:T(2,128)(2,1)S(1)}, u32[]{:S(2)}, u32[]{:S(2)}) collective-permute-start(bf16[4,4,1,2,8]{4,3,2,1,0:T(2,128)(2,1)S(1)} %get-tuple-element.21), channel_id=1, source_target_pairs={{0,4},{1,5},{2,6},{3,7},{4,0},{5,1},{6,2},{7,3},{8,12},{9,13},{10,... | collective-permute-start | bytes 1544 | tf_op jit(solution)/shard_map/ppermute | solution.py:360
  47.3 2.6 %collective-permute-start.8 = (bf16[4,4,1,2,8]{4,3,2,1,0:T(2,128)(2,1)S(1)}, bf16[4,4,1,2,8]{4,3,2,1,0:T(2,128)(2,1)S(1)}, u32[]{:S(2)}, u32[]{:S(2)}) collective-permute-start(bf16[4,4,1,2,8]{4,3,2,1,0:T(2,128)(2,1)S(1)} %get-tuple-element.20), channel_id=1, source_target_pairs={{0,6},{1,7},{2,0},{3,1},{4,2},{5,3},{6,4},{7,5},{8,14},{9,15},{10,... | collective-permute-start | bytes 1544 | tf_op jit(solution)/shard_map/ppermute | solution.py:360
  50.0 4.8 %collective-permute-start.9 = (bf16[4,4,4,1,8]{4,3,2,1,0:T(2,128)(2,1)S(1)}, bf16[4,4,4,1,8]{4,3,2,1,0:T(2,128)(2,1)S(1)}, u32[]{:S(2)}, u32[]{:S(2)}) collective-permute-start(bf16[4,4,4,1,8]{4,3,2,1,0:T(2,128)(2,1)S(1)} %get-tuple-element.18), channel_id=1, source_target_pairs={{0,1},{1,0},{2,3},{3,2},{4,5},{5,4},{6,7},{7,6},{8,9},{9,8},{10,11... | collective-permute-start | bytes 3080 | tf_op jit(solution)/shard_map/ppermute | solution.py:360
  66.6 21.5 %all-to-all-start.1 = ((bf16[32,96,128]{2,1,0:T(8,128)(2,1)}), bf16[32,96,128]{2,1,0:T(8,128)(2,1)S(1)}, u32[]{:S(2)}, u32[]{:S(2)}) async-start(bf16[32,96,128]{2,1,0:T(8,128)(2,1)} %shard_map.82), calls=%async_computation.1 | async-start | bytes 1572864 | tf_op jit(solution)/shard_map/all_to_all | solution.py:368
  88.1 10.8 %collective-permute-start.10 = (bf16[32,16,128]{2,1,0:T(8,128)(2,1)S(1)}, bf16[32,16,128]{2,1,0:T(8,128)(2,1)S(1)}, u32[]{:S(2)}, u32[]{:S(2)}) collective-permute-start(bf16[32,16,128]{2,1,0:T(8,128)(2,1)S(1)} %slice.86), channel_id=1, source_target_pairs={{0,1},{2,3},{4,5},{6,7},{8,9},{10,11},{12,13},{14,15},{16,17},{18,... | collective-permute-start | bytes 393224 | tf_op jit(solution)/shard_map/ppermute | solution.py:372
  98.6 8.7 %collective-permute-start.11 = (bf16[4,384,512]{2,1,0:T(8,128)(2,1)}, bf16[4,384,512]{2,1,0:T(8,128)(2,1)}, u32[]{:S(2)}, u32[]{:S(2)}) collective-permute-start(bf16[4,384,512]{2,1,0:T(8,128)(2,1)} %get-tuple-element.15), channel_id=1, source_target_pairs={{0,1},{1,0},{2,3},{3,2},{4,5},{5,4},{6,7},{7,6},{8,9},{9,8},{10,11... | collective-permute-start | bytes 4718600 | tf_op jit(solution)/shard_map/ppermute | solution.py:399
  106.9 3.7 %collective-permute-start.12 = (bf16[4,384,512]{2,1,0:T(8,128)(2,1)}, bf16[4,384,512]{2,1,0:T(8,128)(2,1)S(1)}, u32[]{:S(2)}, u32[]{:S(2)}) collective-permute-start(bf16[4,384,512]{2,1,0:T(8,128)(2,1)} %get-tuple-element.16), channel_id=1, source_target_pairs={{0,1},{1,0},{2,3},{3,2},{4,5},{5,4},{6,7},{7,6},{8,9},{9,8},{10,11... | collective-permute-start | bytes 4718600 | tf_op jit(solution)/shard_map/ppermute | solution.py:399

commit v8 on v6

--- a/solution.py
+++ b/solution.py
@@ -22,7 +22,7 @@
 ROW_LANES = PHASES * FEAT
 FAR = 8192.0
 ROOT_HALF_LOG2E = (0.5 * 1.4426950408889634) ** 0.5
-SOURCES = 32
+SOURCES = 128
 
 
 def iota(shape, axis):
@@ -73,38 +73,37 @@
             total = total + more[...]
         total = total.reshape(SUBS * SB, KEPT * SB)
         total = jnp.concatenate([total, jnp.zeros((SUBS * SB, SB), jnp.float32)], axis=1)
-        pick = (iota((128, 128), 0) == iota((128, 128), 1) % SB).astype(jnp.float32)
-        density = jnp.dot(
-            total, pick, precision=lax.Precision.HIGHEST, preferred_element_type=jnp.float32
-        )
         lane = iota((SUBS * SB, 128), 1)
+        density = jnp.where(lane < SB, total, 0.0)
+        for places in (SB, 2 * SB, 4 * SB):
+            density = density + pltpu.roll(density, places, axis=1)
         grid = jnp.where(lane < SB, jnp.log1p(density), total / (1.0 + density))
         grid = grid.astype(jnp.bfloat16)
-        target = iota((4 * SB, SUBS * SB), 0)
-        source = iota((4 * SB, SUBS * SB), 1)
-        quad = target % SB
-        wanted = target // SB * BY + quad // 4 * SB + quad % 4
+        target = iota((4 * SB, 1), 0)
+        source = iota((1, SUBS * SB), 1)
+        quad = target & (SB - 1)
+        wanted = (target >> 4) * BY + (quad >> 2) * SB + (quad & 3)
+        wanted = jnp.where(quad < QUADS, wanted, -SUBS * SB)
         parts = []
         for phase in range(PHASES):
-            take = ((quad < QUADS) & (source == wanted + 4 * phase)).astype(jnp.bfloat16)
+            take = (source == wanted + 4 * phase).astype(jnp.bfloat16)
             parts.append(
                 jnp.dot(take, grid, preferred_element_type=jnp.float32).astype(jnp.bfloat16)
             )
         spread = jnp.concatenate(parts, axis=1)
-        lane_in = iota((512, 512), 0)
-        lane_out = iota((512, 512), 1)
-        moved = (
-            lane_in % SB * ROW_LANES + lane_in // 128 * FEAT + lane_in % 128 // SB == lane_out
-        ).astype(jnp.bfloat16)
+        lane_in = iota((512, 1), 0)
+        lane_out = (lane_in & 15) * ROW_LANES + (lane_in >> 7) * FEAT + ((lane_in & 127) >> 4)
+        moved = (iota((1, 512), 1) == lane_out).astype(jnp.bfloat16)
         ordered = jnp.dot(spread, moved, preferred_element_type=jnp.float32).astype(jnp.bfloat16)
-        to = iota((8 * QUADS, 4 * SB), 0)
-        start = iota((8 * QUADS, 4 * SB), 1)
+        to = iota((8 * QUADS, 1), 0)
+        block = to // QUADS
+        quad = to - block * QUADS
+        start = iota((1, 4 * SB), 1)
         for half in range(2):
             rows = None
             for k in range(4):
-                take = (to // QUADS % 4 == k) & (
-                    start == (2 * half + to // (4 * QUADS)) * SB + to % QUADS
-                )
+                wanted = (2 * half + (block >> 2)) * SB + quad
+                take = start == jnp.where((block & 3) == k, wanted, -1)
                 part = jnp.dot(
                     take.astype(jnp.bfloat16),
                     ordered[:, 128 * k : 128 * k + 128],

time: 102 us -> 102 us (level)
  no operation moved by 1% of the time
where the time goes in v8:
time: 102 us
  waiting for transfers between devices  46 us (45%)
  Pallas kernels  30.2 us (30%)
  starting transfers between devices  19 us (19%)
  local copies, waits for them, and re-layouts  5.91 us (6%)
    all_to_all x1, waiting for transfers between devices, shards(): arrived = lax.all_to_all(leaving, ('lat', 'lon'), 0, 0, tiled=True)  33 us
    pallas_call x2, Pallas kernels, convolutions(): pl.pallas_call(functools.partial(conv_kernel, 4 * part), grid_spec=pltpu....  16.1 us
    all_to_all x1, waiting for transfers between devices, shards(): own = lax.all_to_all(halves, 'lon', 0, 0, tiled=True)  12.1 us
    all_to_all x1, starting transfers between devices, shards(): arrived = lax.all_to_all(leaving, ('lat', 'lon'), 0, 0, tiled=True)  11.5 us
    pallas_call x1, Pallas kernels, set_convolution(): pl.pallas_call(setconv_kernel, grid_spec=pltpu.PrefetchScalarGridSpec(num...  11.1 us
    all_to_all x1, starting transfers between devices, shards(): own = lax.all_to_all(halves, 'lon', 0, 0, tiled=True)  4.54 us
    dynamic_update_slice x2, local copies, waits for them, and re-layouts, shards(): lax.dynamic_update_slice_in_dim(whole, rows, (1 - core) * 8 + 4 * part, a...  3.9 us
    pallas_call x1, Pallas kernels, leaving_tiles(): pl.pallas_call(leave_kernel, grid=(2,), in_specs=[pl.BlockSpec(subs.shape...  2.96 us
  transfers between devices with their start and end apart: 5, of which 3 were waited for; matrix products, arithmetic and copies ran while one was open for 5% of the time, Pallas kernels for 16%

profile of v8, /device:TPU:1, one launch (start us, length us, event | category | flops | bytes accessed | tf_op | source)
XLA Modules:
  0.0 101.6 jit_solution(5408157596503588981)
XLA Ops:
  0.0 3.0 %shard_map.82 = bf16[128,9,8,128]{3,2,1,0:T(8,128)(2,1)} custom-call(s32[4,128]{1,0:T(4,128)} %bitcast.27, s32[4,128]{1,0:T(4,128)} %bitcast.28, bf16[128,4,8,256]{3,2,1,0:T(8,128)(2,1)} %bitcast.25), custom_call_target="tpu_custom_call" | custom-call | tf_op jit(solution)/shard_map/pallas_call | solution.py:156
  3.0 11.5 %all-to-all-start = ((bf16[128,9,8,128]{3,2,1,0:T(8,128)(2,1)}), bf16[128,9,8,128]{3,2,1,0:T(8,128)(2,1)S(1)}, u32[]{:S(2)}, u32[]{:S(2)}) async-start(bf16[128,9,8,128]{3,2,1,0:T(8,128)(2,1)} %shard_map.82), calls=%async_computation | async-start | bytes 4718592 | tf_op jit(solution)/shard_map/all_to_all | solution.py:363
  14.5 0.1 pad.8.clone
  14.6 0.1 pad.5.clone
  14.7 0.1 pad_add_fusion.1.refs_0_
  14.8 33.0 %all-to-all-done.tiles_ref = bf16[128,9,8,128]{3,2,1,0:T(8,128)(2,1)S(1)} async-done(((bf16[128,9,8,128]{3,2,1,0:T(8,128)(2,1)}), bf16[128,9,8,128]{3,2,1,0:T(8,128)(2,1)S(1)}, u32[]{:S(2)}, u32[]{:S(2)}) %all-to-all-start) | async-done | bytes 2359328 | tf_op jit(solution)/shard_map/all_to_all | solution.py:363
  47.8 0.1 slice_convert_fusion
  47.8 11.1 %shard_map.83 = bf16[32,96,128]{2,1,0:T(8,128)(2,1)} custom-call(s32[128,8]{1,0:T(8,128)S(1)} %bitcast.23, bf16[128,9,8,128]{3,2,1,0:T(8,128)(2,1)S(1)} %all-to-all-done.tiles_ref), custom_call_target="tpu_custom_call" | custom-call | tf_op jit(solution)/shard_map/pallas_call | solution.py:120
  59.0 4.5 %all-to-all-start.1 = ((bf16[32,96,128]{2,1,0:T(8,128)(2,1)}), bf16[32,96,128]{2,1,0:T(8,128)(2,1)S(1)}, u32[]{:S(2)}, u32[]{:S(2)}) async-start(bf16[32,96,128]{2,1,0:T(8,128)(2,1)} %shard_map.83), calls=%async_computation.1 | async-start | bytes 1572864 | tf_op jit(solution)/shard_map/all_to_all | solution.py:368
  63.5 0.1 pad_add_fusion.refs_0_
  63.6 0.1 convolution_bitcast_fusion
  63.8 0.1 fusion.1
  63.8 0.1 maximum_maximum_fusion.refs_2_.refs_3_
  63.9 1.8 %rev.3 = bf16[3,3,256,512]{3,2,1,0:T(8,128)(2,1)S(1)} reverse(bf16[3,3,256,512]{3,2,1,0:T(8,128)(2,1)} %bitcast.24), dimensions={1} | reverse | bytes 4718592 | tf_op jit(solution)/shard_map/rev | solution.py:383
  65.7 12.1 %all-to-all-done.1.refs_1_.refs_2_ = bf16[32,96,128]{2,1,0:T(8,128)(2,1)S(1)} async-done(((bf16[32,96,128]{2,1,0:T(8,128)(2,1)}), bf16[32,96,128]{2,1,0:T(8,128)(2,1)S(1)}, u32[]{:S(2)}, u32[]{:S(2)}) %all-to-all-start.1) | async-done | bytes 786464 | tf_op jit(solution)/shard_map/all_to_all | solution.py:368
  77.9 2.2 %collective-permute-start = (bf16[32,16,128]{2,1,0:T(8,128)(2,1)S(1)}, bf16[32,16,128]{2,1,0:T(8,128)(2,1)S(1)}, u32[]{:S(2)}, u32[]{:S(2)}) collective-permute-start(bf16[32,16,128]{2,1,0:T(8,128)(2,1)S(1)} %slice.21), channel_id=1, source_target_pairs={{0,1},{2,3},{4,5},{6,7},{8,9},{10,11},{12,13},{14,15},{16,17},{18,... | collective-permute-start | bytes 393224 | tf_op jit(solution)/shard_map/ppermute | solution.py:372
  80.1 8.1 %shard_map.84 = (bf16[16,384,512]{2,1,0:T(8,128)(2,1)}, bf16[4,384,512]{2,1,0:T(8,128)(2,1)}) custom-call(s32[2]{0:T(128)S(1)} %pad_add_fusion.1.refs_0_, bf16[32,96,128]{2,1,0:T(8,128)(2,1)S(1)} %all-to-all-done.1.refs_1_.refs_2_, f32[80,256]{1,0:T(8,128)S(1)} %maximum_maximum_fusion.refs_2_.refs_3_, bf16[3,768,512]{2,1,0:T(8,128)(2,1)S(1)} %bitcast.21), custom_call_target="tpu_custom_call" | custom-call | flops 8999999488 | bytes 12000000 | tf_op jit(solution)/shard_map/pallas_call | solution.py:298
  88.2 0.4 collective-permute-start.1
  88.6 0.0 collective-permute-done.refs_1_
  88.6 8.1 %shard_map.85 = (bf16[16,384,512]{2,1,0:T(8,128)(2,1)}, bf16[4,384,512]{2,1,0:T(8,128)(2,1)}) custom-call(s32[2]{0:T(128)S(1)} %pad_add_fusion.refs_0_, bf16[32,16,128]{2,1,0:T(8,128)(2,1)S(1)} %collective-permute-done.refs_1_, bf16[32,96,128]{2,1,0:T(8,128)(2,1)S(1)} %all-to-all-done.1.refs_1_.refs_2_, ...), custom_call_target="tpu_custom_call", output_to_operand_aliasing={{0}: (5, {})} | custom-call | flops 8999999488 | bytes 12000000 | tf_op jit(solution)/shard_map/pallas_call | solution.py:298
  96.7 0.2 collective-permute-start.2
  96.9 2.7 %constant_dynamic-update-slice_fusion.1 = bf16[16,384,512]{2,1,0:T(8,128)(2,1)} fusion(bf16[16,384,512]{2,1,0:T(8,128)(2,1)} %get-tuple-element.14, bf16[4,384,512]{2,1,0:T(8,128)(2,1)} %collective-permute-done.1, s32[]{:T(128)S(6)} %select_n.19), kind=kLoop, calls=%fused_computation.12 | loop fusion | bytes 3145732 | tf_op jit(solution)/shard_map/dynamic_update_slice | solution.py:401
  99.6 0.8 collective-permute-done.2
  100.4 1.2 %constant_dynamic-update-slice_fusion = bf16[16,384,512]{2,1,0:T(8,128)(2,1)} fusion(bf16[16,384,512]{2,1,0:T(8,128)(2,1)} %constant_dynamic-update-slice_fusion.1, bf16[4,384,512]{2,1,0:T(8,128)(2,1)S(1)} %collective-permute-done.2, s32[]{:T(128)S(6)} %select_n.20), kind=kLoop, calls=%fused_computation.11 | loop fusion | bytes 3145732 | tf_op jit(solution)/shard_map/dynamic_update_slice | solution.py:401
  (14 shorter events, 0.1 us)
Async XLA Ops:
  0.0 63.6 %copy-start = (bf16[6,23]{1,0:T(8,128)(2,1)S(1)}, bf16[6,23]{1,0:T(8,128)(2,1)}, u32[]{:S(2)}) copy-start(bf16[6,23]{1,0:T(8,128)(2,1)} %param.11) | copy-start | bytes 832
  3.0 11.5 %copy-start.2 = (f32[512]{0:T(512)S(1)}, f32[512]{0:T(512)}, u32[]{:S(2)}) copy-start(f32[512]{0:T(512)} %param.15) | copy-start | bytes 6148
  3.0 11.8 %copy-start.3 = (f32[256]{0:T(256)S(1)}, f32[256]{0:T(256)}, u32[]{:S(2)}) copy-start(f32[256]{0:T(256)} %param.13) | copy-start | bytes 3076
  3.0 11.8 %copy-start.1 = (bf16[9,24,256]{2,1,0:T(8,128)(2,1)S(1)}, bf16[9,24,256]{2,1,0:T(8,128)(2,1)}, u32[]{:S(2)}) copy-start(bf16[9,24,256]{2,1,0:T(8,128)(2,1)} %param.12) | copy-start | bytes 331780
  3.0 44.8 %all-to-all-start = ((bf16[128,9,8,128]{3,2,1,0:T(8,128)(2,1)}), bf16[128,9,8,128]{3,2,1,0:T(8,128)(2,1)S(1)}, u32[]{:S(2)}, u32[]{:S(2)}) async-start(bf16[128,9,8,128]{3,2,1,0:T(8,128)(2,1)} %shard_map.82), calls=%async_computation | async-start | bytes 4718592 | tf_op jit(solution)/shard_map/all_to_all | solution.py:363
  59.0 18.9 %all-to-all-start.1 = ((bf16[32,96,128]{2,1,0:T(8,128)(2,1)}), bf16[32,96,128]{2,1,0:T(8,128)(2,1)S(1)}, u32[]{:S(2)}, u32[]{:S(2)}) async-start(bf16[32,96,128]{2,1,0:T(8,128)(2,1)} %shard_map.83), calls=%async_computation.1 | async-start | bytes 1572864 | tf_op jit(solution)/shard_map/all_to_all | solution.py:368
  77.9 10.8 %collective-permute-start = (bf16[32,16,128]{2,1,0:T(8,128)(2,1)S(1)}, bf16[32,16,128]{2,1,0:T(8,128)(2,1)S(1)}, u32[]{:S(2)}, u32[]{:S(2)}) collective-permute-start(bf16[32,16,128]{2,1,0:T(8,128)(2,1)S(1)} %slice.21), channel_id=1, source_target_pairs={{0,1},{2,3},{4,5},{6,7},{8,9},{10,11},{12,13},{14,15},{16,17},{18,... | collective-permute-start | bytes 393224 | tf_op jit(solution)/shard_map/ppermute | solution.py:372
  88.2 8.7 %collective-permute-start.1 = (bf16[4,384,512]{2,1,0:T(8,128)(2,1)}, bf16[4,384,512]{2,1,0:T(8,128)(2,1)}, u32[]{:S(2)}, u32[]{:S(2)}) collective-permute-start(bf16[4,384,512]{2,1,0:T(8,128)(2,1)} %get-tuple-element.15), channel_id=1, source_target_pairs={{0,1},{1,0},{2,3},{3,2},{4,5},{5,4},{6,7},{7,6},{8,9},{9,8},{10,11... | collective-permute-start | bytes 4718600 | tf_op jit(solution)/shard_map/ppermute | solution.py:399
  96.7 3.7 %collective-permute-start.2 = (bf16[4,384,512]{2,1,0:T(8,128)(2,1)}, bf16[4,384,512]{2,1,0:T(8,128)(2,1)S(1)}, u32[]{:S(2)}, u32[]{:S(2)}) collective-permute-start(bf16[4,384,512]{2,1,0:T(8,128)(2,1)} %get-tuple-element.16), channel_id=1, source_target_pairs={{0,1},{1,0},{2,3},{3,2},{4,5},{5,4},{6,7},{7,6},{8,9},{9,8},{10,11... | collective-permute-start | bytes 4718600 | tf_op jit(solution)/shard_map/ppermute | solution.py:399

commit v9 on v8

--- a/solution.py
+++ b/solution.py
@@ -181,13 +181,12 @@
 def conv_kernel(first_block, *refs):
     flag_ref, *halo, own_ref, params_ref, weight2_hbm = refs[: 4 + (first_block == 0)]
     (out_ref, send_ref, wide_ref, grid_ref, moved_ref, even_rows, odd_rows, weight2_ref, odd1_ref,
-     odd2_ref, even1_ref, even2_ref, sem) = refs[-13:]
+     odd2_ref, even1_ref, even2_ref, rows_ref, sem, out_sem) = refs[-15:]
     bias1 = params_ref[9 * FEAT : 9 * FEAT + 1, :]
     bias2 = jnp.concatenate(
         [params_ref[9 * FEAT + 1 : 9 * FEAT + 2, :], params_ref[9 * FEAT + 2 : 9 * FEAT + 3, :]],
         axis=1,
     )
-    step = pl.program_id(0)
     columns = grid_ref.shape[0]
     loads = [
         pltpu.make_async_copy(
@@ -241,45 +240,58 @@
                 preferred_element_type=jnp.float32,
             )
             total = part if total is None else total + part
-        total = (total + bias2).astype(jnp.bfloat16).reshape(out_ref.shape)
-        out_ref[...] = total
-        send_ref[...] = total
-
-    @pl.when(step == 0)
-    def _():
-        for load in loads:
-            load.start()
-        params = params_ref[...].astype(jnp.bfloat16)
-        odd1_ref[...] = placed(params, 128, 1, -1, 0, 3)
-        odd2_ref[...] = placed(params, 256, 3, -1, 0, 3)
-        even1_ref[0:128, :] = placed(params, 128, 1, 1, 1, 3)
-        even1_ref[128:256, :] = placed(params, 128, 1, -3, 0, 1)
-        even2_ref[0:256, :] = placed(params, 256, 3, 1, 1, 3)
-        even2_ref[256:512, :] = placed(params, 256, 3, -3, 0, 1)
-        for source in range(own_ref.shape[0]):
-            own = own_ref[source].astype(jnp.float32)
-            parts = [own[QUADS * k : QUADS * (k + 1)] for k in range(first_block, first_block + 4)]
-            if first_block == 0:
-                parts = [halo[0][source].astype(jnp.float32)[SB - QUADS :]] + parts
-            else:
-                parts = [own[QUADS * (first_block - 1) : QUADS * first_block]] + parts
-            for k, part in enumerate(parts):
-                wide_ref[QUADS * source : QUADS * (source + 1), 128 * k : 128 * (k + 1)] = part
-        grid_ref[...] = wide_ref[...].astype(jnp.bfloat16)
-        moved_ref[...] = pltpu.roll(wide_ref[...], 1, axis=0).astype(jnp.bfloat16)
-        for t in range(3):
-            first_row(t)
-        for load in loads:
-            load.wait()
-        second_row(0)
+        if row >= 2:
+            for store in stores(row - 2):
+                store.wait()
+        rows_ref[row % 2] = (total + bias2).astype(jnp.bfloat16)
+        for store in stores(row):
+            store.start()
+
+    def stores(row):
+        out_row = flag_ref[0] * 8 + first_block + row
+        half = columns // 2
+        return [
+            pltpu.make_async_copy(
+                rows_ref.at[row % 2, pl.ds(half * k, half)],
+                target.at[at, pl.ds(half * k, half)],
+                out_sem.at[row % 2, side, k],
+            )
+            for side, (target, at) in enumerate([(out_ref, out_row), (send_ref, row)])
+            for k in range(2)
+        ]
+
+    for load in loads:
+        load.start()
+    params = params_ref[...].astype(jnp.bfloat16)
+    odd1_ref[...] = placed(params, 128, 1, -1, 0, 3)
+    odd2_ref[...] = placed(params, 256, 3, -1, 0, 3)
+    even1_ref[0:128, :] = placed(params, 128, 1, 1, 1, 3)
+    even1_ref[128:256, :] = placed(params, 128, 1, -3, 0, 1)
+    even2_ref[0:256, :] = placed(params, 256, 3, 1, 1, 3)
+    even2_ref[256:512, :] = placed(params, 256, 3, -3, 0, 1)
+    for source in range(own_ref.shape[0]):
+        own = own_ref[source].astype(jnp.float32)
+        parts = [own[QUADS * k : QUADS * (k + 1)] for k in range(first_block, first_block + 4)]
+        if first_block == 0:
+            parts = [halo[0][source].astype(jnp.float32)[SB - QUADS :]] + parts
+        else:
+            parts = [own[QUADS * (first_block - 1) : QUADS * first_block]] + parts
+        for k, part in enumerate(parts):
+            wide_ref[QUADS * source : QUADS * (source + 1), 128 * k : 128 * (k + 1)] = part
+    grid_ref[...] = wide_ref[...].astype(jnp.bfloat16)
+    moved_ref[...] = pltpu.roll(wide_ref[...], 1, axis=0).astype(jnp.bfloat16)
+    for t in range(3):
+        first_row(t)
+    for load in loads:
+        load.wait()
+    second_row(0)
 
     for row in range(1, 4):
-
-        @pl.when(step == row)
-        def _(row=row):
-            first_row(2 * row + 1)
-            first_row(2 * row + 2)
-            second_row(row)
+        first_row(2 * row + 1)
+        first_row(2 * row + 2)
+        second_row(row)
+    for store in stores(2) + stores(3):
+        store.wait()
 
 
 def convolutions(part, flags, halo, own, params, weights2, whole):
@@ -299,12 +311,9 @@
         functools.partial(conv_kernel, 4 * part),
         grid_spec=pltpu.PrefetchScalarGridSpec(
             num_scalar_prefetch=1,
-            grid=(4,),
+            grid=(1,),
             in_specs=specs,
-            out_specs=[
-                pl.BlockSpec((1, columns, C2), lambda i, flags: (flags[0] * 8 + 4 * part + i, 0, 0)),
-                pl.BlockSpec((1, columns, C2), lambda i, *_: (i, 0, 0)),
-            ],
+            out_specs=[anywhere, anywhere],
             scratch_shapes=[
                 pltpu.VMEM((columns, 640), jnp.float32),
                 pltpu.VMEM((columns, 640), jnp.bfloat16),
@@ -316,7 +325,9 @@
                 pltpu.VMEM((256, C1), jnp.bfloat16),
                 pltpu.VMEM((256, C1), jnp.bfloat16),
                 pltpu.VMEM((512, C1), jnp.bfloat16),
+                pltpu.VMEM((2, columns, C2), jnp.bfloat16),
                 pltpu.SemaphoreType.DMA((3, 3)),
+                pltpu.SemaphoreType.DMA((2, 2, 2)),
             ],
         ),
         out_shape=[

time: 102 us -> 101 us (level)
  transfers between devices with their start and end apart: 5 -> 5, of which waited for: 3 -> 3; matrix products, arithmetic and copies ran while one was open for 5% -> 5% of each run, Pallas kernels for 16% -> 15%
where the time goes in v9:
time: 101 us
  waiting for transfers between devices  46 us (46%)
  Pallas kernels  29.6 us (29%)
  starting transfers between devices  19 us (19%)
  local copies, waits for them, and re-layouts  5.91 us (6%)
    all_to_all x1, waiting for transfers between devices, shards(): arrived = lax.all_to_all(leaving, ('lat', 'lon'), 0, 0, tiled=True)  33 us
    pallas_call x2, Pallas kernels, convolutions(): pl.pallas_call(functools.partial(conv_kernel, 4 * part), grid_spec=pltpu....  15.5 us
    all_to_all x1, waiting for transfers between devices, shards(): own = lax.all_to_all(halves, 'lon', 0, 0, tiled=True)  12.1 us
    all_to_all x1, starting transfers between devices, shards(): arrived = lax.all_to_all(leaving, ('lat', 'lon'), 0, 0, tiled=True)  11.5 us
    pallas_call x1, Pallas kernels, set_convolution(): pl.pallas_call(setconv_kernel, grid_spec=pltpu.PrefetchScalarGridSpec(num...  11.1 us
    all_to_all x1, starting transfers between devices, shards(): own = lax.all_to_all(halves, 'lon', 0, 0, tiled=True)  4.53 us
    dynamic_update_slice x2, local copies, waits for them, and re-layouts, shards(): lax.dynamic_update_slice_in_dim(whole, rows, (1 - core) * 8 + 4 * part, a...  3.9 us
    pallas_call x1, Pallas kernels, leaving_tiles(): pl.pallas_call(leave_kernel, grid=(2,), in_specs=[pl.BlockSpec(subs.shape...  2.96 us
  transfers between devices with their start and end apart: 5, of which 3 were waited for; matrix products, arithmetic and copies ran while one was open for 5% of the time, Pallas kernels for 15%

profile of v9, /device:TPU:1, one launch (start us, length us, event | category | flops | bytes accessed | tf_op | source)
XLA Modules:
  0.0 101.0 jit_solution(17474174855148618217)
XLA Ops:
  0.0 3.0 %shard_map.82 = bf16[128,9,8,128]{3,2,1,0:T(8,128)(2,1)} custom-call(s32[4,128]{1,0:T(4,128)} %bitcast.27, s32[4,128]{1,0:T(4,128)} %bitcast.28, bf16[128,4,8,256]{3,2,1,0:T(8,128)(2,1)} %bitcast.25), custom_call_target="tpu_custom_call" | custom-call | tf_op jit(solution)/shard_map/pallas_call | solution.py:156
  3.0 11.5 %all-to-all-start = ((bf16[128,9,8,128]{3,2,1,0:T(8,128)(2,1)}), bf16[128,9,8,128]{3,2,1,0:T(8,128)(2,1)S(1)}, u32[]{:S(2)}, u32[]{:S(2)}) async-start(bf16[128,9,8,128]{3,2,1,0:T(8,128)(2,1)} %shard_map.82), calls=%async_computation | async-start | bytes 4718592 | tf_op jit(solution)/shard_map/all_to_all | solution.py:374
  14.5 0.1 pad.8.clone
  14.6 0.1 pad.5.clone
  14.7 0.1 pad_add_fusion.1.refs_0_
  14.8 33.0 %all-to-all-done.tiles_ref = bf16[128,9,8,128]{3,2,1,0:T(8,128)(2,1)S(1)} async-done(((bf16[128,9,8,128]{3,2,1,0:T(8,128)(2,1)}), bf16[128,9,8,128]{3,2,1,0:T(8,128)(2,1)S(1)}, u32[]{:S(2)}, u32[]{:S(2)}) %all-to-all-start) | async-done | bytes 2359328 | tf_op jit(solution)/shard_map/all_to_all | solution.py:374
  47.8 0.1 slice_convert_fusion
  47.8 11.1 %shard_map.83 = bf16[32,96,128]{2,1,0:T(8,128)(2,1)} custom-call(s32[128,8]{1,0:T(8,128)S(1)} %bitcast.23, bf16[128,9,8,128]{3,2,1,0:T(8,128)(2,1)S(1)} %all-to-all-done.tiles_ref), custom_call_target="tpu_custom_call" | custom-call | tf_op jit(solution)/shard_map/pallas_call | solution.py:120
  59.0 4.5 %all-to-all-start.1 = ((bf16[32,96,128]{2,1,0:T(8,128)(2,1)}), bf16[32,96,128]{2,1,0:T(8,128)(2,1)S(1)}, u32[]{:S(2)}, u32[]{:S(2)}) async-start(bf16[32,96,128]{2,1,0:T(8,128)(2,1)} %shard_map.83), calls=%async_computation.1 | async-start | bytes 1572864 | tf_op jit(solution)/shard_map/all_to_all | solution.py:379
  63.5 0.1 pad_add_fusion.refs_0_
  63.6 0.1 convolution_bitcast_fusion
  63.7 0.1 fusion.1
  63.8 0.1 maximum_maximum_fusion.refs_2_.refs_3_
  63.9 1.8 %rev.3 = bf16[3,3,256,512]{3,2,1,0:T(8,128)(2,1)S(1)} reverse(bf16[3,3,256,512]{3,2,1,0:T(8,128)(2,1)} %bitcast.24), dimensions={1} | reverse | bytes 4718592 | tf_op jit(solution)/shard_map/rev | solution.py:394
  65.7 12.1 %all-to-all-done.1.refs_1_.refs_2_ = bf16[32,96,128]{2,1,0:T(8,128)(2,1)S(1)} async-done(((bf16[32,96,128]{2,1,0:T(8,128)(2,1)}), bf16[32,96,128]{2,1,0:T(8,128)(2,1)S(1)}, u32[]{:S(2)}, u32[]{:S(2)}) %all-to-all-start.1) | async-done | bytes 786464 | tf_op jit(solution)/shard_map/all_to_all | solution.py:379
  77.9 2.3 %collective-permute-start = (bf16[32,16,128]{2,1,0:T(8,128)(2,1)S(1)}, bf16[32,16,128]{2,1,0:T(8,128)(2,1)S(1)}, u32[]{:S(2)}, u32[]{:S(2)}) collective-permute-start(bf16[32,16,128]{2,1,0:T(8,128)(2,1)S(1)} %slice.21), channel_id=1, source_target_pairs={{0,1},{2,3},{4,5},{6,7},{8,9},{10,11},{12,13},{14,15},{16,17},{18,... | collective-permute-start | bytes 393224 | tf_op jit(solution)/shard_map/ppermute | solution.py:383
  80.1 7.7 %shard_map.84 = (bf16[16,384,512]{2,1,0:T(8,128)(2,1)}, bf16[4,384,512]{2,1,0:T(8,128)(2,1)}) custom-call(s32[2]{0:T(128)S(1)} %pad_add_fusion.1.refs_0_, bf16[32,96,128]{2,1,0:T(8,128)(2,1)S(1)} %all-to-all-done.1.refs_1_.refs_2_, f32[80,256]{1,0:T(8,128)S(1)} %maximum_maximum_fusion.refs_2_.refs_3_, bf16[3,768,512]{2,1,0:T(8,128)(2,1)S(1)} %bitcast.21), custom_call_target="tpu_custom_call" | custom-call | flops 8999999488 | bytes 12000000 | tf_op jit(solution)/shard_map/pallas_call | solution.py:310
  87.9 0.4 collective-permute-start.1
  88.3 0.0 collective-permute-done.refs_1_
  88.3 7.7 %shard_map.85 = (bf16[16,384,512]{2,1,0:T(8,128)(2,1)}, bf16[4,384,512]{2,1,0:T(8,128)(2,1)}) custom-call(s32[2]{0:T(128)S(1)} %pad_add_fusion.refs_0_, bf16[32,16,128]{2,1,0:T(8,128)(2,1)S(1)} %collective-permute-done.refs_1_, bf16[32,96,128]{2,1,0:T(8,128)(2,1)S(1)} %all-to-all-done.1.refs_1_.refs_2_, ...), custom_call_target="tpu_custom_call", output_to_operand_aliasing={{0}: (5, {})} | custom-call | flops 8999999488 | bytes 12000000 | tf_op jit(solution)/shard_map/pallas_call | solution.py:310
  96.0 0.2 collective-permute-start.2
  96.3 2.7 %constant_dynamic-update-slice_fusion.1 = bf16[16,384,512]{2,1,0:T(8,128)(2,1)} fusion(bf16[16,384,512]{2,1,0:T(8,128)(2,1)} %get-tuple-element.14, bf16[4,384,512]{2,1,0:T(8,128)(2,1)} %collective-permute-done.1, s32[]{:T(128)S(6)} %select_n.19), kind=kLoop, calls=%fused_computation.12 | loop fusion | bytes 3145732 | tf_op jit(solution)/shard_map/dynamic_update_slice | solution.py:412
  98.9 0.8 collective-permute-done.2
  99.7 1.2 %constant_dynamic-update-slice_fusion = bf16[16,384,512]{2,1,0:T(8,128)(2,1)} fusion(bf16[16,384,512]{2,1,0:T(8,128)(2,1)} %constant_dynamic-update-slice_fusion.1, bf16[4,384,512]{2,1,0:T(8,128)(2,1)S(1)} %collective-permute-done.2, s32[]{:T(128)S(6)} %select_n.20), kind=kLoop, calls=%fused_computation.11 | loop fusion | bytes 3145732 | tf_op jit(solution)/shard_map/dynamic_update_slice | solution.py:412
  (14 shorter events, 0.1 us)
Async XLA Ops:
  0.0 63.6 %copy-start = (bf16[6,23]{1,0:T(8,128)(2,1)S(1)}, bf16[6,23]{1,0:T(8,128)(2,1)}, u32[]{:S(2)}) copy-start(bf16[6,23]{1,0:T(8,128)(2,1)} %param.11) | copy-start | bytes 832
  3.0 11.5 %copy-start.2 = (f32[512]{0:T(512)S(1)}, f32[512]{0:T(512)}, u32[]{:S(2)}) copy-start(f32[512]{0:T(512)} %param.15) | copy-start | bytes 6148
  3.0 11.8 %copy-start.3 = (f32[256]{0:T(256)S(1)}, f32[256]{0:T(256)}, u32[]{:S(2)}) copy-start(f32[256]{0:T(256)} %param.13) | copy-start | bytes 3076
  3.0 11.8 %copy-start.1 = (bf16[9,24,256]{2,1,0:T(8,128)(2,1)S(1)}, bf16[9,24,256]{2,1,0:T(8,128)(2,1)}, u32[]{:S(2)}) copy-start(bf16[9,24,256]{2,1,0:T(8,128)(2,1)} %param.12) | copy-start | bytes 331780
  3.0 44.8 %all-to-all-start = ((bf16[128,9,8,128]{3,2,1,0:T(8,128)(2,1)}), bf16[128,9,8,128]{3,2,1,0:T(8,128)(2,1)S(1)}, u32[]{:S(2)}, u32[]{:S(2)}) async-start(bf16[128,9,8,128]{3,2,1,0:T(8,128)(2,1)} %shard_map.82), calls=%async_computation | async-start | bytes 4718592 | tf_op jit(solution)/shard_map/all_to_all | solution.py:374
  59.0 18.9 %all-to-all-start.1 = ((bf16[32,96,128]{2,1,0:T(8,128)(2,1)}), bf16[32,96,128]{2,1,0:T(8,128)(2,1)S(1)}, u32[]{:S(2)}, u32[]{:S(2)}) async-start(bf16[32,96,128]{2,1,0:T(8,128)(2,1)} %shard_map.83), calls=%async_computation.1 | async-start | bytes 1572864 | tf_op jit(solution)/shard_map/all_to_all | solution.py:379
  77.9 10.4 %collective-permute-start = (bf16[32,16,128]{2,1,0:T(8,128)(2,1)S(1)}, bf16[32,16,128]{2,1,0:T(8,128)(2,1)S(1)}, u32[]{:S(2)}, u32[]{:S(2)}) collective-permute-start(bf16[32,16,128]{2,1,0:T(8,128)(2,1)S(1)} %slice.21), channel_id=1, source_target_pairs={{0,1},{2,3},{4,5},{6,7},{8,9},{10,11},{12,13},{14,15},{16,17},{18,... | collective-permute-start | bytes 393224 | tf_op jit(solution)/shard_map/ppermute | solution.py:383
  87.9 8.4 %collective-permute-start.1 = (bf16[4,384,512]{2,1,0:T(8,128)(2,1)}, bf16[4,384,512]{2,1,0:T(8,128)(2,1)}, u32[]{:S(2)}, u32[]{:S(2)}) collective-permute-start(bf16[4,384,512]{2,1,0:T(8,128)(2,1)} %get-tuple-element.15), channel_id=1, source_target_pairs={{0,1},{1,0},{2,3},{3,2},{4,5},{5,4},{6,7},{7,6},{8,9},{9,8},{10,11... | collective-permute-start | bytes 4718600 | tf_op jit(solution)/shard_map/ppermute | solution.py:410
  96.0 3.7 %collective-permute-start.2 = (bf16[4,384,512]{2,1,0:T(8,128)(2,1)}, bf16[4,384,512]{2,1,0:T(8,128)(2,1)S(1)}, u32[]{:S(2)}, u32[]{:S(2)}) collective-permute-start(bf16[4,384,512]{2,1,0:T(8,128)(2,1)} %get-tuple-element.16), channel_id=1, source_target_pairs={{0,1},{1,0},{2,3},{3,2},{4,5},{5,4},{6,7},{7,6},{8,9},{9,8},{10,11... | collective-permute-start | bytes 4718600 | tf_op jit(solution)/shard_map/ppermute | solution.py:410
